TPU v7x, 32 devices: a whole 2x2x4 slice. The times are simulated.
32 devices in a mesh: ctx: 8 (over z, y), ws: 4 (over x, core).
Axes of the slice: x: 2, y: 2, z: 4, core: 2. Of those that a mesh axis runs over, the one named last changes fastest.
Arguments:
- tokens: bfloat16 [4, 2048, 576], P('ws', 'ctx'), may hold values from -6 to 6
- attn_gain: bfloat16 [576], P('ws'), may hold values from 0.25 to 1.75
- query_weight: bfloat16 [576, 576], P('ws'), may hold values from -0.375 to 0.375
- key_weight: bfloat16 [576, 192], P('ws'), may hold values from -0.375 to 0.375
- value_weight: bfloat16 [576, 192], P('ws'), may hold values from -0.25 to 0.25
- output_weight: bfloat16 [576, 576], P('ws'), may hold values from -1 to 1
- ffn_gain: bfloat16 [576], P('ws'), may hold values from 0.25 to 1.75
- gate_weight: bfloat16 [576, 1536], P('ws'), may hold values from -0.25 to 0.25
- up_weight: bfloat16 [576, 1536], P('ws'), may hold values from -0.25 to 0.25
- down_weight: bfloat16 [1536, 576], P('ws'), may hold values from -0.21875 to 0.21875
- out_grad: bfloat16 [4, 2048, 576], P('ws', 'ctx'), may hold values from -6 to 6
Outputs:
- layer_out: bfloat16 [4, 2048, 576], P('ws', 'ctx')
- tokens_grad: bfloat16 [4, 2048, 576], P('ws', 'ctx')
- attn_gain_grad: float32 [576], P('ws')
- query_weight_grad: float32 [576, 576], P('ws')
- key_weight_grad: float32 [576, 192], P('ws')
- value_weight_grad: float32 [576, 192], P('ws')
- output_weight_grad: float32 [576, 576], P('ws')
- ffn_gain_grad: float32 [576], P('ws')
- gate_weight_grad: float32 [576, 1536], P('ws')
- up_weight_grad: float32 [576, 1536], P('ws')
- down_weight_grad: float32 [1536, 576], P('ws')
All inputs are finite; a program needn't handle non-finite values.
Results may differ from a plain program's by a relative error of at most 0.022.
Values may be sent and summed in bfloat16 or wider, within the bound.
No kernel may reach another device: no remote copies, remote signals or barrier semaphores. Data moves between devices by JAX's collectives and lax.ppermute only.
A program may use at most 128 MiB of HBM per device.

v0:
```python
import functools
import math

import jax
import jax.numpy as jnp
from jax import lax
from jax.experimental import pallas as pl
from jax.experimental.pallas import tpu as pltpu
from jax.sharding import PartitionSpec as P

H = 9
KV = 3
HD = 64
GROUPS = H // KV
KVW = KV * HD

EPS = 1e-05
THETA = 100000.0
NEGATIVE = -1e30
LANES = 128
FF_STEP = 256
MIB = 1024 * 1024

BF16 = jnp.bfloat16
F32 = jnp.float32

SMEM_SPEC = pl.BlockSpec(memory_space=pltpu.SMEM)
VMEM_SPEC = pl.BlockSpec(memory_space=pltpu.VMEM)


def mm(left, right, left_dim=1, right_dim=0):
    return lax.dot_general(
        left, right, (((left_dim,), (right_dim,)), ((), ())), preferred_element_type=F32
    )


def call(kernel, outs, args, scratch=(), micros=1, smem=0, vmem=16):
    return pl.pallas_call(
        kernel,
        out_shape=outs,
        in_specs=[SMEM_SPEC] * smem + [VMEM_SPEC] * (len(args) - smem),
        out_specs=jax.tree.map(lambda _: VMEM_SPEC, outs),
        scratch_shapes=list(scratch),
        compiler_params=pltpu.CompilerParams(vmem_limit_bytes=vmem * MIB),
        cost_estimate=pl.CostEstimate(
            flops=micros * 1_000_000_000, bytes_accessed=0, transcendentals=0
        ),
    )(*args)


def shaped(shape, dtype):
    return jax.ShapeDtypeStruct(tuple(shape), dtype)


def swap_halves(part):
    lane = lax.broadcasted_iota(jnp.int32, part.shape, 1)
    return jnp.where(
        lane % HD < HD // 2,
        pltpu.roll(part, LANES - HD // 2, axis=1),
        pltpu.roll(part, HD // 2, axis=1),
    )


def rotated(values, cosine, signed_sine, sign):
    rows, width = values.shape
    parts = []
    for start in range(0, width, LANES):
        part = values[:, start : start + LANES]
        used = part.shape[1]
        if used < LANES:
            part = jnp.concatenate([part, jnp.zeros((rows, LANES - used), F32)], -1)
        turned = part * cosine + sign * (swap_halves(part) * signed_sine)
        parts.append(turned[:, :used])
    return jnp.concatenate(parts, -1)


def stacked_heads(ref, group):
    first = group * GROUPS
    return jnp.concatenate(
        [ref[:, (first + g) * HD : (first + g + 1) * HD] for g in range(GROUPS)], 0
    )


def assembled(full, pieces, me):
    rows = pieces[0].shape[0]
    for relative, piece in enumerate(pieces):
        start = pl.multiple_of((me ^ relative) * rows, 16)
        full[pl.ds(start, rows), :] = piece[...]


def projected(tokens, gain, weight, cosine, sine):
    values = tokens.astype(F32)
    scale = lax.rsqrt(jnp.mean(values * values, -1, keepdims=True) + EPS)
    normed = (values * scale * gain).astype(BF16)
    linear = mm(normed, weight)
    keys = rotated(linear[:, :KVW], cosine, sine, 1.0)
    return normed, jnp.concatenate([keys, linear[:, KVW:]], -1).astype(BF16)


def block_at(index, rows):
    return pl.ds(pl.multiple_of(index * rows, rows), rows)


def owner_of(place, here):
    return (here ^ (place % 2)) - 2 * (place // 2)


def table_at(table, owner, rows):
    if table.shape[0] == rows:
        return table[...]
    return table[block_at(jnp.clip(owner, 0, table.shape[0] // rows - 1), rows), :]


def early_kernel(index, p0, p1, p2, p3, cosine, sine, *refs, places, slice_rows):
    pieces = refs[: len(places)]
    (
        normed_out, kv_out, query_out, query_weight, kv_weight, gains_out, gain_scr, raw_scr,
    ) = refs[len(places) :]
    here = index[0]
    more = p0.shape[0] - slice_rows
    packs = (p0, p1, p2, p3)
    for relative, pack in enumerate(packs):
        owner = index[1] ^ relative
        at = pl.ds(pl.multiple_of(owner * slice_rows, 16), slice_rows)
        kv_weight[at, :] = pack[:slice_rows, : 2 * KVW]
        query_weight[at, :] = pack[:slice_rows, 2 * KVW :]
        gain_scr[pl.ds(pl.multiple_of(owner * more, 16), more), :] = pack[
            slice_rows:, : gain_scr.shape[1]
        ]
    gains = jnp.concatenate(
        [
            gain_scr[owner * more : owner * more + 8, :slice_rows].astype(F32)
            for owner in range(len(packs))
        ],
        -1,
    )
    gains_out[...] = gains
    rows = normed_out.shape[1]
    for slot, piece in enumerate(pieces):
        raw_scr[slot] = piece[...]

    def project(slot, carry):
        owner = owner_of(one_of(places, slot), here)
        tables = [table_at(table, owner, rows) for table in (cosine, sine)]
        normed, kv = projected(raw_scr[slot].T, gains_out[0:1, :], kv_weight[...], *tables)
        normed_out[slot] = normed
        kv_out[slot] = kv
        return carry

    lax.fori_loop(0, len(places), project, 0)
    tables = [table_at(table, here, rows) for table in (cosine, sine)]
    linear = mm(normed_out[0], query_weight[...])
    query_out[...] = (rotated(linear, *tables, 1.0) * (1.0 / math.sqrt(HD))).astype(BF16)


def fill_masks(masks):
    shape = masks.shape[1:]
    key_pos = lax.broadcasted_iota(jnp.int32, shape, 0)
    query_pos = lax.broadcasted_iota(jnp.int32, shape, 1)
    masks[0] = jnp.zeros(shape, F32)
    masks[1] = jnp.where(query_pos >= key_pos, 0.0, NEGATIVE)


def one_of(values, at):
    found = values[0]
    for place, value in enumerate(values[1:], 1):
        found = jnp.where(at == place, value, found)
    return found


def forward_kernel(
    index, queries, early_normed, early_kv, kv_weight, gains, cosine, sine, *refs, places, late_places
):
    late, rest = refs[: len(late_places)], refs[len(late_places) :]
    attended, lse_out, kv_all, *rest = rest
    q_scr, acc_scr, max_scr, sum_scr, masks = rest[-5:]
    fill_masks(masks)
    rows = queries.shape[0]
    here = index[0]
    if late_places:
        normed_all, raw_scr = rest[:2]
        for slot, piece in enumerate(late):
            raw_scr[slot] = piece[...]

        def copy(slot, carry):
            owner = owner_of(one_of(places, slot), here)

            @pl.when((owner >= 0) & (owner <= here))
            def _():
                normed_all[block_at(owner, rows), :] = early_normed[slot]
                kv_all[block_at(owner, rows), :] = early_kv[slot]

            return carry

        def project(slot, carry):
            owner = owner_of(one_of(late_places, slot), here)

            @pl.when((owner >= 0) & (owner <= here))
            def _():
                normed, kv = projected(
                    raw_scr[slot].T,
                    gains[0:1, :],
                    kv_weight[...],
                    table_at(cosine, owner, rows),
                    table_at(sine, owner, rows),
                )
                normed_all[block_at(owner, rows), :] = normed
                kv_all[block_at(owner, rows), :] = kv

            return carry

        lax.fori_loop(0, len(places), copy, 0)
        lax.fori_loop(0, len(late_places), project, 0)
    else:
        kv_all[...] = early_kv[...]

    for group in range(KV):
        q_scr[group] = stacked_heads(queries, group)
    acc_scr[...] = jnp.zeros_like(acc_scr)
    max_scr[...] = jnp.full_like(max_scr, NEGATIVE)
    sum_scr[...] = jnp.zeros_like(sum_scr)

    def step(j, carry):
        keys_at = block_at(j, rows)
        mask = jnp.concatenate([masks[jnp.where(j == here, 1, 0)]] * GROUPS, -1)
        for group in range(KV):
            keys = kv_all[keys_at, group * HD : (group + 1) * HD]
            values = kv_all[keys_at, KVW + group * HD : KVW + (group + 1) * HD]
            scores = mm(keys, q_scr[group], 1, 1) + mask
            old_max = max_scr[group, 0:1, :]
            new_max = jnp.maximum(old_max, jnp.max(scores, 0, keepdims=True))
            weights = jnp.exp(scores - new_max)
            factor = jnp.exp(old_max - new_max)
            max_scr[group, 0:1, :] = new_max
            sum_scr[group, 0:1, :] = sum_scr[group, 0:1, :] * factor + jnp.sum(
                weights, 0, keepdims=True
            )
            acc_scr[group] = acc_scr[group] * factor + mm(values, weights.astype(BF16), 0, 0)
        return carry

    lax.fori_loop(0, here + 1, step, 0)
    lse_out[...] = jnp.zeros_like(lse_out)
    for group in range(KV):
        total = sum_scr[group, 0:1, :]
        result = acc_scr[group] / total
        lse_out[group : group + 1, :] = max_scr[group, 0:1, :] + jnp.log(total)
        for g in range(GROUPS):
            head = group * GROUPS + g
            attended[:, head * HD : (head + 1) * HD] = result[:, g * rows : (g + 1) * rows].T


def rms_back(values, gain, grad):
    width = values.shape[-1]
    scale = lax.rsqrt(jnp.mean(values * values, -1, keepdims=True) + EPS)
    scaled = values * scale
    pulled = grad * gain
    along = jnp.sum(pulled * scaled, -1, keepdims=True) * (1.0 / width)
    return scale * (pulled - scaled * along), grad * scaled


def put_tiles(outs, me, grads, grad_lanes, first_row):
    rows = grads.shape[0] // len(outs)
    first, last = grad_lanes
    for relative, out in enumerate(outs):
        start = pl.multiple_of((me ^ relative) * rows, 16)
        for tile in range((last - first) // LANES):
            at = first + tile * LANES
            out[first_row + tile * rows : first_row + (tile + 1) * rows, :] = grads[
                pl.ds(start, rows), at : at + LANES
            ]


def ffn_kernel(
    index, tokens, attended, gains, out_grad,
    wi0, wi1, wi2, wi3, wd0, wd1, wd2, wd3,
    layer_out, middle_grad_out, attended_grad_out, gain_grad,
    in_mine, in_along, in_send, mine, along, send,
    in_weight, down_weight, result_scr, back_scr, tile_scr, down_scr,
):
    me = index[1]
    assembled(in_weight, (wi0, wi1, wi2, wi3), me)
    assembled(down_weight, (wd0, wd1, wd2, wd3), me)
    in_outs = (in_mine, in_send.at[0], in_along, in_send.at[1])
    outs = (mine, send.at[0], along, send.at[1])
    gain = gains[1:2, :]
    ff = down_weight.shape[0]
    out_weight = in_weight.at[:, 2 * ff :]
    owners = len(outs)
    in_rows = in_weight.shape[0] // owners
    down_rows = ff // owners
    attended_low = attended[...].astype(BF16)
    middle = tokens[...].T.astype(F32) + mm(attended_low, out_weight[...])
    scale = lax.rsqrt(jnp.mean(middle * middle, -1, keepdims=True) + EPS)
    normed = (middle * scale * gain).astype(BF16)
    grad_rows = out_grad[...].T
    result_scr[...] = middle
    back_scr[...] = jnp.zeros_like(back_scr)
    width = grad_rows.shape[1]

    def ff_step(step, carry):
        start = pl.multiple_of(step * FF_STEP, FF_STEP)
        gate_at = pl.ds(start, FF_STEP)
        up_at = pl.ds(pl.multiple_of(ff + start, FF_STEP), FF_STEP)
        gate = mm(normed, in_weight[:, gate_at])
        up = mm(normed, in_weight[:, up_at])
        gated = 1.0 / (1.0 + jnp.exp(-gate))
        silu = gate * gated
        hidden = (silu * up).astype(BF16)
        down = down_weight[gate_at, :]
        result_scr[...] += mm(hidden, down)
        hidden_grad = mm(grad_rows, down, 1, 1)
        gate_grad = (hidden_grad * up * (gated * (1.0 + gate * (1.0 - gated)))).astype(BF16)
        up_grad = (hidden_grad * silu).astype(BF16)
        back_scr[...] += mm(gate_grad, in_weight[:, gate_at], 1, 1) + mm(
            up_grad, in_weight[:, up_at], 1, 1
        )
        tile_scr[:, gate_at] = mm(normed, gate_grad, 0, 0).astype(BF16)
        tile_scr[:, up_at] = mm(normed, up_grad, 0, 0).astype(BF16)
        down_scr[gate_at, :width] = mm(hidden, grad_rows, 0, 0).astype(BF16)
        return carry

    lax.fori_loop(0, ff // FF_STEP, ff_step, 0)

    put_tiles(in_outs, me, tile_scr, (0, 2 * ff), 0)
    base = 2 * (ff // LANES) * in_rows
    for out in in_outs:
        if base < out.shape[0]:
            out[base:, :] = jnp.zeros((out.shape[0] - base, LANES), BF16)
    whole = width // LANES * LANES
    put_tiles(outs, me, down_scr, (0, whole), 0)
    base = whole // LANES * down_rows
    half = down_rows // 2
    for relative, out in enumerate(outs):
        start = pl.multiple_of((me ^ relative) * down_rows, 16)
        rest = jnp.concatenate(
            [
                down_scr[pl.ds(start, half), whole:width],
                down_scr[pl.ds(pl.multiple_of(start + half, 16), half), whole:width],
            ],
            -1,
        )
        out[base : base + half, :] = rest
    base += half

    layer_out[...] = result_scr[...].astype(BF16).T
    middle_back, gain_terms = rms_back(middle, gain, back_scr[...])
    gain_grad[...] = jnp.zeros_like(gain_grad)
    gain_grad[0:1, :] = jnp.sum(gain_terms, 0, keepdims=True)
    middle_grad = middle_back + grad_rows.astype(F32)
    middle_grad_out[...] = middle_grad
    branch = middle_grad.astype(BF16)
    attended_grad_out[...] = mm(branch, out_weight[...], 1, 1).astype(BF16)
    out_weight_grad = mm(attended_low, branch, 0, 0).astype(BF16)
    wide = -(-width // LANES) * LANES
    tile_scr[:, :wide] = jnp.concatenate(
        [out_weight_grad, jnp.zeros((width, wide - width), BF16)], -1
    )
    put_tiles(outs, me, tile_scr, (0, wide), base)
    base += wide // LANES * in_rows
    for out in outs:
        out[base:, :] = jnp.zeros((out.shape[0] - base, LANES), BF16)


def put_small(outs, me, tile_scr, query_grad, kv_grad, query_weight, kv_weight, gains, ffn_gain_grad):
    width = query_grad.shape[0]
    wide = -(-width // LANES) * LANES
    gain_columns = gains[...].T
    terms = jnp.sum(query_grad * query_weight.astype(F32), -1, keepdims=True) + jnp.sum(
        kv_grad * kv_weight.astype(F32), -1, keepdims=True
    )
    columns = jnp.concatenate(
        [
            terms / gain_columns[:, 0:1],
            ffn_gain_grad[...].T[:, 0:1],
            jnp.zeros((width, wide - width - 2), F32),
        ],
        -1,
    )
    tile_scr[:, :wide] = jnp.concatenate([query_grad, columns], -1).astype(BF16)
    tile_scr[:, wide : wide + 2 * KVW] = kv_grad.astype(BF16)
    put_tiles(outs, me, tile_scr, (0, wide + 2 * KVW), 0)


def backward_kernel(
    index, queries, kv_all, attended, attended_grad, lse, normed, query_weight, kv_weight, gains,
    ffn_gain_grad, cosine, sine,
    *refs,
):
    q_scr, g_scr, delta_scr, acc_scr, query_grad_scr, masks = refs[-6:]
    fill_masks(masks)
    rows = queries.shape[0]
    blocks = kv_all.shape[0] // rows
    here = index[0]
    whole = normed.shape[0] > rows
    if whole:
        kv_grads, normed_grad, mine, along, send, tile_scr, weight_scr = refs[:-6]
        weight_scr[...] = jnp.zeros_like(weight_scr)
        kv_grads[...] = jnp.zeros_like(kv_grads)
    else:
        kv_grads, normed_grad, query_weight_grad = refs[:-6]
    for group in range(KV):
        q_scr[group] = stacked_heads(queries, group)
        grads = stacked_heads(attended_grad, group)
        g_scr[group] = grads
        terms = (grads.astype(F32) * stacked_heads(attended, group)).T
        delta_scr[group, 0:1, :] = jnp.sum(terms, 0, keepdims=True)
    acc_scr[...] = jnp.zeros_like(acc_scr)

    def step(j, carry):
        keys_at = block_at(j, rows)
        mask = jnp.concatenate([masks[jnp.where(j == here, 1, 0)]] * GROUPS, -1)
        key_grads = []
        value_grads = []
        for group in range(KV):
            keys = kv_all[keys_at, group * HD : (group + 1) * HD]
            values = kv_all[keys_at, KVW + group * HD : KVW + (group + 1) * HD]
            group_q = q_scr[group]
            group_g = g_scr[group]
            scores = mm(keys, group_q, 1, 1) + mask
            prob = jnp.exp(scores - lse[group : group + 1, :])
            prob_grad = mm(values, group_g, 1, 1)
            score_grad = (prob * (prob_grad - delta_scr[group, 0:1, :])).astype(BF16)
            value_grads.append(mm(prob.astype(BF16), group_g))
            key_grads.append(mm(score_grad, group_q))
            acc_scr[group] += mm(keys, score_grad, 0, 0)
        key_grad = jnp.concatenate(key_grads, -1)
        value_grad = jnp.concatenate(value_grads, -1)
        both = jnp.concatenate([key_grad, value_grad], -1).astype(BF16)
        if whole:
            across = (j ^ here) & 1
            distance = (j // 2 - here // 2) & (blocks // 2 - 1)
            kv_grads[across * (blocks // 2) + distance] = both
            turned = rotated(key_grad, cosine[keys_at, :], sine[keys_at, :], -1.0)
            linear = jnp.concatenate([turned, value_grad], -1).astype(BF16)
            weight_scr[...] += mm(normed[keys_at, :], linear, 0, 0)
        else:
            kv_grads[keys_at, :] = both
        return carry

    def clear(j, carry):
        kv_grads[block_at(j, rows), :] = jnp.zeros((rows, kv_grads.shape[1]), BF16)
        return carry

    lax.fori_loop(0, here + 1, step, 0)
    if not whole:
        lax.fori_loop(here + 1, blocks, clear, 0)
    for group in range(KV):
        for g in range(GROUPS):
            head = group * GROUPS + g
            part = acc_scr[group, :, g * rows : (g + 1) * rows]
            query_grad_scr[:, head * HD : (head + 1) * HD] = part.T
    tables = (table_at(cosine, here, rows), table_at(sine, here, rows))
    back = rotated(query_grad_scr[...], *tables, -1.0) * (1.0 / math.sqrt(HD))
    back = back.astype(BF16)
    own_normed = normed[block_at(here, rows), :] if whole else normed[...]
    query_grad = mm(own_normed, back, 0, 0)
    normed_grad[...] = mm(back, query_weight[...], 1, 1)
    if whole:
        outs = (mine, send.at[0], along, send.at[1])
        put_small(
            outs, index[1], tile_scr, query_grad, weight_scr[...], query_weight[...],
            kv_weight[...], gains, ffn_gain_grad,
        )
    else:
        query_weight_grad[...] = query_grad


def small_kernel(
    index, query_grad, kv_grad, query_weight, kv_weight, gains, ffn_gain_grad,
    mine, along, send, tile_scr,
):
    outs = (mine, send.at[0], along, send.at[1])
    for out in outs:
        out[...] = jnp.zeros(out.shape, BF16)
    put_small(
        outs, index[1], tile_scr, query_grad[...], kv_grad[...], query_weight[...], kv_weight[...],
        gains, ffn_gain_grad,
    )


def tail_kernel(
    tokens, gains, normed_grad, middle_grad, kv_weight, cosine, sine, *refs
):
    kv_parts, tokens_grad = refs[:-1], refs[-1]
    rows = normed_grad.shape[0]
    if len(kv_parts) == 1:

        def add(j, total):
            return total + kv_parts[0][block_at(j, rows), :].astype(F32)

        parts = kv_parts[0].shape[0] // rows
        kv_grad = lax.fori_loop(0, parts, add, jnp.zeros((rows, 2 * KVW), F32))
    else:
        column, *moved = kv_parts
        kv_grad = column[0].astype(F32)
        for part in moved:
            kv_grad = kv_grad + part[...].astype(F32)
    key_back = rotated(kv_grad[:, :KVW], cosine[...], sine[...], -1.0)
    back = jnp.concatenate([key_back, kv_grad[:, KVW:]], -1).astype(BF16)
    total = normed_grad[...] + mm(back, kv_weight[...], 1, 1)
    values = tokens[...].T.astype(F32)
    input_grad, _ = rms_back(values, gains[0:1, :], total)
    tokens_grad[...] = (middle_grad[...] + input_grad).astype(BF16).T


def spread_kernel(index, *refs, count):
    *terms, keep, send = refs
    here = index[0]
    rows = keep.shape[1]
    for distance in range(count // 2):
        for across, out in enumerate((keep, send)):
            owner = ((here ^ across) + 2 * distance) & (count - 1)
            at = pl.ds(pl.multiple_of(owner * rows, 16), rows)
            total = terms[0][at, :].astype(F32)
            for term in terms[1:]:
                total = total + term[at, :].astype(F32)
            out[distance] = total.astype(BF16)


def spread_both_kernel(index, mine, along, got, keep_mine, keep_along, send, count):
    spread_kernel(index, mine, got.at[0], keep_mine, send.at[0], count=count)
    spread_kernel(index, along, got.at[1], keep_along, send.at[1], count=count)


def flattened(index, pieces, parts):
    here = index[0]
    if len(pieces) == 1:
        (piece,) = pieces
        total = sum(rows for _, rows in parts)
        count = piece.shape[0] // total
        owners = [(owner, piece, owner * total) for owner in range(count)]
    else:
        count = 2 * pieces[0].shape[0]
        owners = [
            (((here ^ across) + (count - 2 * distance)) & (count - 1), column.at[distance], 0)
            for across, column in enumerate(pieces)
            for distance in range(count // 2)
        ]
    for owner, piece, start in owners:
        for flat, rows in parts:
            at = pl.ds(pl.multiple_of(owner * rows, 16), rows)
            flat[at, :] = piece[start : start + rows, :]
            start += rows


def untile(out, flat, base, columns):
    rows = out.shape[0]
    for tile in range(columns // LANES):
        out[:, tile * LANES : (tile + 1) * LANES] = flat[base : base + rows, :].astype(F32)
        base += rows
    return base


def gate_up_kernel(index, *refs, rows):
    pieces, (gate_out, up_out, flat) = refs[:-3], refs[-3:]
    flattened(index, pieces, [(flat, rows)])
    base = untile(gate_out, flat, 0, gate_out.shape[1])
    untile(up_out, flat, base, up_out.shape[1])


def outputs_kernel(index, *refs, rows, more_rows):
    down_out, out_out, query_out, key_out, value_out, gain_out, flat, small = refs[-8:]
    flattened(index, refs[:-8], [(flat, rows), (small, more_rows)])
    base = 0
    width, rows = down_out.shape
    whole = width // LANES * LANES
    for tile in range(whole // LANES):
        part = flat[base : base + rows, :].astype(F32)
        down_out[tile * LANES : (tile + 1) * LANES, :] = part.T
        base += rows
    half = rows // 2
    rest = flat[base : base + half, :].astype(F32).T
    down_out[whole:, :] = jnp.concatenate([rest[: width - whole], rest[width - whole :]], -1)
    base = untile(out_out, flat, base + half, whole)
    rows = out_out.shape[0]
    out_out[:, whole:] = flat[base : base + rows, : width - whole].astype(F32)
    base = untile(query_out, small, 0, whole)
    tile = small[base : base + rows, :].astype(F32)
    query_out[:, whole:] = tile[:, : width - whole]
    gain_out[...] = tile[:, width - whole : width - whole + 8].T
    base += rows
    both = [
        small[base + at * rows : base + (at + 1) * rows, :].astype(F32)
        for at in range(2 * KVW // LANES)
    ]
    both = jnp.concatenate(both, -1)
    key_out[...] = both[:, :KVW]
    value_out[...] = both[:, KVW:]


def swap(value, axis, bit):
    count = lax.axis_size(axis)
    return lax.ppermute(value, axis, [(i, i ^ (1 << bit)) for i in range(count)])


def gathered_ws(value):
    along = swap(value, "ws", 1)
    return value, swap(value, "ws", 0), along, swap(along, "ws", 0)


def gathered_ctx(value):
    count = lax.axis_size("ctx")
    if count != 8:
        return (lax.all_gather(value, "ctx", axis=0, tiled=True),)
    column = jnp.stack([value] + [shifted(value, by, False) for by in (1, 2, 3)])
    return column, swap(column, "ctx", 0)


def shifted(value, by, upward_only):
    count = lax.axis_size("ctx")
    pairs = [(i, i + 2 * by) for i in range(count)]
    if upward_only:
        pairs = [(i, j) for i, j in pairs if j < count]
    return lax.ppermute(value, "ctx", [(i, j % count) for i, j in pairs])


def rms_scale(values, gain_vec):
    return values * lax.rsqrt(jnp.mean(values * values, -1, keepdims=True) + EPS) * gain_vec


def added(*values):
    total = values[0].astype(F32)
    for value in values[1:]:
        total = total + value.astype(F32)
    return total.astype(values[0].dtype)


def scattered_ctx(values, counts):
    count = lax.axis_size("ctx")
    value = jnp.concatenate(
        [v.reshape(count, rows, LANES) for v, rows in zip(values, counts)], 1
    ).reshape(-1, LANES)
    parts = lax.all_to_all(value, "ctx", split_axis=0, concat_axis=0, tiled=True)
    parts = parts.reshape(count, -1, LANES).astype(F32)
    return jnp.sum(parts, 0).astype(value.dtype)


def rope_tables(positions):
    frequency = jnp.exp(jnp.arange(HD // 2).astype(F32) * (-2.0 * math.log(THETA) / HD))
    angles = positions.astype(F32)[:, None] * frequency[None, :]
    return jnp.cos(angles), jnp.sin(angles)


def turned_heads(values, cosine, sine):
    heads = values.reshape(values.shape[0], -1, 2, HD // 2)
    cosine, sine = cosine[:, None], sine[:, None]
    first, second = heads[:, :, 0], heads[:, :, 1]
    pair = [first * cosine - second * sine, second * cosine + first * sine]
    return jnp.stack(pair, 2).reshape(values.shape)


def scattered_parts(column, downward_only):
    count = lax.axis_size("ctx")
    parts = []
    for by in (1, 2, 3):
        pairs = [(i, i + 2 * by) for i in range(count)]
        if downward_only:
            pairs = [(i, j) for i, j in pairs if j >= count]
        parts.append(lax.ppermute(column[by], "ctx", [(i, j % count) for i, j in pairs]))
    return parts


def spread(index, terms):
    count = lax.axis_size("ctx")
    shape = shaped((count // 2, terms[0].shape[0] // count, LANES), BF16)
    return call(
        functools.partial(spread_kernel, count=count),
        (shape, shape),
        (index, *terms),
        micros=2,
        smem=1,
    )


def spread_both(index, mine, along, got):
    count = lax.axis_size("ctx")
    shape = shaped((count // 2, mine.shape[0] // count, LANES), BF16)
    return call(
        functools.partial(spread_both_kernel, count=count),
        (shape, shape, shaped((2,) + shape.shape, BF16)),
        (index, mine, along, got),
        micros=3,
        smem=1,
    )


def padded_rows(rows, count):
    return -(-rows // (16 * count)) * 16 * count


def body(
    tokens,
    attn_gain,
    query_weight,
    key_weight,
    value_weight,
    output_weight,
    ffn_gain,
    gate_weight,
    up_weight,
    down_weight,
    out_grad,
):
    seq_count, rows, width = tokens.shape
    ctx_count = lax.axis_size("ctx")
    owners = lax.axis_size("ws")
    slice_rows = query_weight.shape[0]
    ff = gate_weight.shape[1]
    wide = -(-width // LANES) * LANES
    by_hops = ctx_count == 8
    tokens = tokens.reshape(rows, width).T
    out_grad = out_grad.reshape(rows, width).T
    ctx_index = lax.axis_index("ctx")
    index = jnp.stack([ctx_index, lax.axis_index("ws")]).astype(jnp.int32)

    if by_hops:
        behind_two = shifted(tokens, 2, True)

    gains = jnp.concatenate([attn_gain, ffn_gain]).reshape(2, slice_rows)
    packed = jnp.concatenate(
        [
            jnp.concatenate([key_weight, value_weight, query_weight], -1),
            jnp.pad(gains, ((0, 14), (0, 2 * KVW + width - slice_rows))),
        ],
        0,
    )
    packs = gathered_ws(packed)
    in_weight = jnp.concatenate([gate_weight, up_weight, output_weight], -1)
    in_along = swap(in_weight, "ws", 1)
    down_along = swap(down_weight, "ws", 1)

    def wide_tables(positions):
        cosine, sine = rope_tables(positions)
        return jnp.concatenate([cosine] * 4, -1), jnp.concatenate([-sine, sine] * 2, -1)

    first_pos = ctx_index * rows
    cosine, sine = wide_tables(first_pos + jnp.arange(rows, dtype=jnp.int32))
    if by_hops:
        tables = wide_tables(jnp.arange(ctx_count * rows, dtype=jnp.int32))
        later_tokens, tables = lax.optimization_barrier((tokens, tables))
        behind_one = shifted(later_tokens, 1, True)
        mate = swap(later_tokens, "ctx", 0)
        behind_three = shifted(behind_two, 1, True)
    else:
        tables = (cosine, sine)

    places = (0, 1, 4) if by_hops else (0,)
    late_places = (2, 5, 3, 6, 7) if by_hops else ()
    early = (tokens, mate, behind_two) if by_hops else (tokens,)
    early_normed, early_kv, queries, full_query, full_kv, gains = call(
        functools.partial(early_kernel, places=places, slice_rows=slice_rows),
        (
            shaped((len(places), rows, width), BF16),
            shaped((len(places), rows, 2 * KVW), BF16),
            shaped((rows, width), BF16),
            shaped((width, width), BF16),
            shaped((width, 2 * KVW), BF16),
            shaped((8, width), F32),
        ),
        (index,) + packs + tables + early,
        scratch=(
            pltpu.VMEM((owners * 16, 2 * LANES), BF16),
            pltpu.VMEM((len(places), width, rows), BF16),
        ),
        micros=6,
        smem=1,
        vmem=60,
    )
    if by_hops:
        behind_three, queries = lax.optimization_barrier((behind_three, queries))
        late = (
            behind_one,
            swap(behind_two, "ctx", 0),
            swap(behind_one, "ctx", 0),
            behind_three,
            swap(behind_three, "ctx", 0),
        )
        normed_shape = (shaped((ctx_count * rows, width), BF16),)
        raw_scr = (pltpu.VMEM((len(late_places), width, rows), BF16),)
    else:
        tokens_all = lax.all_gather(tokens.T, "ctx", axis=0, tiled=True).astype(F32)
        normed_all = rms_scale(tokens_all, gains[0]).astype(BF16)
        linear = jnp.dot(normed_all, full_kv, preferred_element_type=F32)
        full_tables = rope_tables(jnp.arange(ctx_count * rows, dtype=jnp.int32))
        early_kv = jnp.concatenate(
            [turned_heads(linear[:, :KVW], *full_tables), linear[:, KVW:]], -1
        ).astype(BF16)
        late = ()
        normed_shape = ()
        raw_scr = ()

    late, in_weight, down_weight, in_along = lax.optimization_barrier(
        (late, in_weight, down_weight, in_along)
    )
    in_pieces = (in_weight, swap(in_weight, "ws", 0), in_along, swap(in_along, "ws", 0))
    down_core = swap(down_weight, "ws", 0)

    attended, lse, kv_all, *normed_out = call(
        functools.partial(forward_kernel, places=places, late_places=late_places),
        (
            shaped((rows, width), F32),
            shaped((8, GROUPS * rows), F32),
            shaped((ctx_count * rows, 2 * KVW), BF16),
            *normed_shape,
        ),
        (index, queries, early_normed, early_kv, full_kv, gains, *tables, *late),
        scratch=(
            *raw_scr,
            pltpu.VMEM((KV, GROUPS * rows, HD), BF16),
            pltpu.VMEM((KV, HD, GROUPS * rows), F32),
            pltpu.VMEM((KV, 8, GROUPS * rows), F32),
            pltpu.VMEM((KV, 8, GROUPS * rows), F32),
            pltpu.VMEM((2, rows, rows), F32),
        ),
        micros=20,
        smem=1,
        vmem=60,
    )

    attended, down_along = lax.optimization_barrier((attended, down_along))
    down_pieces = (down_weight, down_core, down_along, swap(down_along, "ws", 0))

    first_count = padded_rows(2 * slice_rows * ff // LANES, ctx_count)
    second_count = padded_rows(((ff // owners) * width + slice_rows * wide) // LANES, ctx_count)
    small_count = padded_rows(slice_rows * (wide + 2 * KVW) // LANES, ctx_count)
    first_rows, second_rows, small_rows = (
        rows_of // ctx_count for rows_of in (first_count, second_count, small_count)
    )

    def tile_shapes(rows_of):
        return (
            shaped((rows_of, LANES), BF16),
            shaped((rows_of, LANES), BF16),
            shaped((2, rows_of, LANES), BF16),
        )

    layer_out, middle_grad, attended_grad, ffn_gain_grad, *tiles = call(
        ffn_kernel,
        (
            shaped((width, rows), BF16),
            shaped((rows, width), F32),
            shaped((rows, width), BF16),
            shaped((8, width), F32),
            *tile_shapes(first_count),
            *tile_shapes(second_count),
        ),
        (index, tokens, attended, gains, out_grad) + in_pieces + down_pieces,
        scratch=(
            pltpu.VMEM((width, 2 * ff + width), BF16),
            pltpu.VMEM((ff, width), BF16),
            pltpu.VMEM((rows, width), F32),
            pltpu.VMEM((rows, width), F32),
            pltpu.VMEM((width, 2 * ff), BF16),
            pltpu.VMEM((ff, wide), BF16),
        ),
        micros=14,
        smem=1,
        vmem=60,
    )

    in_mine, in_along, in_send, mine, along, send = tiles
    in_got = swap(in_send, "ws", 0)
    got = swap(send, "ws", 0)
    in_crossing = added(in_along, in_got[1])
    if by_hops:
        keep_mine, keep_along, to_mate = spread_both(index, mine, along, got)
    else:
        to_mate = added(along, got[1])
    attended_grad, in_crossing, to_mate = lax.optimization_barrier(
        (attended_grad, in_crossing, to_mate)
    )
    in_crossed = swap(in_crossing, "ws", 1)
    from_mate = swap(to_mate, "ctx", 0) if by_hops else swap(to_mate, "ws", 1)

    tile_scr = pltpu.VMEM((width, wide + 2 * KVW), BF16)
    if by_hops:
        kv_shape = shaped((ctx_count, rows, 2 * KVW), BF16)
        backward_normed = normed_out[0]
        more_shapes = tile_shapes(small_count)
        more_scratch = (tile_scr, pltpu.VMEM((width, 2 * KVW), F32))
    else:
        kv_shape = shaped((ctx_count * rows, 2 * KVW), BF16)
        backward_normed = early_normed[0]
        more_shapes = (shaped((width, width), F32),)
        more_scratch = ()
    kv_grads, normed_grad, *small = call(
        backward_kernel,
        (kv_shape, shaped((rows, width), F32), *more_shapes),
        (
            index, queries, kv_all, attended, attended_grad, lse, backward_normed, full_query,
            full_kv, gains, ffn_gain_grad, *tables,
        ),
        scratch=(
            *more_scratch,
            pltpu.VMEM((KV, GROUPS * rows, HD), BF16),
            pltpu.VMEM((KV, GROUPS * rows, HD), BF16),
            pltpu.VMEM((KV, 8, GROUPS * rows), F32),
            pltpu.VMEM((KV, HD, GROUPS * rows), F32),
            pltpu.VMEM((rows, width), F32),
            pltpu.VMEM((2, rows, rows), F32),
        ),
        micros=23,
        smem=1,
        vmem=32 if by_hops else 60,
    )
    if not by_hops:
        linear = turned_heads(kv_grads[:, :KVW].astype(F32), full_tables[0], -full_tables[1])
        linear = jnp.concatenate([linear.astype(BF16), kv_grads[:, KVW:]], -1)
        kv_weight_grad = jnp.einsum("nd,nh->dh", normed_all, linear, preferred_element_type=F32)
        small = call(
            small_kernel,
            tile_shapes(small_count),
            (index, small[0], kv_weight_grad, full_query, full_kv, gains, ffn_gain_grad),
            scratch=(tile_scr,),
            smem=1,
        )
    kv_grads, small, in_crossed, from_mate = lax.optimization_barrier(
        (kv_grads, tuple(small), in_crossed, from_mate)
    )
    small_mine, small_along, small_send = small
    small_got = swap(small_send, "ws", 0)
    small_crossed = swap(added(small_along, small_got[1]), "ws", 1)

    if by_hops:
        in_keep, in_to_mate = spread(index, (in_mine, in_got[0], in_crossed))
        in_from_mate = swap(in_to_mate, "ctx", 0)
        crossed = swap(added(keep_along, from_mate[1]), "ws", 1)
        in_from_mate, crossed, small_crossed = lax.optimization_barrier(
            (in_from_mate, crossed, small_crossed)
        )
        small_keep, small_to_mate = spread(index, (small_mine, small_got[0], small_crossed))
        small_to_mate, kv_to_mate = lax.optimization_barrier(
            (small_to_mate, kv_grads[ctx_count // 2 :])
        )
        small_from_mate = swap(small_to_mate, "ctx", 0)
        kv_from_mate = swap(kv_to_mate, "ctx", 0)
        in_column = added(in_keep, in_from_mate)
        in_share = added(in_column[0], *scattered_parts(in_column, False))
        column = jnp.concatenate(
            [added(keep_mine, from_mate[0], crossed), added(small_keep, small_from_mate)], 1
        )
        share = added(column[0], *scattered_parts(column, False))
        kv_column = added(kv_grads[: ctx_count // 2], kv_from_mate)
        kv_parts = (kv_column, *scattered_parts(kv_column, True))
    else:
        kv_parts = (lax.all_to_all(kv_grads, "ctx", split_axis=0, concat_axis=0, tiled=True),)
        in_total = added(in_mine, in_got[0], in_crossed)
        total = added(mine, got[0], from_mate)
        small_total = added(small_mine, small_got[0], small_crossed)
        in_share = scattered_ctx((in_total,), (first_rows,))
        share = scattered_ctx((total, small_total), (second_rows, small_rows))
    in_pieces = gathered_ctx(in_share)
    pieces = gathered_ctx(share)

    tokens_grad = call(
        tail_kernel,
        shaped((width, rows), BF16),
        (
            tokens, gains, normed_grad, middle_grad, full_kv, cosine, sine, *kv_parts,
        ),
        micros=4,
        vmem=16 if by_hops else 60,
    )

    gate_weight_grad, up_weight_grad = call(
        functools.partial(gate_up_kernel, rows=first_rows),
        (shaped(gate_weight.shape, F32), shaped(up_weight.shape, F32)),
        (index,) + in_pieces,
        scratch=(pltpu.VMEM((first_count, LANES), BF16),),
        micros=3,
        smem=1,
    )
    (
        down_weight_grad,
        output_weight_grad,
        query_weight_grad,
        key_weight_grad,
        value_weight_grad,
        gain_grads,
    ) = call(
        functools.partial(outputs_kernel, rows=second_rows, more_rows=small_rows),
        (
            shaped(down_weight.shape[::-1], F32),
            shaped(output_weight.shape, F32),
            shaped(query_weight.shape, F32),
            shaped(key_weight.shape, F32),
            shaped(value_weight.shape, F32),
            shaped((8, slice_rows), F32),
        ),
        (index,) + pieces,
        scratch=(pltpu.VMEM((second_count, LANES), BF16), pltpu.VMEM((small_count, LANES), BF16)),
        micros=3,
        smem=1,
    )
    return (
        layer_out.T.reshape(seq_count, rows, width),
        tokens_grad.T.reshape(seq_count, rows, width),
        gain_grads[0],
        query_weight_grad,
        key_weight_grad,
        value_weight_grad,
        output_weight_grad,
        gain_grads[1],
        gate_weight_grad,
        up_weight_grad,
        down_weight_grad.T,
    )


def solution(mesh):
    in_specs = (
        P("ws", "ctx", None),
        P("ws"),
        P("ws", None),
        P("ws", None),
        P("ws", None),
        P("ws", None),
        P("ws"),
        P("ws", None),
        P("ws", None),
        P("ws", None),
        P("ws", "ctx", None),
    )
    out_specs = (
        P("ws", "ctx", None),
        P("ws", "ctx", None),
        P("ws"),
        P("ws", None),
        P("ws", None),
        P("ws", None),
        P("ws", None),
        P("ws"),
        P("ws", None),
        P("ws", None),
        P("ws", None),
    )
    return jax.shard_map(body, mesh=mesh, in_specs=in_specs, out_specs=out_specs, check_vma=False)
```

profile of v0, /device:TPU:0, one launch (start us, length us, event | category | flops | bytes accessed | tf_op | source)
XLA Modules:
  0.0 214.6 jit_solution(6133967462969667)
XLA Ops:
  0.6 0.7 pad_maximum_fusion.7
  1.5 1.1 fusion.7.p0
  2.6 3.0 %collective-permute-start.3 = (bf16[160,960]{1,0:T(8,128)(2,1)S(1)}, bf16[160,960]{1,0:T(8,128)(2,1)S(1)}, u32[]{:S(2)}, u32[]{:S(2)}) collective-permute-start(bf16[160,960]{1,0:T(8,128)(2,1)S(1)} %fusion.7.p0), channel_id=1, source_target_pairs={{0,2},{1,3},{2,0},{3,1},{4,6},{5,7},{6,4},{7,5},{8,10},{9,11},{10,... | collective-permute-start | bytes 921608 | tf_op jit(solution)/shard_map/ppermute | solution.py:593
  5.6 5.2 %collective-permute-start = (bf16[576,256]{1,0:T(8,128)(2,1)}, bf16[576,256]{1,0:T(8,128)(2,1)}, u32[]{:S(2)}, u32[]{:S(2)}) collective-permute-start(bf16[576,256]{1,0:T(8,128)(2,1)} %bitcast.73), channel_id=1, source_target_pairs={{0,16},{4,20},{8,24},{12,28},{1,17},{5,21},{9,25},{13,29},{2,18},{... | collective-permute-start | bytes 884744 | tf_op jit(solution)/shard_map/ppermute | solution.py:614
  10.8 3.7 %fusion.6 = (f32[2048,32]{1,0:T(8,128)S(1)}, f32[2048,32]{1,0:T(8,128)S(1)}, f32[2048,32]{1,0:T(8,128)S(1)}) fusion(f32[32]{0:T(128)S(1)} %multiply_exponential_fusion, f32[2048]{0:T(1024)S(1)} %iota_convert_fusion), kind=kLoop, calls=%fused_computation.27 | loop fusion | flops 131072 | bytes 794752 | tf_op jit(solution)/shard_map/neg | solution.py:734
  14.6 3.0 %pad_maximum_fusion = (f32[2048,128]{1,0:T(8,128)}, f32[2048,128]{1,0:T(8,128)}) fusion(f32[2048,32]{1,0:T(8,128)S(1)} %get-tuple-element.160, f32[2048,32]{1,0:T(8,128)S(1)} %get-tuple-element.159, f32[2048,32]{1,0:T(8,128)S(1)} %get-tuple-element.158), kind=kLoop, calls=%fused_computation.5 | loop fusion | flops 1572864 | bytes 2883584 | tf_op jit(solution)/shard_map/concatenate | solution.py:734
  17.6 1.5 collective-permute-start.5
  19.2 4.2 %collective-permute-start.6 = (bf16[576,256]{1,0:T(8,128)(2,1)S(1)}, bf16[576,256]{1,0:T(8,128)(2,1)}, u32[]{:S(2)}, u32[]{:S(2)}) collective-permute-start(bf16[576,256]{1,0:T(8,128)(2,1)S(1)} %bitcast.77), channel_id=1, source_target_pairs={{0,8},{4,12},{8,16},{12,20},{16,24},{20,28},{1,9},{5,13},{9,17},{1... | collective-permute-start | bytes 884744 | tf_op jit(solution)/shard_map/ppermute | solution.py:614
  23.6 3.2 %collective-permute-done.5.refs_1_ = bf16[576,256]{1,0:T(8,128)(2,1)S(1)} collective-permute-done((bf16[576,256]{1,0:T(8,128)(2,1)S(1)}, bf16[576,256]{1,0:T(8,128)(2,1)S(1)}, u32[]{:S(2)}, u32[]{:S(2)}) %collective-permute-start.5) | collective-permute-done | bytes 294944 | tf_op jit(solution)/shard_map/ppermute | solution.py:593
  26.8 0.7 copy-done.32
  28.7 4.3 %collective-permute-start.1 = (bf16[576,256]{1,0:T(8,128)(2,1)}, bf16[576,256]{1,0:T(8,128)(2,1)}, u32[]{:S(2)}, u32[]{:S(2)}) collective-permute-start(bf16[576,256]{1,0:T(8,128)(2,1)} %collective-permute-done.refs_2_), channel_id=1, source_target_pairs={{0,8},{4,12},{8,16},{12,20},{16,24},{20,28},{1,9},{5,13},{9,17},{1... | collective-permute-start | bytes 884744 | tf_op jit(solution)/shard_map/ppermute | solution.py:614
  33.0 1.5 collective-permute-start.7
  35.3 0.8 copy-done.31
  36.0 6.3 %shard_map.194 = (bf16[3,256,576]{2,1,0:T(8,128)(2,1)}, bf16[3,256,384]{2,1,0:T(8,128)(2,1)}, bf16[256,576]{1,0:T(8,128)(2,1)}, bf16[576,576]{1,0:T(8,128)(2,1)}...) custom-call(s32[2]{0:T(128)} %pad_add_fusion.index, bf16[160,960]{1,0:T(8,128)(2,1)} %copy-done.24, ...), custom_call_target="tpu_custom_call" | custom-call | flops 6000000000 | tf_op jit(solution)/shard_map/pallas_call | solution.py:38
  42.3 1.4 collective-permute-start.9
  44.0 1.6 collective-permute-start.11
  45.5 4.0 %collective-permute-done.8.refs_2_ = bf16[576,256]{1,0:T(8,128)(2,1)} collective-permute-done((bf16[576,256]{1,0:T(8,128)(2,1)}, bf16[576,256]{1,0:T(8,128)(2,1)}, u32[]{:S(2)}, u32[]{:S(2)}) %collective-permute-start.8) | collective-permute-done | bytes 294944 | tf_op jit(solution)/shard_map/ppermute | solution.py:593
  49.6 4.1 %collective-permute-done.9.refs_4_ = bf16[576,256]{1,0:T(8,128)(2,1)S(1)} collective-permute-done((bf16[576,256]{1,0:T(8,128)(2,1)}, bf16[576,256]{1,0:T(8,128)(2,1)S(1)}, u32[]{:S(2)}, u32[]{:S(2)}) %collective-permute-start.9) | collective-permute-done | bytes 294944 | tf_op jit(solution)/shard_map/ppermute | solution.py:593
  54.6 7.4 %shard_map.195 = (f32[256,576]{1,0:T(8,128)}, f32[8,768]{1,0:T(8,128)}, bf16[2048,384]{1,0:T(8,128)(2,1)}, bf16[2048,576]{1,0:T(8,128)(2,1)}) custom-call(s32[2]{0:T(128)} %pad_add_fusion.index, bf16[256,576]{1,0:T(8,128)(2,1)} %get-tuple-element.84.queries, bf16[3,256,576]{2,1,0:T(8,128)(2,1)} %get-tuple-element.85.early_normed, ...), custom_call_target="tpu_custom_call" | custom-call | flops 20000000000 | tf_op jit(solution)/shard_map/pallas_call | solution.py:38
  62.0 0.9 collective-permute-done.11.wd2
  63.8 1.1 collective-permute-done.15.wd3
  65.5 0.8 copy-done.28
  66.3 16.7 %shard_map.196 = (bf16[576,256]{1,0:T(8,128)(2,1)}, f32[256,576]{1,0:T(8,128)}, bf16[256,576]{1,0:T(8,128)(2,1)}, f32[8,576]{1,0:T(8,128)}, bf16[3456,128]{1,0:T...) custom-call(s32[2]{0:T(128)} %pad_add_fusion.index, ...), custom_call_target="tpu_custom_call" | custom-call | flops 14000000000 | tf_op jit(solution)/shard_map/pallas_call | solution.py:38
  84.0 4.7 %collective-permute-done.17.got = bf16[2,2560,128]{2,1,0:T(8,128)(2,1)S(1)} collective-permute-done((bf16[2,2560,128]{2,1,0:T(8,128)(2,1)}, bf16[2,2560,128]{2,1,0:T(8,128)(2,1)S(1)}, u32[]{:S(2)}, u32[]{:S(2)}) %collective-permute-start.17) | collective-permute-done | bytes 1310752 | tf_op jit(solution)/shard_map/ppermute | solution.py:593
  88.8 1.1 copy-done.6
  89.9 1.1 copy-done.7
  91.0 0.8 shard_map.197
  93.0 3.2 %collective-permute-start.19 = (bf16[2,4,320,128]{3,2,1,0:T(8,128)(2,1)S(1)}, bf16[2,4,320,128]{3,2,1,0:T(8,128)(2,1)S(1)}, u32[]{:S(2)}, u32[]{:S(2)}) collective-permute-start(bf16[2,4,320,128]{3,2,1,0:T(8,128)(2,1)S(1)} %get-tuple-element.122), channel_id=1, source_target_pairs={{0,4},{4,0},{8,12},{12,8},{16,20},{20,16},{24,28},{28,24},{1,5},{5... | collective-permute-start | bytes 1966088 | tf_op jit(solution)/shard_map/ppermute | solution.py:593
  96.2 5.6 %shard_map.198 = (bf16[8,256,384]{2,1,0:T(8,128)(2,1)S(1)}, f32[256,576]{1,0:T(8,128)S(1)}, bf16[1152,128]{1,0:T(8,128)(2,1)S(1)}, bf16[1152,128]{1,0:T(8,128)(2,1)S(1)}, bf16[2,1152,128]{2,1,0:T(8,128)(2,1)S(1)}) custom-call(s32[2]{0:T(128)S(1)} %copy-done.4, bf16[256,576]{1,0:T(8,128)(2,1)S(1)} %copy-done.11, bf16[2048,384]{1,0:T(8,128)(2,1)S(1)} %copy-done.13, ...), custom_call_target="tpu_custom_call" | custom-call | flops 23000000512 | tf_op jit(solution)/shard_map/pallas_call | solution.py:38
  101.9 9.0 %collective-permute-done.19 = bf16[2,4,320,128]{3,2,1,0:T(8,128)(2,1)S(1)} collective-permute-done((bf16[2,4,320,128]{3,2,1,0:T(8,128)(2,1)S(1)}, bf16[2,4,320,128]{3,2,1,0:T(8,128)(2,1)S(1)}, u32[]{:S(2)}, u32[]{:S(2)}) %collective-permute-start.19) | collective-permute-done | bytes 655392 | tf_op jit(solution)/shard_map/ppermute | solution.py:593
  110.9 3.2 %collective-permute-done.18.refs_2_ = bf16[3456,128]{1,0:T(8,128)(2,1)S(1)} collective-permute-done((bf16[3456,128]{1,0:T(8,128)(2,1)S(1)}, bf16[3456,128]{1,0:T(8,128)(2,1)S(1)}, u32[]{:S(2)}, u32[]{:S(2)}) %collective-permute-start.18) | collective-permute-done | bytes 884768 | tf_op jit(solution)/shard_map/ppermute | solution.py:593
  114.9 0.9 shard_map.199
  115.8 3.2 %collective-permute-start.21 = (bf16[4,432,128]{2,1,0:T(8,128)(2,1)S(1)}, bf16[4,432,128]{2,1,0:T(8,128)(2,1)S(1)}, u32[]{:S(2)}, u32[]{:S(2)}) collective-permute-start(bf16[4,432,128]{2,1,0:T(8,128)(2,1)S(1)} %get-tuple-element.128), channel_id=1, source_target_pairs={{0,4},{4,0},{8,12},{12,8},{16,20},{20,16},{24,28},{28,24},{1,5},{5... | collective-permute-start | bytes 1327112 | tf_op jit(solution)/shard_map/ppermute | solution.py:593
  119.2 0.8 collective-permute-start.23
  120.0 4.8 %collective-permute-done.22 = bf16[4,320,128]{2,1,0:T(8,128)(2,1)S(1)} collective-permute-done((bf16[4,320,128]{2,1,0:T(8,128)(2,1)S(1)}, bf16[4,320,128]{2,1,0:T(8,128)(2,1)S(1)}, u32[]{:S(2)}, u32[]{:S(2)}) %collective-permute-start.22) | collective-permute-done | bytes 327712 | tf_op jit(solution)/shard_map/ppermute | solution.py:593
  124.9 4.7 %collective-permute-done.21 = bf16[4,432,128]{2,1,0:T(8,128)(2,1)S(1)} collective-permute-done((bf16[4,432,128]{2,1,0:T(8,128)(2,1)S(1)}, bf16[4,432,128]{2,1,0:T(8,128)(2,1)S(1)}, u32[]{:S(2)}, u32[]{:S(2)}) %collective-permute-start.21) | collective-permute-done | bytes 442400 | tf_op jit(solution)/shard_map/ppermute | solution.py:593
  129.6 1.2 collective-permute-done.23.refs_2_
  130.9 5.7 %collective-permute-start.36 = (bf16[432,128]{1,0:T(8,128)(2,1)S(1)}, bf16[432,128]{1,0:T(8,128)(2,1)S(1)}, u32[]{:S(2)}, u32[]{:S(2)}) collective-permute-start(bf16[432,128]{1,0:T(8,128)(2,1)S(1)} %get-tuple-element.155), channel_id=1, source_target_pairs={{0,8},{4,12},{8,16},{12,20},{16,24},{20,28},{24,0},{28,4},{1,9},{5... | collective-permute-start | bytes 331784 | tf_op jit(solution)/shard_map/ppermute | solution.py:659
  136.7 10.3 %collective-permute-start.37 = (bf16[432,128]{1,0:T(8,128)(2,1)S(1)}, bf16[432,128]{1,0:T(8,128)(2,1)S(1)}, u32[]{:S(2)}, u32[]{:S(2)}) collective-permute-start(bf16[432,128]{1,0:T(8,128)(2,1)S(1)} %get-tuple-element.157), channel_id=1, source_target_pairs={{0,16},{4,20},{8,24},{12,28},{16,0},{20,4},{24,8},{28,12},{1,17},{... | collective-permute-start | bytes 331784 | tf_op jit(solution)/shard_map/ppermute | solution.py:659
  147.0 0.7 shard_map.200
  147.7 4.0 %collective-permute-start.28 = (bf16[4,144,128]{2,1,0:T(8,128)(2,1)S(1)}, bf16[4,144,128]{2,1,0:T(8,128)(2,1)S(1)}, u32[]{:S(2)}, u32[]{:S(2)}) collective-permute-start(bf16[4,144,128]{2,1,0:T(8,128)(2,1)S(1)} %get-tuple-element.138), channel_id=1, source_target_pairs={{0,4},{4,0},{8,12},{12,8},{16,20},{20,16},{24,28},{28,24},{1,5},{5... | collective-permute-start | bytes 442376 | tf_op jit(solution)/shard_map/ppermute | solution.py:593
  151.9 2.4 %collective-permute-done.37 = bf16[432,128]{1,0:T(8,128)(2,1)S(1)} collective-permute-done((bf16[432,128]{1,0:T(8,128)(2,1)S(1)}, bf16[432,128]{1,0:T(8,128)(2,1)S(1)}, u32[]{:S(2)}, u32[]{:S(2)}) %collective-permute-start.37) | collective-permute-done | bytes 110624 | tf_op jit(solution)/shard_map/ppermute | solution.py:659
  154.3 2.9 %collective-permute-start.39 = (bf16[432,128]{1,0:T(8,128)(2,1)S(1)}, bf16[432,128]{1,0:T(8,128)(2,1)S(1)}, u32[]{:S(2)}, u32[]{:S(2)}) collective-permute-start(bf16[432,128]{1,0:T(8,128)(2,1)S(1)} %fusion.13), channel_id=1, source_target_pairs={{0,8},{4,12},{8,16},{12,20},{16,24},{20,28},{24,0},{28,4},{1,9},{5... | collective-permute-start | bytes 331784 | tf_op jit(solution)/shard_map/ppermute | solution.py:614
  157.6 2.1 collective-permute-start.41
  159.8 2.3 %collective-permute-done.39 = bf16[432,128]{1,0:T(8,128)(2,1)S(1)} collective-permute-done((bf16[432,128]{1,0:T(8,128)(2,1)S(1)}, bf16[432,128]{1,0:T(8,128)(2,1)S(1)}, u32[]{:S(2)}, u32[]{:S(2)}) %collective-permute-start.39) | collective-permute-done | bytes 110624 | tf_op jit(solution)/shard_map/ppermute | solution.py:614
  162.1 0.9 collective-permute-start.30
  162.9 3.9 %collective-permute-done.40 = bf16[432,128]{1,0:T(8,128)(2,1)S(1)} collective-permute-done((bf16[432,128]{1,0:T(8,128)(2,1)S(1)}, bf16[432,128]{1,0:T(8,128)(2,1)S(1)}, u32[]{:S(2)}, u32[]{:S(2)}) %collective-permute-start.40) | collective-permute-done | bytes 110624 | tf_op jit(solution)/shard_map/ppermute | solution.py:614
  166.8 3.9 %collective-permute-start.31 = (bf16[464,128]{1,0:T(8,128)(2,1)S(1)}, bf16[464,128]{1,0:T(8,128)(2,1)S(1)}, u32[]{:S(2)}, u32[]{:S(2)}) collective-permute-start(bf16[464,128]{1,0:T(8,128)(2,1)S(1)} %get-tuple-element.153), channel_id=1, source_target_pairs={{0,24},{4,28},{8,0},{12,4},{16,8},{20,12},{24,16},{28,20},{1,25},{... | collective-permute-start | bytes 356360 | tf_op jit(solution)/shard_map/ppermute | solution.py:659
  170.8 3.8 %collective-permute-start.42 = (bf16[4,432,128]{2,1,0:T(8,128)(2,1)S(1)}, bf16[4,432,128]{2,1,0:T(8,128)(2,1)S(1)}, u32[]{:S(2)}, u32[]{:S(2)}) collective-permute-start(bf16[4,432,128]{2,1,0:T(8,128)(2,1)S(1)} %pad_maximum_fusion.3.refs_0_), channel_id=1, source_target_pairs={{0,4},{4,0},{8,12},{12,8},{16,20},{20,16},{24,28},{28,24},{1,5},{5... | collective-permute-start | bytes 1327112 | tf_op jit(solution)/shard_map/ppermute | solution.py:593
  174.6 1.3 collective-permute-done.30
  176.0 3.1 %collective-permute-start.32 = (bf16[464,128]{1,0:T(8,128)(2,1)S(1)}, bf16[464,128]{1,0:T(8,128)(2,1)S(1)}, u32[]{:S(2)}, u32[]{:S(2)}) collective-permute-start(bf16[464,128]{1,0:T(8,128)(2,1)S(1)} %fusion.10), channel_id=1, source_target_pairs={{0,8},{4,12},{8,16},{12,20},{16,24},{20,28},{24,0},{28,4},{1,9},{5... | collective-permute-start | bytes 356360 | tf_op jit(solution)/shard_map/ppermute | solution.py:614
  179.1 1.8 collective-permute-start.33
  180.8 0.7 collective-permute-start.34
  181.8 2.5 %collective-permute-done.32 = bf16[464,128]{1,0:T(8,128)(2,1)S(1)} collective-permute-done((bf16[464,128]{1,0:T(8,128)(2,1)S(1)}, bf16[464,128]{1,0:T(8,128)(2,1)S(1)}, u32[]{:S(2)}, u32[]{:S(2)}) %collective-permute-start.32) | collective-permute-done | bytes 118816 | tf_op jit(solution)/shard_map/ppermute | solution.py:614
  184.3 4.1 %collective-permute-done.33 = bf16[464,128]{1,0:T(8,128)(2,1)S(1)} collective-permute-done((bf16[464,128]{1,0:T(8,128)(2,1)S(1)}, bf16[464,128]{1,0:T(8,128)(2,1)S(1)}, u32[]{:S(2)}, u32[]{:S(2)}) %collective-permute-start.33) | collective-permute-done | bytes 118816 | tf_op jit(solution)/shard_map/ppermute | solution.py:614
  188.4 3.8 %collective-permute-start.35 = (bf16[4,464,128]{2,1,0:T(8,128)(2,1)S(1)}, bf16[4,464,128]{2,1,0:T(8,128)(2,1)S(1)}, u32[]{:S(2)}, u32[]{:S(2)}) collective-permute-start(bf16[4,464,128]{2,1,0:T(8,128)(2,1)S(1)} %pad_maximum_fusion.2.refs_0_), channel_id=1, source_target_pairs={{0,4},{4,0},{8,12},{12,8},{16,20},{20,16},{24,28},{28,24},{1,5},{5... | collective-permute-start | bytes 1425416 | tf_op jit(solution)/shard_map/ppermute | solution.py:593
  192.3 1.9 shard_map.203
  194.5 1.3 collective-permute-start.25
  195.8 1.3 collective-permute-start.26
  197.1 1.4 collective-permute-start.27
  198.5 4.7 %collective-permute-done.35.refs_1_ = bf16[4,464,128]{2,1,0:T(8,128)(2,1)S(1)} collective-permute-done((bf16[4,464,128]{2,1,0:T(8,128)(2,1)S(1)}, bf16[4,464,128]{2,1,0:T(8,128)(2,1)S(1)}, u32[]{:S(2)}, u32[]{:S(2)}) %collective-permute-start.35) | collective-permute-done | bytes 475168 | tf_op jit(solution)/shard_map/ppermute | solution.py:593
  203.2 2.1 shard_map.202
  206.1 7.1 %collective-permute-done.26.refs_2_ = bf16[256,384]{1,0:T(8,128)(2,1)S(1)} collective-permute-done((bf16[256,384]{1,0:T(8,128)(2,1)S(1)}, bf16[256,384]{1,0:T(8,128)(2,1)S(1)}, u32[]{:S(2)}, u32[]{:S(2)}) %collective-permute-start.26) | collective-permute-done | bytes 196640 | tf_op jit(solution)/shard_map/ppermute | solution.py:659
  213.1 1.5 shard_map.201
  (134 shorter events, 10.3 us)
Async XLA Ops:
  2.6 12.0 %copy-start.24 = (bf16[160,960]{1,0:T(8,128)(2,1)}, bf16[160,960]{1,0:T(8,128)(2,1)S(1)}, u32[]{:S(2)}) copy-start(bf16[160,960]{1,0:T(8,128)(2,1)S(1)} %fusion.7.p0) | copy-start | bytes 921604
  2.6 20.8 %collective-permute-start.3 = (bf16[160,960]{1,0:T(8,128)(2,1)S(1)}, bf16[160,960]{1,0:T(8,128)(2,1)S(1)}, u32[]{:S(2)}, u32[]{:S(2)}) collective-permute-start(bf16[160,960]{1,0:T(8,128)(2,1)S(1)} %fusion.7.p0), channel_id=1, source_target_pairs={{0,2},{1,3},{2,0},{3,1},{4,6},{5,7},{6,4},{7,5},{8,10},{9,11},{10,... | collective-permute-start | bytes 921608 | tf_op jit(solution)/shard_map/ppermute | solution.py:593
  5.6 28.9 %collective-permute-start.2 = (bf16[160,960]{1,0:T(8,128)(2,1)S(1)}, bf16[160,960]{1,0:T(8,128)(2,1)S(1)}, u32[]{:S(2)}, u32[]{:S(2)}) collective-permute-start(bf16[160,960]{1,0:T(8,128)(2,1)S(1)} %fusion.7.p0), channel_id=1, source_target_pairs={{0,1},{1,0},{2,3},{3,2},{4,5},{5,4},{6,7},{7,6},{8,9},{9,8},{10,11... | collective-permute-start | bytes 921608 | tf_op jit(solution)/shard_map/ppermute | solution.py:593
  5.6 23.0 %collective-permute-start = (bf16[576,256]{1,0:T(8,128)(2,1)}, bf16[576,256]{1,0:T(8,128)(2,1)}, u32[]{:S(2)}, u32[]{:S(2)}) collective-permute-start(bf16[576,256]{1,0:T(8,128)(2,1)} %bitcast.73), channel_id=1, source_target_pairs={{0,16},{4,20},{8,24},{12,28},{1,17},{5,21},{9,25},{13,29},{2,18},{... | collective-permute-start | bytes 884744 | tf_op jit(solution)/shard_map/ppermute | solution.py:614
  14.6 8.7 %copy-start.22 = (bf16[144,1536]{1,0:T(8,128)(2,1)S(1)}, bf16[144,1536]{1,0:T(8,128)(2,1)}, u32[]{:S(2)}) copy-start(bf16[144,1536]{1,0:T(8,128)(2,1)} %param.18) | copy-start | bytes 1327108
  14.6 8.8 %copy-start.23 = (bf16[144,1536]{1,0:T(8,128)(2,1)S(1)}, bf16[144,1536]{1,0:T(8,128)(2,1)}, u32[]{:S(2)}) copy-start(bf16[144,1536]{1,0:T(8,128)(2,1)} %param.19) | copy-start | bytes 1327108
  17.6 5.9 %copy-start.25 = (bf16[144,576]{1,0:T(8,128)(2,1)S(1)}, bf16[144,576]{1,0:T(8,128)(2,1)}, u32[]{:S(2)}) copy-start(bf16[144,576]{1,0:T(8,128)(2,1)} %param.16) | copy-start | bytes 497668
  17.6 9.1 %collective-permute-start.5 = (bf16[576,256]{1,0:T(8,128)(2,1)S(1)}, bf16[576,256]{1,0:T(8,128)(2,1)S(1)}, u32[]{:S(2)}, u32[]{:S(2)}) collective-permute-start(bf16[576,256]{1,0:T(8,128)(2,1)S(1)} %bitcast.76), channel_id=1, source_target_pairs={{0,4},{4,0},{8,12},{12,8},{16,20},{20,16},{24,28},{28,24},{1,5},{5... | collective-permute-start | bytes 884744 | tf_op jit(solution)/shard_map/ppermute | solution.py:593
  19.2 13.9 %collective-permute-start.6 = (bf16[576,256]{1,0:T(8,128)(2,1)S(1)}, bf16[576,256]{1,0:T(8,128)(2,1)}, u32[]{:S(2)}, u32[]{:S(2)}) collective-permute-start(bf16[576,256]{1,0:T(8,128)(2,1)S(1)} %bitcast.77), channel_id=1, source_target_pairs={{0,8},{4,12},{8,16},{12,20},{16,24},{20,28},{1,9},{5,13},{9,17},{1... | collective-permute-start | bytes 884744 | tf_op jit(solution)/shard_map/ppermute | solution.py:614
  23.4 11.6 %copy-start.29 = (bf16[160,960]{1,0:T(8,128)(2,1)}, bf16[160,960]{1,0:T(8,128)(2,1)S(1)}, u32[]{:S(2)}) copy-start(bf16[160,960]{1,0:T(8,128)(2,1)S(1)} %collective-permute-done.3.p2) | copy-start | bytes 921604
  23.4 11.6 %collective-permute-start.4 = (bf16[160,960]{1,0:T(8,128)(2,1)S(1)}, bf16[160,960]{1,0:T(8,128)(2,1)S(1)}, u32[]{:S(2)}, u32[]{:S(2)}) collective-permute-start(bf16[160,960]{1,0:T(8,128)(2,1)S(1)} %collective-permute-done.3.p2), channel_id=1, source_target_pairs={{0,1},{1,0},{2,3},{3,2},{4,5},{5,4},{6,7},{7,6},{8,9},{9,8},{10,11... | collective-permute-start | bytes 921608 | tf_op jit(solution)/shard_map/ppermute | solution.py:593
  23.6 30.6 %copy-start.26 = (bf16[144,3648]{1,0:T(8,128)(2,1)}, bf16[144,3648]{1,0:T(8,128)(2,1)S(1)}, u32[]{:S(2)}) copy-start(bf16[144,3648]{1,0:T(8,128)(2,1)S(1)} %constant_dynamic-update-slice_fusion.wi0) | copy-start | bytes 3151876
  27.5 26.6 %collective-permute-start.10 = (bf16[144,3648]{1,0:T(8,128)(2,1)S(1)}, bf16[144,3648]{1,0:T(8,128)(2,1)}, u32[]{:S(2)}, u32[]{:S(2)}) collective-permute-start(bf16[144,3648]{1,0:T(8,128)(2,1)S(1)} %constant_dynamic-update-slice_fusion.wi0), channel_id=1, source_target_pairs={{0,2},{1,3},{2,0},{3,1},{4,6},{5,7},{6,4},{7,5},{8,10},{9,11},{10,... | collective-permute-start | bytes 3151880 | tf_op jit(solution)/shard_map/ppermute | solution.py:593
  28.7 15.1 %copy-start.19 = (bf16[384,576]{0,1:T(8,128)(2,1)S(1)}, bf16[384,576]{0,1:T(8,128)(2,1)}, u32[]{:S(2)}) copy-start(bf16[384,576]{0,1:T(8,128)(2,1)} %param.20) | copy-start | bytes 1327108
  28.7 13.7 %collective-permute-start.1 = (bf16[576,256]{1,0:T(8,128)(2,1)}, bf16[576,256]{1,0:T(8,128)(2,1)}, u32[]{:S(2)}, u32[]{:S(2)}) collective-permute-start(bf16[576,256]{1,0:T(8,128)(2,1)} %collective-permute-done.refs_2_), channel_id=1, source_target_pairs={{0,8},{4,12},{8,16},{12,20},{16,24},{20,28},{1,9},{5,13},{9,17},{1... | collective-permute-start | bytes 884744 | tf_op jit(solution)/shard_map/ppermute | solution.py:614
  33.0 16.6 %collective-permute-start.7 = (bf16[576,256]{1,0:T(8,128)(2,1)}, bf16[576,256]{1,0:T(8,128)(2,1)}, u32[]{:S(2)}, u32[]{:S(2)}) collective-permute-start(bf16[576,256]{1,0:T(8,128)(2,1)} %collective-permute-done.refs_2_), channel_id=1, source_target_pairs={{0,4},{4,0},{8,12},{12,8},{16,20},{20,16},{24,28},{28,24},{1,5},{5... | collective-permute-start | bytes 884744 | tf_op jit(solution)/shard_map/ppermute | solution.py:593
  34.5 15.1 %collective-permute-start.8 = (bf16[576,256]{1,0:T(8,128)(2,1)}, bf16[576,256]{1,0:T(8,128)(2,1)}, u32[]{:S(2)}, u32[]{:S(2)}) collective-permute-start(bf16[576,256]{1,0:T(8,128)(2,1)} %collective-permute-done.6.refs_0_), channel_id=1, source_target_pairs={{0,4},{4,0},{8,12},{12,8},{16,20},{20,16},{24,28},{28,24},{1,5},{5... | collective-permute-start | bytes 884744 | tf_op jit(solution)/shard_map/ppermute | solution.py:593
  42.3 11.4 %collective-permute-start.9 = (bf16[576,256]{1,0:T(8,128)(2,1)}, bf16[576,256]{1,0:T(8,128)(2,1)S(1)}, u32[]{:S(2)}, u32[]{:S(2)}) collective-permute-start(bf16[576,256]{1,0:T(8,128)(2,1)} %collective-permute-done.1.refs_3_), channel_id=1, source_target_pairs={{0,4},{4,0},{8,12},{12,8},{16,20},{20,16},{24,28},{28,24},{1,5},{5... | collective-permute-start | bytes 884744 | tf_op jit(solution)/shard_map/ppermute | solution.py:593
  44.0 19.0 %collective-permute-start.11 = (bf16[384,576]{1,0:T(8,128)(2,1)S(1)}, bf16[384,576]{1,0:T(8,128)(2,1)S(1)}, u32[]{:S(2)}, u32[]{:S(2)}) collective-permute-start(bf16[384,576]{1,0:T(8,128)(2,1)S(1)} %copy.26), channel_id=1, source_target_pairs={{0,2},{1,3},{2,0},{3,1},{4,6},{5,7},{6,4},{7,5},{8,10},{9,11},{10,... | collective-permute-start | bytes 1327112 | tf_op jit(solution)/shard_map/ppermute | solution.py:593
  54.1 11.4 %collective-permute-start.12 = (bf16[144,3648]{1,0:T(8,128)(2,1)S(1)}, bf16[144,3648]{1,0:T(8,128)(2,1)}, u32[]{:S(2)}, u32[]{:S(2)}) collective-permute-start(bf16[144,3648]{1,0:T(8,128)(2,1)S(1)} %constant_dynamic-update-slice_fusion.wi0), channel_id=1, source_target_pairs={{0,1},{1,0},{2,3},{3,2},{4,5},{5,4},{6,7},{7,6},{8,9},{9,8},{10,11... | collective-permute-start | bytes 3151880 | tf_op jit(solution)/shard_map/ppermute | solution.py:593
  54.1 11.4 %collective-permute-start.13 = (bf16[144,3648]{1,0:T(8,128)(2,1)}, bf16[144,3648]{1,0:T(8,128)(2,1)}, u32[]{:S(2)}, u32[]{:S(2)}) collective-permute-start(bf16[144,3648]{1,0:T(8,128)(2,1)} %collective-permute-done.10.wi2), channel_id=1, source_target_pairs={{0,1},{1,0},{2,3},{3,2},{4,5},{5,4},{6,7},{7,6},{8,9},{9,8},{10,11... | collective-permute-start | bytes 3151880 | tf_op jit(solution)/shard_map/ppermute | solution.py:593
  62.9 2.0 collective-permute-start.15
  63.2 2.3 %collective-permute-start.14 = (bf16[384,576]{1,0:T(8,128)(2,1)S(1)}, bf16[384,576]{1,0:T(8,128)(2,1)S(1)}, u32[]{:S(2)}, u32[]{:S(2)}) collective-permute-start(bf16[384,576]{1,0:T(8,128)(2,1)S(1)} %copy.28.wd0), channel_id=1, source_target_pairs={{0,1},{1,0},{2,3},{3,2},{4,5},{5,4},{6,7},{7,6},{8,9},{9,8},{10,11... | collective-permute-start | bytes 1327112 | tf_op jit(solution)/shard_map/ppermute | solution.py:593
  66.3 22.5 %copy-start.4 = (s32[2]{0:T(128)S(1)}, s32[2]{0:T(128)}, u32[]{:S(2)}) copy-start(s32[2]{0:T(128)} %pad_add_fusion.index) | copy-start | bytes 28
  83.0 8.9 %collective-permute-start.16 = (bf16[2,3456,128]{2,1,0:T(8,128)(2,1)}, bf16[2,3456,128]{2,1,0:T(8,128)(2,1)S(1)}, u32[]{:S(2)}, u32[]{:S(2)}) collective-permute-start(bf16[2,3456,128]{2,1,0:T(8,128)(2,1)} %get-tuple-element.105), channel_id=1, source_target_pairs={{0,1},{1,0},{2,3},{3,2},{4,5},{5,4},{6,7},{7,6},{8,9},{9,8},{10,11... | collective-permute-start | bytes 5308424 | tf_op jit(solution)/shard_map/ppermute | solution.py:593
  83.1 5.6 %collective-permute-start.17 = (bf16[2,2560,128]{2,1,0:T(8,128)(2,1)}, bf16[2,2560,128]{2,1,0:T(8,128)(2,1)S(1)}, u32[]{:S(2)}, u32[]{:S(2)}) collective-permute-start(bf16[2,2560,128]{2,1,0:T(8,128)(2,1)} %get-tuple-element.108), channel_id=1, source_target_pairs={{0,1},{1,0},{2,3},{3,2},{4,5},{5,4},{6,7},{7,6},{8,9},{9,8},{10,11... | collective-permute-start | bytes 3932168 | tf_op jit(solution)/shard_map/ppermute | solution.py:593
  90.9 5.2 %copy-start.10 = (bf16[576,576]{1,0:T(8,128)(2,1)S(1)}, bf16[576,576]{1,0:T(8,128)(2,1)}, u32[]{:S(2)}) copy-start(bf16[576,576]{1,0:T(8,128)(2,1)} %get-tuple-element.113.query_weight) | copy-start | bytes 1990660
  90.9 5.2 %copy-start.11 = (bf16[256,576]{1,0:T(8,128)(2,1)S(1)}, bf16[256,576]{1,0:T(8,128)(2,1)}, u32[]{:S(2)}) copy-start(bf16[256,576]{1,0:T(8,128)(2,1)} %get-tuple-element.84.queries) | copy-start | bytes 884740
  91.0 5.2 %copy-start.12 = (bf16[2048,576]{1,0:T(8,128)(2,1)S(1)}, bf16[2048,576]{1,0:T(8,128)(2,1)}, u32[]{:S(2)}) copy-start(bf16[2048,576]{1,0:T(8,128)(2,1)} %get-tuple-element.112.normed) | copy-start | bytes 7077892
  91.0 5.2 %copy-start.13 = (bf16[2048,384]{1,0:T(8,128)(2,1)S(1)}, bf16[2048,384]{1,0:T(8,128)(2,1)}, u32[]{:S(2)}) copy-start(bf16[2048,384]{1,0:T(8,128)(2,1)} %get-tuple-element.102.kv_all) | copy-start | bytes 4718596
  91.0 5.2 %copy-start.14 = (f32[256,576]{1,0:T(8,128)S(1)}, f32[256,576]{1,0:T(8,128)}, u32[]{:S(2)}) copy-start(f32[256,576]{1,0:T(8,128)} %get-tuple-element.96.attended) | copy-start | bytes 1769476
  91.0 5.2 %copy-start.16 = (bf16[256,576]{1,0:T(8,128)(2,1)S(1)}, bf16[256,576]{1,0:T(8,128)(2,1)}, u32[]{:S(2)}) copy-start(bf16[256,576]{1,0:T(8,128)(2,1)} %get-tuple-element.110.attended_grad) | copy-start | bytes 884740
  91.8 4.3 %copy-start = (f32[2048,128]{1,0:T(8,128)S(1)}, f32[2048,128]{1,0:T(8,128)}, u32[]{:S(2)}) copy-start(f32[2048,128]{1,0:T(8,128)} %get-tuple-element.80.cosine) | copy-start | bytes 3145732
  91.9 4.3 %copy-start.1 = (f32[2048,128]{1,0:T(8,128)S(1)}, f32[2048,128]{1,0:T(8,128)}, u32[]{:S(2)}) copy-start(f32[2048,128]{1,0:T(8,128)} %get-tuple-element.81.sine) | copy-start | bytes 3145732
  91.9 4.3 %copy-start.9 = (bf16[576,384]{1,0:T(8,128)(2,1)S(1)}, bf16[576,384]{1,0:T(8,128)(2,1)}, u32[]{:S(2)}) copy-start(bf16[576,384]{1,0:T(8,128)(2,1)} %get-tuple-element.87.kv_weight) | copy-start | bytes 1327108
  91.9 4.3 %copy-start.15 = (f32[8,576]{1,0:T(8,128)S(1)}, f32[8,576]{1,0:T(8,128)}, u32[]{:S(2)}) copy-start(f32[8,576]{1,0:T(8,128)} %get-tuple-element.88.gains) | copy-start | bytes 55300
  92.3 21.8 %collective-permute-start.18 = (bf16[3456,128]{1,0:T(8,128)(2,1)S(1)}, bf16[3456,128]{1,0:T(8,128)(2,1)S(1)}, u32[]{:S(2)}, u32[]{:S(2)}) collective-permute-start(bf16[3456,128]{1,0:T(8,128)(2,1)S(1)} %fusion), channel_id=1, source_target_pairs={{0,2},{1,3},{2,0},{3,1},{4,6},{5,7},{6,4},{7,5},{8,10},{9,11},{10,... | collective-permute-start | bytes 2654216 | tf_op jit(solution)/shard_map/ppermute | solution.py:593
  93.0 17.9 %collective-permute-start.19 = (bf16[2,4,320,128]{3,2,1,0:T(8,128)(2,1)S(1)}, bf16[2,4,320,128]{3,2,1,0:T(8,128)(2,1)S(1)}, u32[]{:S(2)}, u32[]{:S(2)}) collective-permute-start(bf16[2,4,320,128]{3,2,1,0:T(8,128)(2,1)S(1)} %get-tuple-element.122), channel_id=1, source_target_pairs={{0,4},{4,0},{8,12},{12,8},{16,20},{20,16},{24,28},{28,24},{1,5},{5... | collective-permute-start | bytes 1966088 | tf_op jit(solution)/shard_map/ppermute | solution.py:593
  101.9 13.0 %copy-start.5 = (bf16[3456,128]{1,0:T(8,128)(2,1)S(1)}, bf16[3456,128]{1,0:T(8,128)(2,1)}, u32[]{:S(2)}) copy-start(bf16[3456,128]{1,0:T(8,128)(2,1)} %get-tuple-element.126.refs_0_) | copy-start | bytes 2654212
  114.1 5.0 %collective-permute-start.20 = (bf16[2,1152,128]{2,1,0:T(8,128)(2,1)S(1)}, bf16[2,1152,128]{2,1,0:T(8,128)(2,1)S(1)}, u32[]{:S(2)}, u32[]{:S(2)}) collective-permute-start(bf16[2,1152,128]{2,1,0:T(8,128)(2,1)S(1)} %get-tuple-element.125), channel_id=1, source_target_pairs={{0,1},{1,0},{2,3},{3,2},{4,5},{5,4},{6,7},{7,6},{8,9},{9,8},{10,11... | collective-permute-start | bytes 1769480 | tf_op jit(solution)/shard_map/ppermute | solution.py:593
  114.3 10.6 %collective-permute-start.22 = (bf16[4,320,128]{2,1,0:T(8,128)(2,1)S(1)}, bf16[4,320,128]{2,1,0:T(8,128)(2,1)S(1)}, u32[]{:S(2)}, u32[]{:S(2)}) collective-permute-start(bf16[4,320,128]{2,1,0:T(8,128)(2,1)S(1)} %fusion.3), channel_id=1, source_target_pairs={{0,2},{1,3},{2,0},{3,1},{4,6},{5,7},{6,4},{7,5},{8,10},{9,11},{10,... | collective-permute-start | bytes 983048 | tf_op jit(solution)/shard_map/ppermute | solution.py:593
  115.8 13.8 %collective-permute-start.21 = (bf16[4,432,128]{2,1,0:T(8,128)(2,1)S(1)}, bf16[4,432,128]{2,1,0:T(8,128)(2,1)S(1)}, u32[]{:S(2)}, u32[]{:S(2)}) collective-permute-start(bf16[4,432,128]{2,1,0:T(8,128)(2,1)S(1)} %get-tuple-element.128), channel_id=1, source_target_pairs={{0,4},{4,0},{8,12},{12,8},{16,20},{20,16},{24,28},{28,24},{1,5},{5... | collective-permute-start | bytes 1327112 | tf_op jit(solution)/shard_map/ppermute | solution.py:593
  119.2 11.6 %collective-permute-start.23 = (bf16[1152,128]{1,0:T(8,128)(2,1)S(1)}, bf16[1152,128]{1,0:T(8,128)(2,1)S(1)}, u32[]{:S(2)}, u32[]{:S(2)}) collective-permute-start(bf16[1152,128]{1,0:T(8,128)(2,1)S(1)} %fusion.5), channel_id=1, source_target_pairs={{0,2},{1,3},{2,0},{3,1},{4,6},{5,7},{6,4},{7,5},{8,10},{9,11},{10,... | collective-permute-start | bytes 884744 | tf_op jit(solution)/shard_map/ppermute | solution.py:593
  130.9 20.9 %collective-permute-start.36 = (bf16[432,128]{1,0:T(8,128)(2,1)S(1)}, bf16[432,128]{1,0:T(8,128)(2,1)S(1)}, u32[]{:S(2)}, u32[]{:S(2)}) collective-permute-start(bf16[432,128]{1,0:T(8,128)(2,1)S(1)} %get-tuple-element.155), channel_id=1, source_target_pairs={{0,8},{4,12},{8,16},{12,20},{16,24},{20,28},{24,0},{28,4},{1,9},{5... | collective-permute-start | bytes 331784 | tf_op jit(solution)/shard_map/ppermute | solution.py:659
  136.7 17.6 %collective-permute-start.37 = (bf16[432,128]{1,0:T(8,128)(2,1)S(1)}, bf16[432,128]{1,0:T(8,128)(2,1)S(1)}, u32[]{:S(2)}, u32[]{:S(2)}) collective-permute-start(bf16[432,128]{1,0:T(8,128)(2,1)S(1)} %get-tuple-element.157), channel_id=1, source_target_pairs={{0,16},{4,20},{8,24},{12,28},{16,0},{20,4},{24,8},{28,12},{1,17},{... | collective-permute-start | bytes 331784 | tf_op jit(solution)/shard_map/ppermute | solution.py:659
  147.0 7.2 %collective-permute-start.38 = (bf16[432,128]{1,0:T(8,128)(2,1)S(1)}, bf16[432,128]{1,0:T(8,128)(2,1)S(1)}, u32[]{:S(2)}, u32[]{:S(2)}) collective-permute-start(bf16[432,128]{1,0:T(8,128)(2,1)S(1)} %get-tuple-element.156), channel_id=1, source_target_pairs={{0,24},{4,28},{8,0},{12,4},{16,8},{20,12},{24,16},{28,20},{1,25},{... | collective-permute-start | bytes 331784 | tf_op jit(solution)/shard_map/ppermute | solution.py:659
  147.7 12.0 %collective-permute-start.28 = (bf16[4,144,128]{2,1,0:T(8,128)(2,1)S(1)}, bf16[4,144,128]{2,1,0:T(8,128)(2,1)S(1)}, u32[]{:S(2)}, u32[]{:S(2)}) collective-permute-start(bf16[4,144,128]{2,1,0:T(8,128)(2,1)S(1)} %get-tuple-element.138), channel_id=1, source_target_pairs={{0,4},{4,0},{8,12},{12,8},{16,20},{20,16},{24,28},{28,24},{1,5},{5... | collective-permute-start | bytes 442376 | tf_op jit(solution)/shard_map/ppermute | solution.py:593
  151.7 42.5 %collective-permute-start.24 = (bf16[4,256,384]{2,1,0:T(8,128)(2,1)S(1)}, bf16[4,256,384]{2,1,0:T(8,128)(2,1)S(1)}, u32[]{:S(2)}, u32[]{:S(2)}) collective-permute-start(bf16[4,256,384]{2,1,0:T(8,128)(2,1)S(1)} %slice.69), channel_id=1, source_target_pairs={{0,4},{4,0},{8,12},{12,8},{16,20},{20,16},{24,28},{28,24},{1,5},{5... | collective-permute-start | bytes 2359304 | tf_op jit(solution)/shard_map/ppermute | solution.py:593
  154.3 7.7 %collective-permute-start.39 = (bf16[432,128]{1,0:T(8,128)(2,1)S(1)}, bf16[432,128]{1,0:T(8,128)(2,1)S(1)}, u32[]{:S(2)}, u32[]{:S(2)}) collective-permute-start(bf16[432,128]{1,0:T(8,128)(2,1)S(1)} %fusion.13), channel_id=1, source_target_pairs={{0,8},{4,12},{8,16},{12,20},{16,24},{20,28},{24,0},{28,4},{1,9},{5... | collective-permute-start | bytes 331784 | tf_op jit(solution)/shard_map/ppermute | solution.py:614
  157.2 9.6 %collective-permute-start.40 = (bf16[432,128]{1,0:T(8,128)(2,1)S(1)}, bf16[432,128]{1,0:T(8,128)(2,1)S(1)}, u32[]{:S(2)}, u32[]{:S(2)}) collective-permute-start(bf16[432,128]{1,0:T(8,128)(2,1)S(1)} %fusion.13), channel_id=1, source_target_pairs={{0,16},{4,20},{8,24},{12,28},{16,0},{20,4},{24,8},{28,12},{1,17},{... | collective-permute-start | bytes 331784 | tf_op jit(solution)/shard_map/ppermute | solution.py:614
  157.6 13.1 %collective-permute-start.41 = (bf16[432,128]{1,0:T(8,128)(2,1)S(1)}, bf16[432,128]{1,0:T(8,128)(2,1)S(1)}, u32[]{:S(2)}, u32[]{:S(2)}) collective-permute-start(bf16[432,128]{1,0:T(8,128)(2,1)S(1)} %fusion.13), channel_id=1, source_target_pairs={{0,24},{4,28},{8,0},{12,4},{16,8},{20,12},{24,16},{28,20},{1,25},{... | collective-permute-start | bytes 331784 | tf_op jit(solution)/shard_map/ppermute | solution.py:614
  159.8 14.8 %collective-permute-start.29 = (bf16[464,128]{1,0:T(8,128)(2,1)S(1)}, bf16[464,128]{1,0:T(8,128)(2,1)S(1)}, u32[]{:S(2)}, u32[]{:S(2)}) collective-permute-start(bf16[464,128]{1,0:T(8,128)(2,1)S(1)} %get-tuple-element.152), channel_id=1, source_target_pairs={{0,8},{4,12},{8,16},{12,20},{16,24},{20,28},{24,0},{28,4},{1,9},{5... | collective-permute-start | bytes 356360 | tf_op jit(solution)/shard_map/ppermute | solution.py:659
  162.1 13.8 %collective-permute-start.30 = (bf16[464,128]{1,0:T(8,128)(2,1)S(1)}, bf16[464,128]{1,0:T(8,128)(2,1)S(1)}, u32[]{:S(2)}, u32[]{:S(2)}) collective-permute-start(bf16[464,128]{1,0:T(8,128)(2,1)S(1)} %get-tuple-element.154), channel_id=1, source_target_pairs={{0,16},{4,20},{8,24},{12,28},{16,0},{20,4},{24,8},{28,12},{1,17},{... | collective-permute-start | bytes 356360 | tf_op jit(solution)/shard_map/ppermute | solution.py:659
  166.8 9.1 %collective-permute-start.31 = (bf16[464,128]{1,0:T(8,128)(2,1)S(1)}, bf16[464,128]{1,0:T(8,128)(2,1)S(1)}, u32[]{:S(2)}, u32[]{:S(2)}) collective-permute-start(bf16[464,128]{1,0:T(8,128)(2,1)S(1)} %get-tuple-element.153), channel_id=1, source_target_pairs={{0,24},{4,28},{8,0},{12,4},{16,8},{20,12},{24,16},{28,20},{1,25},{... | collective-permute-start | bytes 356360 | tf_op jit(solution)/shard_map/ppermute | solution.py:659
  170.8 21.5 %collective-permute-start.42 = (bf16[4,432,128]{2,1,0:T(8,128)(2,1)S(1)}, bf16[4,432,128]{2,1,0:T(8,128)(2,1)S(1)}, u32[]{:S(2)}, u32[]{:S(2)}) collective-permute-start(bf16[4,432,128]{2,1,0:T(8,128)(2,1)S(1)} %pad_maximum_fusion.3.refs_0_), channel_id=1, source_target_pairs={{0,4},{4,0},{8,12},{12,8},{16,20},{20,16},{24,28},{28,24},{1,5},{5... | collective-permute-start | bytes 1327112 | tf_op jit(solution)/shard_map/ppermute | solution.py:593
  176.0 8.3 %collective-permute-start.32 = (bf16[464,128]{1,0:T(8,128)(2,1)S(1)}, bf16[464,128]{1,0:T(8,128)(2,1)S(1)}, u32[]{:S(2)}, u32[]{:S(2)}) collective-permute-start(bf16[464,128]{1,0:T(8,128)(2,1)S(1)} %fusion.10), channel_id=1, source_target_pairs={{0,8},{4,12},{8,16},{12,20},{16,24},{20,28},{24,0},{28,4},{1,9},{5... | collective-permute-start | bytes 356360 | tf_op jit(solution)/shard_map/ppermute | solution.py:614
  179.1 9.3 %collective-permute-start.33 = (bf16[464,128]{1,0:T(8,128)(2,1)S(1)}, bf16[464,128]{1,0:T(8,128)(2,1)S(1)}, u32[]{:S(2)}, u32[]{:S(2)}) collective-permute-start(bf16[464,128]{1,0:T(8,128)(2,1)S(1)} %fusion.10), channel_id=1, source_target_pairs={{0,16},{4,20},{8,24},{12,28},{16,0},{20,4},{24,8},{28,12},{1,17},{... | collective-permute-start | bytes 356360 | tf_op jit(solution)/shard_map/ppermute | solution.py:614
  180.8 7.6 %collective-permute-start.34 = (bf16[464,128]{1,0:T(8,128)(2,1)S(1)}, bf16[464,128]{1,0:T(8,128)(2,1)S(1)}, u32[]{:S(2)}, u32[]{:S(2)}) collective-permute-start(bf16[464,128]{1,0:T(8,128)(2,1)S(1)} %fusion.10), channel_id=1, source_target_pairs={{0,24},{4,28},{8,0},{12,4},{16,8},{20,12},{24,16},{28,20},{1,25},{... | collective-permute-start | bytes 356360 | tf_op jit(solution)/shard_map/ppermute | solution.py:614
  188.4 14.8 %collective-permute-start.35 = (bf16[4,464,128]{2,1,0:T(8,128)(2,1)S(1)}, bf16[4,464,128]{2,1,0:T(8,128)(2,1)S(1)}, u32[]{:S(2)}, u32[]{:S(2)}) collective-permute-start(bf16[4,464,128]{2,1,0:T(8,128)(2,1)S(1)} %pad_maximum_fusion.2.refs_0_), channel_id=1, source_target_pairs={{0,4},{4,0},{8,12},{12,8},{16,20},{20,16},{24,28},{28,24},{1,5},{5... | collective-permute-start | bytes 1425416 | tf_op jit(solution)/shard_map/ppermute | solution.py:593
  194.5 11.6 %collective-permute-start.25 = (bf16[256,384]{1,0:T(8,128)(2,1)S(1)}, bf16[256,384]{1,0:T(8,128)(2,1)S(1)}, u32[]{:S(2)}, u32[]{:S(2)}) collective-permute-start(bf16[256,384]{1,0:T(8,128)(2,1)S(1)} %get-tuple-element.151), channel_id=1, source_target_pairs={{24,0},{28,4},{25,1},{29,5},{26,2},{30,6},{27,3},{31,7}} | collective-permute-start | bytes 589832 | tf_op jit(solution)/shard_map/ppermute | solution.py:659
  195.8 17.4 %collective-permute-start.26 = (bf16[256,384]{1,0:T(8,128)(2,1)S(1)}, bf16[256,384]{1,0:T(8,128)(2,1)S(1)}, u32[]{:S(2)}, u32[]{:S(2)}) collective-permute-start(bf16[256,384]{1,0:T(8,128)(2,1)S(1)} %get-tuple-element.150), channel_id=1, source_target_pairs={{16,0},{20,4},{24,8},{28,12},{17,1},{21,5},{25,9},{29,13},{18,2},{... | collective-permute-start | bytes 589832 | tf_op jit(solution)/shard_map/ppermute | solution.py:659
  197.1 16.1 %copy-start.3 = (bf16[1,256,576]{1,2,0:T(8,128)(2,1)S(1)}, bf16[1,256,576]{1,2,0:T(8,128)(2,1)}, u32[]{:S(2)}) copy-start(bf16[1,256,576]{1,2,0:T(8,128)(2,1)} %param.11) | copy-start | bytes 884740
  197.1 16.1 %copy-start.8 = (f32[256,576]{1,0:T(8,128)S(1)}, f32[256,576]{1,0:T(8,128)}, u32[]{:S(2)}) copy-start(f32[256,576]{1,0:T(8,128)} %get-tuple-element.116.middle_grad) | copy-start | bytes 1769476
  197.1 16.0 %collective-permute-start.27 = (bf16[256,384]{1,0:T(8,128)(2,1)S(1)}, bf16[256,384]{1,0:T(8,128)(2,1)S(1)}, u32[]{:S(2)}, u32[]{:S(2)}) collective-permute-start(bf16[256,384]{1,0:T(8,128)(2,1)S(1)} %get-tuple-element.149), channel_id=1, source_target_pairs={{8,0},{12,4},{16,8},{20,12},{24,16},{28,20},{9,1},{13,5},{17,9},{2... | collective-permute-start | bytes 589832 | tf_op jit(solution)/shard_map/ppermute | solution.py:659
  (13 other events, 23.8 us)
where the time goes:
time: 217 us; the launch traced here: 215 us
  starting transfers between devices  81.2 us (37%)
  waiting for transfers between devices  70.6 us (33%)
  Pallas kernels  43.8 us (20%)
  other arithmetic  11.2 us (5%)
  local copies, waits for them, and re-layouts  6.47 us (3%)
    ppermute x25, waiting for transfers between devices, swap(): return lax.ppermute(value, axis, [(i, i ^ 1 << bit) for i in range(count)])  46.9 us
    pallas_call x10, Pallas kernels, call(): pl.pallas_call(kernel, out_shape=outs, in_specs=[SMEM_SPEC] * smem + [VME...  43.8 us
    ppermute x25, starting transfers between devices, swap(): return lax.ppermute(value, axis, [(i, i ^ 1 << bit) for i in range(count)])  31.7 us
    ppermute x9, starting transfers between devices, scattered_parts(): lax.ppermute(column[by], 'ctx', [(i, j % count) for i, j in pairs])  24.9 us
    ppermute x9, starting transfers between devices, shifted(): return lax.ppermute(value, 'ctx', [(i, j % count) for i, j in pairs])  24.6 us
    ppermute x9, waiting for transfers between devices, shifted(): return lax.ppermute(value, 'ctx', [(i, j % count) for i, j in pairs])  12.7 us
    ppermute x9, waiting for transfers between devices, scattered_parts(): lax.ppermute(column[by], 'ctx', [(i, j % count) for i, j in pairs])  11 us
    unnamed x71, local copies, waits for them, and re-layouts  5.29 us
  transfers between devices with their start and end apart: 43, of which 22 were waited for; matrix products, arithmetic and copies ran while one was open for 5% of the time, Pallas kernels for 12%

commit v1 on v0

--- a/solution.py
+++ b/solution.py
@@ -111,14 +111,14 @@
     return table[block_at(jnp.clip(owner, 0, table.shape[0] // rows - 1), rows), :]
 
 
-def early_kernel(index, p0, p1, p2, p3, cosine, sine, *refs, places, slice_rows):
+def early_kernel(index, here_pair, core_pair, cosine, sine, *refs, places, slice_rows):
     pieces = refs[: len(places)]
     (
         normed_out, kv_out, query_out, query_weight, kv_weight, gains_out, gain_scr, raw_scr,
     ) = refs[len(places) :]
     here = index[0]
-    more = p0.shape[0] - slice_rows
-    packs = (p0, p1, p2, p3)
+    packs = (here_pair.at[0], core_pair.at[0], here_pair.at[1], core_pair.at[1])
+    more = packs[0].shape[0] - slice_rows
     for relative, pack in enumerate(packs):
         owner = index[1] ^ relative
         at = pl.ds(pl.multiple_of(owner * slice_rows, 16), slice_rows)
@@ -427,9 +427,8 @@
         value_grad = jnp.concatenate(value_grads, -1)
         both = jnp.concatenate([key_grad, value_grad], -1).astype(BF16)
         if whole:
-            across = (j ^ here) & 1
-            distance = (j // 2 - here // 2) & (blocks // 2 - 1)
-            kv_grads[across * (blocks // 2) + distance] = both
+            apart = j ^ here
+            kv_grads[(apart & 1) * (blocks // 2) + apart // 2] = both
             turned = rotated(key_grad, cosine[keys_at, :], sine[keys_at, :], -1.0)
             linear = jnp.concatenate([turned, value_grad], -1).astype(BF16)
             weight_scr[...] += mm(normed[keys_at, :], linear, 0, 0)
@@ -483,7 +482,7 @@
 ):
     kv_parts, tokens_grad = refs[:-1], refs[-1]
     rows = normed_grad.shape[0]
-    if len(kv_parts) == 1:
+    if kv_parts[0].shape[0] > rows:
 
         def add(j, total):
             return total + kv_parts[0][block_at(j, rows), :].astype(F32)
@@ -491,10 +490,7 @@
         parts = kv_parts[0].shape[0] // rows
         kv_grad = lax.fori_loop(0, parts, add, jnp.zeros((rows, 2 * KVW), F32))
     else:
-        column, *moved = kv_parts
-        kv_grad = column[0].astype(F32)
-        for part in moved:
-            kv_grad = kv_grad + part[...].astype(F32)
+        kv_grad = kv_parts[0][...].astype(F32)
     key_back = rotated(kv_grad[:, :KVW], cosine[...], sine[...], -1.0)
     back = jnp.concatenate([key_back, kv_grad[:, KVW:]], -1).astype(BF16)
     total = normed_grad[...] + mm(back, kv_weight[...], 1, 1)
@@ -507,14 +503,12 @@
     *terms, keep, send = refs
     here = index[0]
     rows = keep.shape[1]
-    for distance in range(count // 2):
-        for across, out in enumerate((keep, send)):
-            owner = ((here ^ across) + 2 * distance) & (count - 1)
-            at = pl.ds(pl.multiple_of(owner * rows, 16), rows)
-            total = terms[0][at, :].astype(F32)
-            for term in terms[1:]:
-                total = total + term[at, :].astype(F32)
-            out[distance] = total.astype(BF16)
+    for apart in range(count):
+        at = pl.ds(pl.multiple_of((here ^ apart) * rows, 16), rows)
+        total = terms[0][at, :].astype(F32)
+        for term in terms[1:]:
+            total = total + term[at, :].astype(F32)
+        (send if apart & 1 else keep)[apart // 2] = total.astype(BF16)
 
 
 def spread_both_kernel(index, mine, along, got, keep_mine, keep_along, send, count):
@@ -530,11 +524,10 @@
         count = piece.shape[0] // total
         owners = [(owner, piece, owner * total) for owner in range(count)]
     else:
-        count = 2 * pieces[0].shape[0]
         owners = [
-            (((here ^ across) + (count - 2 * distance)) & (count - 1), column.at[distance], 0)
+            (here ^ (2 * slot + across), column.at[slot], 0)
             for across, column in enumerate(pieces)
-            for distance in range(count // 2)
+            for slot in range(column.shape[0])
         ]
     for owner, piece, start in owners:
         for flat, rows in parts:
@@ -594,16 +587,14 @@
 
 
 def gathered_ws(value):
-    along = swap(value, "ws", 1)
-    return value, swap(value, "ws", 0), along, swap(along, "ws", 0)
-
-
-def gathered_ctx(value):
-    count = lax.axis_size("ctx")
-    if count != 8:
-        return (lax.all_gather(value, "ctx", axis=0, tiled=True),)
-    column = jnp.stack([value] + [shifted(value, by, False) for by in (1, 2, 3)])
-    return column, swap(column, "ctx", 0)
+    pair = jnp.stack([value, swap(value, "ws", 1)])
+    return pair, swap(pair, "ws", 0)
+
+
+def column_of(value):
+    far = swap(value, "ctx", 2)
+    near = swap(jnp.stack([value, far]), "ctx", 1)
+    return jnp.stack([value, near[0], far, near[1]])
 
 
 def shifted(value, by, upward_only):
@@ -649,15 +640,13 @@
     return jnp.stack(pair, 2).reshape(values.shape)
 
 
-def scattered_parts(column, downward_only):
-    count = lax.axis_size("ctx")
-    parts = []
-    for by in (1, 2, 3):
-        pairs = [(i, i + 2 * by) for i in range(count)]
-        if downward_only:
-            pairs = [(i, j) for i, j in pairs if j >= count]
-        parts.append(lax.ppermute(column[by], "ctx", [(i, j % count) for i, j in pairs]))
-    return parts
+def summed_column(terms):
+    def slot(at):
+        return added(*[term[at] for term in terms])
+
+    got = swap(jnp.stack([slot(1), slot(3)]), "ctx", 1)
+    far = swap(added(*[term[2] for term in terms], got[1]), "ctx", 2)
+    return added(*[term[0] for term in terms], got[0], far)
 
 
 def spread(index, terms):
@@ -740,7 +729,8 @@
         later_tokens, tables = lax.optimization_barrier((tokens, tables))
         behind_one = shifted(later_tokens, 1, True)
         mate = swap(later_tokens, "ctx", 0)
-        behind_three = shifted(behind_two, 1, True)
+        last = [(i - 2, i) for i in range(ctx_count - 2, ctx_count)]
+        behind_three = lax.ppermute(behind_two, "ctx", last)
     else:
         tables = (cosine, sine)
 
@@ -859,8 +849,8 @@
     )
 
     in_mine, in_along, in_send, mine, along, send = tiles
+    got = swap(send, "ws", 0)
     in_got = swap(in_send, "ws", 0)
-    got = swap(send, "ws", 0)
     in_crossing = added(in_along, in_got[1])
     if by_hops:
         keep_mine, keep_along, to_mate = spread_both(index, mine, along, got)
@@ -919,38 +909,53 @@
     )
     small_mine, small_along, small_send = small
     small_got = swap(small_send, "ws", 0)
-    small_crossed = swap(added(small_along, small_got[1]), "ws", 1)
 
     if by_hops:
         in_keep, in_to_mate = spread(index, (in_mine, in_got[0], in_crossed))
         in_from_mate = swap(in_to_mate, "ctx", 0)
-        crossed = swap(added(keep_along, from_mate[1]), "ws", 1)
-        in_from_mate, crossed, small_crossed = lax.optimization_barrier(
-            (in_from_mate, crossed, small_crossed)
+        more_rows = keep_along.shape[0] * second_rows
+        crossing = jnp.concatenate(
+            [
+                added(keep_along, from_mate[1]).reshape(more_rows, LANES),
+                added(small_along, small_got[1]),
+            ],
+            0,
         )
-        small_keep, small_to_mate = spread(index, (small_mine, small_got[0], small_crossed))
+        crossed = swap(crossing, "ws", 1)
+        in_from_mate, crossed = lax.optimization_barrier((in_from_mate, crossed))
+        small_keep, small_to_mate = spread(
+            index, (small_mine, small_got[0], crossed[more_rows:])
+        )
+        crossed = crossed[:more_rows].reshape(keep_mine.shape)
         small_to_mate, kv_to_mate = lax.optimization_barrier(
             (small_to_mate, kv_grads[ctx_count // 2 :])
         )
         small_from_mate = swap(small_to_mate, "ctx", 0)
         kv_from_mate = swap(kv_to_mate, "ctx", 0)
-        in_column = added(in_keep, in_from_mate)
-        in_share = added(in_column[0], *scattered_parts(in_column, False))
-        column = jnp.concatenate(
-            [added(keep_mine, from_mate[0], crossed), added(small_keep, small_from_mate)], 1
+        in_share = summed_column((in_keep, in_from_mate))
+        share = summed_column(
+            (
+                jnp.concatenate([added(keep_mine, from_mate[0], crossed), small_keep], 1),
+                jnp.concatenate([jnp.zeros_like(keep_mine), small_from_mate], 1),
+            )
         )
-        share = added(column[0], *scattered_parts(column, False))
-        kv_column = added(kv_grads[: ctx_count // 2], kv_from_mate)
-        kv_parts = (kv_column, *scattered_parts(kv_column, True))
+        share, kv_from_mate = lax.optimization_barrier((share, kv_from_mate))
+        in_column = column_of(in_share)
+        in_pieces = (in_column, swap(in_column, "ctx", 0))
+        column = column_of(share)
+        pieces = (column, swap(column, "ctx", 0))
+        kv_parts = (summed_column((kv_grads[: ctx_count // 2], kv_from_mate)),)
     else:
         kv_parts = (lax.all_to_all(kv_grads, "ctx", split_axis=0, concat_axis=0, tiled=True),)
         in_total = added(in_mine, in_got[0], in_crossed)
         total = added(mine, got[0], from_mate)
+        small_crossed = swap(added(small_along, small_got[1]), "ws", 1)
         small_total = added(small_mine, small_got[0], small_crossed)
         in_share = scattered_ctx((in_total,), (first_rows,))
         share = scattered_ctx((total, small_total), (second_rows, small_rows))
-    in_pieces = gathered_ctx(in_share)
-    pieces = gathered_ctx(share)
+        in_pieces, pieces = (
+            (lax.all_gather(value, "ctx", axis=0, tiled=True),) for value in (in_share, share)
+        )
 
     tokens_grad = call(
         tail_kernel,

time: 217 us -> 198 us (0.912); the launches traced: 215 us -> 198 us
  starting transfers between devices: 81.2 us -> 47.4 us
  waiting for transfers between devices: 70.6 us -> 87.1 us
    ppermute x25 -> x33, waiting for transfers between devices: 46.9 us -> 86.5 us  [swap(): return lax.ppermute(value, axis, [(i, i ^ 1 << bit) for i in range(count)])]
    ppermute x9 -> x1, starting transfers between devices: 24.9 us -> 1.5 us  [body(): behind_three = lax.ppermute(behind_two, 'ctx', last)]
    ppermute x9 -> x2, starting transfers between devices: 24.6 us -> 9.45 us  [shifted(): return lax.ppermute(value, 'ctx', [(i, j % count) for i, j in pairs])]
    ppermute x9 -> x2, waiting for transfers between devices: 12.7 us -> 0.59 us  [shifted(): return lax.ppermute(value, 'ctx', [(i, j % count) for i, j in pairs])]
    ppermute x9 -> x1, waiting for transfers between devices: 11 us -> 0.01 us  [body(): behind_three = lax.ppermute(behind_two, 'ctx', last)]
    ppermute x25 -> x33, starting transfers between devices: 31.7 us -> 36.5 us  [swap(): return lax.ppermute(value, axis, [(i, i ^ 1 << bit) for i in range(count)])]
  transfers between devices with their start and end apart: 43 -> 36, of which waited for: 22 -> 23; matrix products, arithmetic and copies ran while one was open for 5% -> 6% of each run, Pallas kernels for 12% -> 13%
where the time goes in v1:
time: 198 us
  waiting for transfers between devices  87.1 us (44%)
  starting transfers between devices  47.4 us (24%)
  Pallas kernels  44 us (22%)
  other arithmetic  11.6 us (6%)
  local copies, waits for them, and re-layouts  6.42 us (3%)
    ppermute x33, waiting for transfers between devices, swap(): return lax.ppermute(value, axis, [(i, i ^ 1 << bit) for i in range(count)])  86.5 us
    pallas_call x10, Pallas kernels, call(): pl.pallas_call(kernel, out_shape=outs, in_specs=[SMEM_SPEC] * smem + [VME...  44 us
    ppermute x33, starting transfers between devices, swap(): return lax.ppermute(value, axis, [(i, i ^ 1 << bit) for i in range(count)])  36.5 us
    ppermute x2, starting transfers between devices, shifted(): return lax.ppermute(value, 'ctx', [(i, j % count) for i, j in pairs])  9.45 us
    unnamed x71, local copies, waits for them, and re-layouts  5.25 us
    neg x2, other arithmetic, wide_tables(): -sine  4.26 us
  transfers between devices with their start and end apart: 36, of which 23 were waited for; matrix products, arithmetic and copies ran while one was open for 6% of the time, Pallas kernels for 13%

profile of v1, /device:TPU:0, one launch (start us, length us, event | category | flops | bytes accessed | tf_op | source)
XLA Modules:
  0.0 197.9 jit_solution(2080844327688210204)
XLA Ops:
  0.6 6.0 %collective-permute-start = (bf16[576,256]{1,0:T(8,128)(2,1)}, bf16[576,256]{1,0:T(8,128)(2,1)S(1)}, u32[]{:S(2)}, u32[]{:S(2)}) collective-permute-start(bf16[576,256]{1,0:T(8,128)(2,1)} %bitcast.65), channel_id=1, source_target_pairs={{0,16},{4,20},{8,24},{12,28},{1,17},{5,21},{9,25},{13,29},{2,18},{... | collective-permute-start | bytes 884744 | tf_op jit(solution)/shard_map/ppermute | solution.py:605
  6.6 0.7 pad_maximum_fusion.14
  7.4 1.1 fusion.7
  8.6 1.6 collective-permute-start.2
  10.1 3.7 %fusion.6 = (f32[2048,32]{1,0:T(8,128)S(1)}, f32[2048,32]{1,0:T(8,128)S(1)}, f32[2048,32]{1,0:T(8,128)S(1)}) fusion(f32[32]{0:T(128)S(1)} %multiply_exponential_fusion, f32[2048]{0:T(1024)S(1)} %iota_convert_fusion), kind=kLoop, calls=%fused_computation.37 | loop fusion | flops 131072 | bytes 794752 | tf_op jit(solution)/shard_map/neg | solution.py:723
  13.9 3.0 %pad_maximum_fusion = (f32[2048,128]{1,0:T(8,128)}, f32[2048,128]{1,0:T(8,128)}) fusion(f32[2048,32]{1,0:T(8,128)S(1)} %get-tuple-element.163, f32[2048,32]{1,0:T(8,128)S(1)} %get-tuple-element.162, f32[2048,32]{1,0:T(8,128)S(1)} %get-tuple-element.161), kind=kLoop, calls=%fused_computation.4 | loop fusion | flops 1572864 | bytes 2883584 | tf_op jit(solution)/shard_map/concatenate | solution.py:723
  16.9 1.5 collective-permute-start.4
  18.4 3.5 %collective-permute-start.5 = (bf16[576,256]{1,0:T(8,128)(2,1)S(1)}, bf16[576,256]{1,0:T(8,128)(2,1)S(1)}, u32[]{:S(2)}, u32[]{:S(2)}) collective-permute-start(bf16[576,256]{1,0:T(8,128)(2,1)S(1)} %bitcast.69), channel_id=1, source_target_pairs={{0,8},{4,12},{8,16},{12,20},{16,24},{20,28},{1,9},{5,13},{9,17},{1... | collective-permute-start | bytes 884744 | tf_op jit(solution)/shard_map/ppermute | solution.py:605
  22.3 0.7 copy-done.28
  23.0 0.6 collective-permute-start.9
  23.6 0.7 pad_add_fusion.index
  24.3 1.5 collective-permute-start.1
  25.8 0.9 collective-permute-start.6
  26.7 0.6 collective-permute-done.5.refs_0_
  27.3 0.6 collective-permute-start.7
  28.0 6.3 %shard_map.194 = (bf16[3,256,576]{2,1,0:T(8,128)(2,1)}, bf16[3,256,384]{2,1,0:T(8,128)(2,1)}, bf16[256,576]{1,0:T(8,128)(2,1)}, bf16[576,576]{1,0:T(8,128)(2,1)}...) custom-call(s32[2]{0:T(128)} %pad_add_fusion.index, bf16[2,160,960]{2,1,0:T(8,128)(2,1)} %copy-done.22, ...), custom_call_target="tpu_custom_call" | custom-call | flops 6000000000 | tf_op jit(solution)/shard_map/pallas_call | solution.py:38
  34.3 1.4 collective-permute-start.8
  36.0 0.6 collective-permute-start.10
  36.6 5.6 %collective-permute-done.7.refs_2_ = bf16[576,256]{1,0:T(8,128)(2,1)} collective-permute-done((bf16[576,256]{1,0:T(8,128)(2,1)S(1)}, bf16[576,256]{1,0:T(8,128)(2,1)}, u32[]{:S(2)}, u32[]{:S(2)}) %collective-permute-start.7) | collective-permute-done | bytes 294944 | tf_op jit(solution)/shard_map/ppermute | solution.py:586
  42.2 7.5 %collective-permute-done.9.wi2 = bf16[144,3648]{1,0:T(8,128)(2,1)} collective-permute-done((bf16[144,3648]{1,0:T(8,128)(2,1)S(1)}, bf16[144,3648]{1,0:T(8,128)(2,1)}, u32[]{:S(2)}, u32[]{:S(2)}) %collective-permute-start.9) | collective-permute-done | bytes 1050656 | tf_op jit(solution)/shard_map/ppermute | solution.py:586
  50.2 7.4 %shard_map.195 = (f32[256,576]{1,0:T(8,128)}, f32[8,768]{1,0:T(8,128)}, bf16[2048,384]{1,0:T(8,128)(2,1)}, bf16[2048,576]{1,0:T(8,128)(2,1)}) custom-call(s32[2]{0:T(128)} %pad_add_fusion.index, bf16[256,576]{1,0:T(8,128)(2,1)} %get-tuple-element.85.queries, bf16[3,256,576]{2,1,0:T(8,128)(2,1)} %get-tuple-element.86.early_normed, ...), custom_call_target="tpu_custom_call" | custom-call | flops 20000000000 | tf_op jit(solution)/shard_map/pallas_call | solution.py:38
  57.6 1.4 collective-permute-done.10.wd2
  59.3 0.6 collective-permute-start.13
  59.8 1.1 collective-permute-done.14.wd3
  61.0 0.6 collective-permute-done.13.wd1
  61.6 0.8 copy-done.31
  62.3 16.7 %shard_map.196 = (bf16[576,256]{1,0:T(8,128)(2,1)}, f32[256,576]{1,0:T(8,128)}, bf16[256,576]{1,0:T(8,128)(2,1)}, f32[8,576]{1,0:T(8,128)}, bf16[3456,128]{1,0:T...) custom-call(s32[2]{0:T(128)} %pad_add_fusion.index, ...), custom_call_target="tpu_custom_call" | custom-call | flops 14000000000 | tf_op jit(solution)/shard_map/pallas_call | solution.py:38
  80.1 4.7 %collective-permute-done.16.got = bf16[2,2560,128]{2,1,0:T(8,128)(2,1)S(1)} collective-permute-done((bf16[2,2560,128]{2,1,0:T(8,128)(2,1)}, bf16[2,2560,128]{2,1,0:T(8,128)(2,1)S(1)}, u32[]{:S(2)}, u32[]{:S(2)}) %collective-permute-start.16) | collective-permute-done | bytes 1310752 | tf_op jit(solution)/shard_map/ppermute | solution.py:586
  84.8 1.1 copy-done.6
  85.9 1.1 copy-done.7
  87.0 0.8 shard_map.197
  88.4 0.6 collective-permute-start.17
  89.0 0.9 collective-permute-start.18
  90.9 5.9 %shard_map.198 = (bf16[8,256,384]{2,1,0:T(8,128)(2,1)S(1)}, f32[256,576]{1,0:T(8,128)S(1)}, bf16[1152,128]{1,0:T(8,128)(2,1)S(1)}, bf16[1152,128]{1,0:T(8,128)(2,1)S(1)}, bf16[2,1152,128]{2,1,0:T(8,128)(2,1)S(1)}) custom-call(s32[2]{0:T(128)S(1)} %copy-done.4, bf16[256,576]{1,0:T(8,128)(2,1)S(1)} %copy-done.11, bf16[2048,384]{1,0:T(8,128)(2,1)S(1)} %copy-done.13, ...), custom_call_target="tpu_custom_call" | custom-call | flops 23000000512 | tf_op jit(solution)/shard_map/pallas_call | solution.py:38
  96.8 8.7 %collective-permute-done.18 = bf16[2,4,320,128]{3,2,1,0:T(8,128)(2,1)S(1)} collective-permute-done((bf16[2,4,320,128]{3,2,1,0:T(8,128)(2,1)S(1)}, bf16[2,4,320,128]{3,2,1,0:T(8,128)(2,1)S(1)}, u32[]{:S(2)}, u32[]{:S(2)}) %collective-permute-start.18) | collective-permute-done | bytes 655392 | tf_op jit(solution)/shard_map/ppermute | solution.py:586
  105.5 4.7 %collective-permute-done.17.refs_2_ = bf16[3456,128]{1,0:T(8,128)(2,1)S(1)} collective-permute-done((bf16[3456,128]{1,0:T(8,128)(2,1)S(1)}, bf16[3456,128]{1,0:T(8,128)(2,1)S(1)}, u32[]{:S(2)}, u32[]{:S(2)}) %collective-permute-start.17) | collective-permute-done | bytes 884768 | tf_op jit(solution)/shard_map/ppermute | solution.py:586
  110.4 1.8 collective-permute-done.20
  112.3 0.6 collective-permute-start.21
  112.9 0.9 shard_map.199
  113.8 1.0 collective-permute-start.19
  114.9 10.9 %collective-permute-done.19 = bf16[4,432,128]{2,1,0:T(8,128)(2,1)S(1)} collective-permute-done((bf16[4,432,128]{2,1,0:T(8,128)(2,1)S(1)}, bf16[4,432,128]{2,1,0:T(8,128)(2,1)S(1)}, u32[]{:S(2)}, u32[]{:S(2)}) %collective-permute-start.19) | collective-permute-done | bytes 442400 | tf_op jit(solution)/shard_map/ppermute | solution.py:586
  125.8 2.7 %collective-permute-done.21 = bf16[2432,128]{1,0:T(8,128)(2,1)S(1)} collective-permute-done((bf16[2432,128]{1,0:T(8,128)(2,1)S(1)}, bf16[2432,128]{1,0:T(8,128)(2,1)S(1)}, u32[]{:S(2)}, u32[]{:S(2)}) %collective-permute-start.21) | collective-permute-done | bytes 622624 | tf_op jit(solution)/shard_map/ppermute | solution.py:586
  128.6 3.5 %collective-permute-start.31 = (bf16[2,432,128]{2,1,0:T(8,128)(2,1)S(1)}, bf16[2,432,128]{2,1,0:T(8,128)(2,1)S(1)}, u32[]{:S(2)}, u32[]{:S(2)}) collective-permute-start(bf16[2,432,128]{2,1,0:T(8,128)(2,1)S(1)} %pad_maximum_fusion.9), channel_id=1, source_target_pairs={{0,8},{4,12},{8,0},{12,4},{16,24},{20,28},{24,16},{28,20},{1,9},{5... | collective-permute-start | bytes 663560 | tf_op jit(solution)/shard_map/ppermute | solution.py:586
  132.1 0.7 shard_map.200
  132.8 2.3 %collective-permute-start.22 = (bf16[4,144,128]{2,1,0:T(8,128)(2,1)S(1)}, bf16[4,144,128]{2,1,0:T(8,128)(2,1)S(1)}, u32[]{:S(2)}, u32[]{:S(2)}) collective-permute-start(bf16[4,144,128]{2,1,0:T(8,128)(2,1)S(1)} %get-tuple-element.137), channel_id=1, source_target_pairs={{0,4},{4,0},{8,12},{12,8},{16,20},{20,16},{24,28},{28,24},{1,5},{5... | collective-permute-start | bytes 442376 | tf_op jit(solution)/shard_map/ppermute | solution.py:586
  135.3 4.6 %collective-permute-done.22 = bf16[4,144,128]{2,1,0:T(8,128)(2,1)S(1)} collective-permute-done((bf16[4,144,128]{2,1,0:T(8,128)(2,1)S(1)}, bf16[4,144,128]{2,1,0:T(8,128)(2,1)S(1)}, u32[]{:S(2)}, u32[]{:S(2)}) %collective-permute-start.22) | collective-permute-done | bytes 147488 | tf_op jit(solution)/shard_map/ppermute | solution.py:586
  139.9 8.8 %collective-permute-start.32 = (bf16[432,128]{1,0:T(8,128)(2,1)S(1)}, bf16[432,128]{1,0:T(8,128)(2,1)S(1)}, u32[]{:S(2)}, u32[]{:S(2)}) collective-permute-start(bf16[432,128]{1,0:T(8,128)(2,1)S(1)} %fusion.15), channel_id=1, source_target_pairs={{0,16},{4,20},{8,24},{12,28},{16,0},{20,4},{24,8},{28,12},{1,17},{... | collective-permute-start | bytes 331784 | tf_op jit(solution)/shard_map/ppermute | solution.py:586
  148.9 4.4 %collective-permute-done.32 = bf16[432,128]{1,0:T(8,128)(2,1)S(1)} collective-permute-done((bf16[432,128]{1,0:T(8,128)(2,1)S(1)}, bf16[432,128]{1,0:T(8,128)(2,1)S(1)}, u32[]{:S(2)}, u32[]{:S(2)}) %collective-permute-start.32) | collective-permute-done | bytes 110624 | tf_op jit(solution)/shard_map/ppermute | solution.py:586
  153.4 2.2 %collective-permute-start.33 = (bf16[432,128]{1,0:T(8,128)(2,1)S(1)}, bf16[432,128]{1,0:T(8,128)(2,1)S(1)}, u32[]{:S(2)}, u32[]{:S(2)}) collective-permute-start(bf16[432,128]{1,0:T(8,128)(2,1)S(1)} %fusion.9), channel_id=1, source_target_pairs={{0,16},{4,20},{8,24},{12,28},{16,0},{20,4},{24,8},{28,12},{1,17},{... | collective-permute-start | bytes 331784 | tf_op jit(solution)/shard_map/ppermute | solution.py:586
  155.5 1.4 collective-permute-done.23
  157.3 2.6 %collective-permute-done.33 = bf16[432,128]{1,0:T(8,128)(2,1)S(1)} collective-permute-done((bf16[432,128]{1,0:T(8,128)(2,1)S(1)}, bf16[432,128]{1,0:T(8,128)(2,1)S(1)}, u32[]{:S(2)}, u32[]{:S(2)}) %collective-permute-start.33) | collective-permute-done | bytes 110624 | tf_op jit(solution)/shard_map/ppermute | solution.py:586
  160.0 4.1 %collective-permute-done.24 = bf16[464,128]{1,0:T(8,128)(2,1)S(1)} collective-permute-done((bf16[464,128]{1,0:T(8,128)(2,1)S(1)}, bf16[464,128]{1,0:T(8,128)(2,1)S(1)}, u32[]{:S(2)}, u32[]{:S(2)}) %collective-permute-start.24) | collective-permute-done | bytes 118816 | tf_op jit(solution)/shard_map/ppermute | solution.py:586
  164.2 1.9 collective-permute-done.34
  166.1 2.1 %collective-permute-start.35 = (bf16[4,432,128]{2,1,0:T(8,128)(2,1)S(1)}, bf16[4,432,128]{2,1,0:T(8,128)(2,1)S(1)}, u32[]{:S(2)}, u32[]{:S(2)}) collective-permute-start(bf16[4,432,128]{2,1,0:T(8,128)(2,1)S(1)} %pad_maximum_fusion.5.refs_0_), channel_id=1, source_target_pairs={{0,4},{4,0},{8,12},{12,8},{16,20},{20,16},{24,28},{28,24},{1,5},{5... | collective-permute-start | bytes 1327112 | tf_op jit(solution)/shard_map/ppermute | solution.py:586
  168.2 4.0 %collective-permute-start.28 = (bf16[464,128]{1,0:T(8,128)(2,1)S(1)}, bf16[464,128]{1,0:T(8,128)(2,1)S(1)}, u32[]{:S(2)}, u32[]{:S(2)}) collective-permute-start(bf16[464,128]{1,0:T(8,128)(2,1)S(1)} %fusion.8), channel_id=1, source_target_pairs={{0,16},{4,20},{8,24},{12,28},{16,0},{20,4},{24,8},{28,12},{1,17},{... | collective-permute-start | bytes 356360 | tf_op jit(solution)/shard_map/ppermute | solution.py:586
  172.5 3.5 %collective-permute-done.28 = bf16[464,128]{1,0:T(8,128)(2,1)S(1)} collective-permute-done((bf16[464,128]{1,0:T(8,128)(2,1)S(1)}, bf16[464,128]{1,0:T(8,128)(2,1)S(1)}, u32[]{:S(2)}, u32[]{:S(2)}) %collective-permute-start.28) | collective-permute-done | bytes 118816 | tf_op jit(solution)/shard_map/ppermute | solution.py:586
  176.1 1.9 shard_map.203
  178.0 5.8 %collective-permute-done.26 = bf16[2,256,384]{2,1,0:T(8,128)(2,1)S(1)} collective-permute-done((bf16[2,256,384]{2,1,0:T(8,128)(2,1)S(1)}, bf16[2,256,384]{2,1,0:T(8,128)(2,1)S(1)}, u32[]{:S(2)}, u32[]{:S(2)}) %collective-permute-start.26) | collective-permute-done | bytes 393248 | tf_op jit(solution)/shard_map/ppermute | solution.py:586
  183.9 0.7 collective-permute-start.27
  184.6 1.7 collective-permute-done.29
  186.9 5.7 %collective-permute-done.27 = bf16[256,384]{1,0:T(8,128)(2,1)S(1)} collective-permute-done((bf16[256,384]{1,0:T(8,128)(2,1)S(1)}, bf16[256,384]{1,0:T(8,128)(2,1)S(1)}, u32[]{:S(2)}, u32[]{:S(2)}) %collective-permute-start.27) | collective-permute-done | bytes 196640 | tf_op jit(solution)/shard_map/ppermute | solution.py:586
  192.7 1.4 shard_map.201
  194.1 1.1 collective-permute-done.30.refs_1_
  195.2 2.1 %shard_map.202 = (f32[576,384]{1,0:T(8,128)}, f32[144,576]{1,0:T(8,128)}, f32[144,576]{1,0:T(8,128)}, f32[144,192]{1,0:T(8,128)}, f32[144,192]{1,0:T(8,128)}, /*index=5*/f32[8,144]{1,0:T(8,128)S(1)}) custom-call(s32[2]{0:T(128)S(1)} %copy-done.4, bf16[4,464,128]{2,1,0:T(8,128)(2,1)S(1)} %pad_maximum_fusion.4.refs_0_, ...), custom_call_target="tpu_custom_call" | custom-call | flops 3000000000 | tf_op jit(solution)/shard_map/pallas_call | solution.py:38
  (133 shorter events, 7.2 us)
Async XLA Ops:
  0.6 23.7 %collective-permute-start = (bf16[576,256]{1,0:T(8,128)(2,1)}, bf16[576,256]{1,0:T(8,128)(2,1)S(1)}, u32[]{:S(2)}, u32[]{:S(2)}) collective-permute-start(bf16[576,256]{1,0:T(8,128)(2,1)} %bitcast.65), channel_id=1, source_target_pairs={{0,16},{4,20},{8,24},{12,28},{1,17},{5,21},{9,25},{13,29},{2,18},{... | collective-permute-start | bytes 884744 | tf_op jit(solution)/shard_map/ppermute | solution.py:605
  8.6 13.5 %collective-permute-start.2 = (bf16[160,960]{1,0:T(8,128)(2,1)S(1)}, bf16[160,960]{1,0:T(8,128)(2,1)S(1)}, u32[]{:S(2)}, u32[]{:S(2)}) collective-permute-start(bf16[160,960]{1,0:T(8,128)(2,1)S(1)} %fusion.7), channel_id=1, source_target_pairs={{0,2},{1,3},{2,0},{3,1},{4,6},{5,7},{6,4},{7,5},{8,10},{9,11},{10,... | collective-permute-start | bytes 921608 | tf_op jit(solution)/shard_map/ppermute | solution.py:586
  13.9 3.0 %copy-start.2 = (bf16[1,256,576]{1,2,0:T(8,128)(2,1)S(1)}, bf16[1,256,576]{1,2,0:T(8,128)(2,1)}, u32[]{:S(2)}) copy-start(bf16[1,256,576]{1,2,0:T(8,128)(2,1)} %param.11) | copy-start | bytes 884740
  13.9 8.0 %copy-start.21 = (bf16[144,576]{1,0:T(8,128)(2,1)S(1)}, bf16[144,576]{1,0:T(8,128)(2,1)}, u32[]{:S(2)}) copy-start(bf16[144,576]{1,0:T(8,128)(2,1)} %param.13) | copy-start | bytes 497668
  13.9 8.0 %copy-start.26 = (bf16[144,192]{1,0:T(8,128)(2,1)S(1)}, bf16[144,192]{1,0:T(8,128)(2,1)}, u32[]{:S(2)}) copy-start(bf16[144,192]{1,0:T(8,128)(2,1)} %param.15) | copy-start | bytes 165892
  13.9 8.0 %copy-start.27 = (bf16[144,192]{1,0:T(8,128)(2,1)S(1)}, bf16[144,192]{1,0:T(8,128)(2,1)}, u32[]{:S(2)}) copy-start(bf16[144,192]{1,0:T(8,128)(2,1)} %param.14) | copy-start | bytes 165892
  16.9 5.3 %copy-start.24 = (bf16[144,1536]{1,0:T(8,128)(2,1)S(1)}, bf16[144,1536]{1,0:T(8,128)(2,1)}, u32[]{:S(2)}) copy-start(bf16[144,1536]{1,0:T(8,128)(2,1)} %param.18) | copy-start | bytes 1327108
  16.9 5.4 %copy-start.25 = (bf16[144,1536]{1,0:T(8,128)(2,1)S(1)}, bf16[144,1536]{1,0:T(8,128)(2,1)}, u32[]{:S(2)}) copy-start(bf16[144,1536]{1,0:T(8,128)(2,1)} %param.19) | copy-start | bytes 1327108
  16.9 8.9 %collective-permute-start.4 = (bf16[576,256]{1,0:T(8,128)(2,1)S(1)}, bf16[576,256]{1,0:T(8,128)(2,1)}, u32[]{:S(2)}, u32[]{:S(2)}) collective-permute-start(bf16[576,256]{1,0:T(8,128)(2,1)S(1)} %bitcast.68), channel_id=1, source_target_pairs={{0,4},{4,0},{8,12},{12,8},{16,20},{20,16},{24,28},{28,24},{1,5},{5... | collective-permute-start | bytes 884744 | tf_op jit(solution)/shard_map/ppermute | solution.py:586
  18.4 8.9 %collective-permute-start.5 = (bf16[576,256]{1,0:T(8,128)(2,1)S(1)}, bf16[576,256]{1,0:T(8,128)(2,1)S(1)}, u32[]{:S(2)}, u32[]{:S(2)}) collective-permute-start(bf16[576,256]{1,0:T(8,128)(2,1)S(1)} %bitcast.69), channel_id=1, source_target_pairs={{0,8},{4,12},{8,16},{12,20},{16,24},{20,28},{1,9},{5,13},{9,17},{1... | collective-permute-start | bytes 884744 | tf_op jit(solution)/shard_map/ppermute | solution.py:605
  22.2 5.8 %copy-start.22 = (bf16[2,160,960]{2,1,0:T(8,128)(2,1)}, bf16[2,160,960]{2,1,0:T(8,128)(2,1)S(1)}, u32[]{:S(2)}) copy-start(bf16[2,160,960]{2,1,0:T(8,128)(2,1)S(1)} %pad_maximum_fusion.2.here_pair) | copy-start | bytes 1843204
  22.2 5.8 %collective-permute-start.3 = (bf16[2,160,960]{2,1,0:T(8,128)(2,1)S(1)}, bf16[2,160,960]{2,1,0:T(8,128)(2,1)}, u32[]{:S(2)}, u32[]{:S(2)}) collective-permute-start(bf16[2,160,960]{2,1,0:T(8,128)(2,1)S(1)} %pad_maximum_fusion.2.here_pair), channel_id=1, source_target_pairs={{0,1},{1,0},{2,3},{3,2},{4,5},{5,4},{6,7},{7,6},{8,9},{9,8},{10,11... | collective-permute-start | bytes 1843208 | tf_op jit(solution)/shard_map/ppermute | solution.py:586
  23.0 26.7 %copy-start.29 = (bf16[144,3648]{1,0:T(8,128)(2,1)}, bf16[144,3648]{1,0:T(8,128)(2,1)S(1)}, u32[]{:S(2)}) copy-start(bf16[144,3648]{1,0:T(8,128)(2,1)S(1)} %constant_dynamic-update-slice_fusion.wi0) | copy-start | bytes 3151876
  23.0 26.7 %collective-permute-start.9 = (bf16[144,3648]{1,0:T(8,128)(2,1)S(1)}, bf16[144,3648]{1,0:T(8,128)(2,1)}, u32[]{:S(2)}, u32[]{:S(2)}) collective-permute-start(bf16[144,3648]{1,0:T(8,128)(2,1)S(1)} %constant_dynamic-update-slice_fusion.wi0), channel_id=1, source_target_pairs={{0,2},{1,3},{2,0},{3,1},{4,6},{5,7},{6,4},{7,5},{8,10},{9,11},{10,... | collective-permute-start | bytes 3151880 | tf_op jit(solution)/shard_map/ppermute | solution.py:586
  24.3 11.4 %copy-start.19 = (bf16[384,576]{0,1:T(8,128)(2,1)S(1)}, bf16[384,576]{0,1:T(8,128)(2,1)}, u32[]{:S(2)}) copy-start(bf16[384,576]{0,1:T(8,128)(2,1)} %param.20) | copy-start | bytes 1327108
  24.3 3.7 %copy-start.32 = (bf16[576,256]{1,0:T(8,128)(2,1)}, bf16[576,256]{1,0:T(8,128)(2,1)S(1)}, u32[]{:S(2)}) copy-start(bf16[576,256]{1,0:T(8,128)(2,1)S(1)} %collective-permute-done.refs_2_) | copy-start | bytes 884740
  24.3 10.0 %collective-permute-start.1 = (bf16[576,256]{1,0:T(8,128)(2,1)S(1)}, bf16[576,256]{1,0:T(8,128)(2,1)}, u32[]{:S(2)}, u32[]{:S(2)}) collective-permute-start(bf16[576,256]{1,0:T(8,128)(2,1)S(1)} %collective-permute-done.refs_2_), channel_id=1, source_target_pairs={{16,24},{20,28},{17,25},{21,29},{18,26},{22,30},{19,27},{23,31}} | collective-permute-start | bytes 884744 | tf_op jit(solution)/shard_map/ppermute | solution.py:733
  25.8 16.4 %collective-permute-start.6 = (bf16[576,256]{1,0:T(8,128)(2,1)S(1)}, bf16[576,256]{1,0:T(8,128)(2,1)}, u32[]{:S(2)}, u32[]{:S(2)}) collective-permute-start(bf16[576,256]{1,0:T(8,128)(2,1)S(1)} %collective-permute-done.refs_2_), channel_id=1, source_target_pairs={{0,4},{4,0},{8,12},{12,8},{16,20},{20,16},{24,28},{28,24},{1,5},{5... | collective-permute-start | bytes 884744 | tf_op jit(solution)/shard_map/ppermute | solution.py:586
  27.3 7.0 %copy-start.33 = (bf16[576,256]{1,0:T(8,128)(2,1)}, bf16[576,256]{1,0:T(8,128)(2,1)S(1)}, u32[]{:S(2)}) copy-start(bf16[576,256]{1,0:T(8,128)(2,1)S(1)} %collective-permute-done.5.refs_0_) | copy-start | bytes 884740
  27.3 14.8 %collective-permute-start.7 = (bf16[576,256]{1,0:T(8,128)(2,1)S(1)}, bf16[576,256]{1,0:T(8,128)(2,1)}, u32[]{:S(2)}, u32[]{:S(2)}) collective-permute-start(bf16[576,256]{1,0:T(8,128)(2,1)S(1)} %collective-permute-done.5.refs_0_), channel_id=1, source_target_pairs={{0,4},{4,0},{8,12},{12,8},{16,20},{20,16},{24,28},{28,24},{1,5},{5... | collective-permute-start | bytes 884744 | tf_op jit(solution)/shard_map/ppermute | solution.py:586
  34.3 15.4 %collective-permute-start.8 = (bf16[576,256]{1,0:T(8,128)(2,1)}, bf16[576,256]{1,0:T(8,128)(2,1)}, u32[]{:S(2)}, u32[]{:S(2)}) collective-permute-start(bf16[576,256]{1,0:T(8,128)(2,1)} %collective-permute-done.1.refs_3_), channel_id=1, source_target_pairs={{0,4},{4,0},{8,12},{12,8},{16,20},{20,16},{24,28},{28,24},{1,5},{5... | collective-permute-start | bytes 884744 | tf_op jit(solution)/shard_map/ppermute | solution.py:586
  36.0 23.0 %collective-permute-start.10 = (bf16[384,576]{1,0:T(8,128)(2,1)S(1)}, bf16[384,576]{1,0:T(8,128)(2,1)S(1)}, u32[]{:S(2)}, u32[]{:S(2)}) collective-permute-start(bf16[384,576]{1,0:T(8,128)(2,1)S(1)} %copy.26), channel_id=1, source_target_pairs={{0,2},{1,3},{2,0},{3,1},{4,6},{5,7},{6,4},{7,5},{8,10},{9,11},{10,... | collective-permute-start | bytes 1327112 | tf_op jit(solution)/shard_map/ppermute | solution.py:586
  49.7 11.9 %collective-permute-start.11 = (bf16[144,3648]{1,0:T(8,128)(2,1)S(1)}, bf16[144,3648]{1,0:T(8,128)(2,1)}, u32[]{:S(2)}, u32[]{:S(2)}) collective-permute-start(bf16[144,3648]{1,0:T(8,128)(2,1)S(1)} %constant_dynamic-update-slice_fusion.wi0), channel_id=1, source_target_pairs={{0,1},{1,0},{2,3},{3,2},{4,5},{5,4},{6,7},{7,6},{8,9},{9,8},{10,11... | collective-permute-start | bytes 3151880 | tf_op jit(solution)/shard_map/ppermute | solution.py:586
  49.7 11.9 %collective-permute-start.12 = (bf16[144,3648]{1,0:T(8,128)(2,1)}, bf16[144,3648]{1,0:T(8,128)(2,1)}, u32[]{:S(2)}, u32[]{:S(2)}) collective-permute-start(bf16[144,3648]{1,0:T(8,128)(2,1)} %collective-permute-done.9.wi2), channel_id=1, source_target_pairs={{0,1},{1,0},{2,3},{3,2},{4,5},{5,4},{6,7},{7,6},{8,9},{9,8},{10,11... | collective-permute-start | bytes 3151880 | tf_op jit(solution)/shard_map/ppermute | solution.py:586
  59.0 2.6 %copy-start.30 = (bf16[384,576]{1,0:T(8,128)(2,1)}, bf16[384,576]{1,0:T(8,128)(2,1)S(1)}, u32[]{:S(2)}) copy-start(bf16[384,576]{1,0:T(8,128)(2,1)S(1)} %collective-permute-done.10.wd2) | copy-start | bytes 1327108
  59.0 2.0 %collective-permute-start.14 = (bf16[384,576]{1,0:T(8,128)(2,1)S(1)}, bf16[384,576]{1,0:T(8,128)(2,1)}, u32[]{:S(2)}, u32[]{:S(2)}) collective-permute-start(bf16[384,576]{1,0:T(8,128)(2,1)S(1)} %collective-permute-done.10.wd2), channel_id=1, source_target_pairs={{0,1},{1,0},{2,3},{3,2},{4,5},{5,4},{6,7},{7,6},{8,9},{9,8},{10,11... | collective-permute-start | bytes 1327112 | tf_op jit(solution)/shard_map/ppermute | solution.py:586
  59.3 2.3 %collective-permute-start.13 = (bf16[384,576]{1,0:T(8,128)(2,1)S(1)}, bf16[384,576]{1,0:T(8,128)(2,1)S(1)}, u32[]{:S(2)}, u32[]{:S(2)}) collective-permute-start(bf16[384,576]{1,0:T(8,128)(2,1)S(1)} %copy.28.wd0), channel_id=1, source_target_pairs={{0,1},{1,0},{2,3},{3,2},{4,5},{5,4},{6,7},{7,6},{8,9},{9,8},{10,11... | collective-permute-start | bytes 1327112 | tf_op jit(solution)/shard_map/ppermute | solution.py:586
  62.3 22.4 %copy-start.4 = (s32[2]{0:T(128)S(1)}, s32[2]{0:T(128)}, u32[]{:S(2)}) copy-start(s32[2]{0:T(128)} %pad_add_fusion.index) | copy-start | bytes 28
  79.0 8.9 %collective-permute-start.15 = (bf16[2,3456,128]{2,1,0:T(8,128)(2,1)}, bf16[2,3456,128]{2,1,0:T(8,128)(2,1)S(1)}, u32[]{:S(2)}, u32[]{:S(2)}) collective-permute-start(bf16[2,3456,128]{2,1,0:T(8,128)(2,1)} %get-tuple-element.106), channel_id=1, source_target_pairs={{0,1},{1,0},{2,3},{3,2},{4,5},{5,4},{6,7},{7,6},{8,9},{9,8},{10,11... | collective-permute-start | bytes 5308424 | tf_op jit(solution)/shard_map/ppermute | solution.py:586
  79.2 5.6 %collective-permute-start.16 = (bf16[2,2560,128]{2,1,0:T(8,128)(2,1)}, bf16[2,2560,128]{2,1,0:T(8,128)(2,1)S(1)}, u32[]{:S(2)}, u32[]{:S(2)}) collective-permute-start(bf16[2,2560,128]{2,1,0:T(8,128)(2,1)} %get-tuple-element.109), channel_id=1, source_target_pairs={{0,1},{1,0},{2,3},{3,2},{4,5},{5,4},{6,7},{7,6},{8,9},{9,8},{10,11... | collective-permute-start | bytes 3932168 | tf_op jit(solution)/shard_map/ppermute | solution.py:586
  87.0 3.0 %copy-start.10 = (bf16[576,576]{1,0:T(8,128)(2,1)S(1)}, bf16[576,576]{1,0:T(8,128)(2,1)}, u32[]{:S(2)}) copy-start(bf16[576,576]{1,0:T(8,128)(2,1)} %get-tuple-element.114.query_weight) | copy-start | bytes 1990660
  87.0 3.0 %copy-start.11 = (bf16[256,576]{1,0:T(8,128)(2,1)S(1)}, bf16[256,576]{1,0:T(8,128)(2,1)}, u32[]{:S(2)}) copy-start(bf16[256,576]{1,0:T(8,128)(2,1)} %get-tuple-element.85.queries) | copy-start | bytes 884740
  87.0 3.0 %copy-start.12 = (bf16[2048,576]{1,0:T(8,128)(2,1)S(1)}, bf16[2048,576]{1,0:T(8,128)(2,1)}, u32[]{:S(2)}) copy-start(bf16[2048,576]{1,0:T(8,128)(2,1)} %get-tuple-element.113.normed) | copy-start | bytes 7077892
  87.0 2.9 %copy-start.13 = (bf16[2048,384]{1,0:T(8,128)(2,1)S(1)}, bf16[2048,384]{1,0:T(8,128)(2,1)}, u32[]{:S(2)}) copy-start(bf16[2048,384]{1,0:T(8,128)(2,1)} %get-tuple-element.103.kv_all) | copy-start | bytes 4718596
  87.0 2.9 %copy-start.14 = (f32[256,576]{1,0:T(8,128)S(1)}, f32[256,576]{1,0:T(8,128)}, u32[]{:S(2)}) copy-start(f32[256,576]{1,0:T(8,128)} %get-tuple-element.97.attended) | copy-start | bytes 1769476
  87.0 3.0 %copy-start.15 = (bf16[256,576]{1,0:T(8,128)(2,1)S(1)}, bf16[256,576]{1,0:T(8,128)(2,1)}, u32[]{:S(2)}) copy-start(bf16[256,576]{1,0:T(8,128)(2,1)} %get-tuple-element.111.attended_grad) | copy-start | bytes 884740
  88.1 2.4 %copy-start = (f32[2048,128]{1,0:T(8,128)S(1)}, f32[2048,128]{1,0:T(8,128)}, u32[]{:S(2)}) copy-start(f32[2048,128]{1,0:T(8,128)} %get-tuple-element.81.cosine) | copy-start | bytes 3145732
  88.1 2.7 %copy-start.1 = (f32[2048,128]{1,0:T(8,128)S(1)}, f32[2048,128]{1,0:T(8,128)}, u32[]{:S(2)}) copy-start(f32[2048,128]{1,0:T(8,128)} %get-tuple-element.82.sine) | copy-start | bytes 3145732
  88.1 2.7 %copy-start.9 = (bf16[576,384]{1,0:T(8,128)(2,1)S(1)}, bf16[576,384]{1,0:T(8,128)(2,1)}, u32[]{:S(2)}) copy-start(bf16[576,384]{1,0:T(8,128)(2,1)} %get-tuple-element.88.kv_weight) | copy-start | bytes 1327108
  88.1 2.7 %copy-start.16 = (f32[8,576]{1,0:T(8,128)S(1)}, f32[8,576]{1,0:T(8,128)}, u32[]{:S(2)}) copy-start(f32[8,576]{1,0:T(8,128)} %get-tuple-element.89.gains) | copy-start | bytes 55300
  88.1 2.7 %copy-start.17 = (f32[8,576]{1,0:T(8,128)S(1)}, f32[8,576]{1,0:T(8,128)}, u32[]{:S(2)}) copy-start(f32[8,576]{1,0:T(8,128)} %get-tuple-element.115.ffn_gain_grad) | copy-start | bytes 55300
  88.2 2.7 %copy-start.18 = (f32[8,768]{1,0:T(8,128)S(1)}, f32[8,768]{1,0:T(8,128)}, u32[]{:S(2)}) copy-start(f32[8,768]{1,0:T(8,128)} %get-tuple-element.112.lse) | copy-start | bytes 73732
  88.4 21.8 %collective-permute-start.17 = (bf16[3456,128]{1,0:T(8,128)(2,1)S(1)}, bf16[3456,128]{1,0:T(8,128)(2,1)S(1)}, u32[]{:S(2)}, u32[]{:S(2)}) collective-permute-start(bf16[3456,128]{1,0:T(8,128)(2,1)S(1)} %fusion), channel_id=1, source_target_pairs={{0,2},{1,3},{2,0},{3,1},{4,6},{5,7},{6,4},{7,5},{8,10},{9,11},{10,... | collective-permute-start | bytes 2654216 | tf_op jit(solution)/shard_map/ppermute | solution.py:586
  89.0 16.5 %collective-permute-start.18 = (bf16[2,4,320,128]{3,2,1,0:T(8,128)(2,1)S(1)}, bf16[2,4,320,128]{3,2,1,0:T(8,128)(2,1)S(1)}, u32[]{:S(2)}, u32[]{:S(2)}) collective-permute-start(bf16[2,4,320,128]{3,2,1,0:T(8,128)(2,1)S(1)} %get-tuple-element.123), channel_id=1, source_target_pairs={{0,4},{4,0},{8,12},{12,8},{16,20},{20,16},{24,28},{28,24},{1,5},{5... | collective-permute-start | bytes 1966088 | tf_op jit(solution)/shard_map/ppermute | solution.py:586
  110.2 2.0 %collective-permute-start.20 = (bf16[2,1152,128]{2,1,0:T(8,128)(2,1)S(1)}, bf16[2,1152,128]{2,1,0:T(8,128)(2,1)S(1)}, u32[]{:S(2)}, u32[]{:S(2)}) collective-permute-start(bf16[2,1152,128]{2,1,0:T(8,128)(2,1)S(1)} %get-tuple-element.132), channel_id=1, source_target_pairs={{0,1},{1,0},{2,3},{3,2},{4,5},{5,4},{6,7},{7,6},{8,9},{9,8},{10,11... | collective-permute-start | bytes 1769480 | tf_op jit(solution)/shard_map/ppermute | solution.py:586
  110.3 2.6 %copy-start.5 = (bf16[3456,128]{1,0:T(8,128)(2,1)S(1)}, bf16[3456,128]{1,0:T(8,128)(2,1)}, u32[]{:S(2)}) copy-start(bf16[3456,128]{1,0:T(8,128)(2,1)} %get-tuple-element.127.refs_0_) | copy-start | bytes 2654212
  112.3 16.1 %collective-permute-start.21 = (bf16[2432,128]{1,0:T(8,128)(2,1)S(1)}, bf16[2432,128]{1,0:T(8,128)(2,1)S(1)}, u32[]{:S(2)}, u32[]{:S(2)}) collective-permute-start(bf16[2432,128]{1,0:T(8,128)(2,1)S(1)} %pad_maximum_fusion.3), channel_id=1, source_target_pairs={{0,2},{1,3},{2,0},{3,1},{4,6},{5,7},{6,4},{7,5},{8,10},{9,11},{10,... | collective-permute-start | bytes 1867784 | tf_op jit(solution)/shard_map/ppermute | solution.py:586
  113.8 12.0 %collective-permute-start.19 = (bf16[4,432,128]{2,1,0:T(8,128)(2,1)S(1)}, bf16[4,432,128]{2,1,0:T(8,128)(2,1)S(1)}, u32[]{:S(2)}, u32[]{:S(2)}) collective-permute-start(bf16[4,432,128]{2,1,0:T(8,128)(2,1)S(1)} %get-tuple-element.129), channel_id=1, source_target_pairs={{0,4},{4,0},{8,12},{12,8},{16,20},{20,16},{24,28},{28,24},{1,5},{5... | collective-permute-start | bytes 1327112 | tf_op jit(solution)/shard_map/ppermute | solution.py:586
  128.6 11.3 %collective-permute-start.31 = (bf16[2,432,128]{2,1,0:T(8,128)(2,1)S(1)}, bf16[2,432,128]{2,1,0:T(8,128)(2,1)S(1)}, u32[]{:S(2)}, u32[]{:S(2)}) collective-permute-start(bf16[2,432,128]{2,1,0:T(8,128)(2,1)S(1)} %pad_maximum_fusion.9), channel_id=1, source_target_pairs={{0,8},{4,12},{8,0},{12,4},{16,24},{20,28},{24,16},{28,20},{1,9},{5... | collective-permute-start | bytes 663560 | tf_op jit(solution)/shard_map/ppermute | solution.py:586
  132.8 7.1 %collective-permute-start.22 = (bf16[4,144,128]{2,1,0:T(8,128)(2,1)S(1)}, bf16[4,144,128]{2,1,0:T(8,128)(2,1)S(1)}, u32[]{:S(2)}, u32[]{:S(2)}) collective-permute-start(bf16[4,144,128]{2,1,0:T(8,128)(2,1)S(1)} %get-tuple-element.137), channel_id=1, source_target_pairs={{0,4},{4,0},{8,12},{12,8},{16,20},{20,16},{24,28},{28,24},{1,5},{5... | collective-permute-start | bytes 442376 | tf_op jit(solution)/shard_map/ppermute | solution.py:586
  135.1 33.2 %collective-permute-start.25 = (bf16[4,256,384]{2,1,0:T(8,128)(2,1)S(1)}, bf16[4,256,384]{2,1,0:T(8,128)(2,1)S(1)}, u32[]{:S(2)}, u32[]{:S(2)}) collective-permute-start(bf16[4,256,384]{2,1,0:T(8,128)(2,1)S(1)} %slice.150), channel_id=1, source_target_pairs={{0,4},{4,0},{8,12},{12,8},{16,20},{20,16},{24,28},{28,24},{1,5},{5... | collective-permute-start | bytes 2359304 | tf_op jit(solution)/shard_map/ppermute | solution.py:586
  139.9 13.4 %collective-permute-start.32 = (bf16[432,128]{1,0:T(8,128)(2,1)S(1)}, bf16[432,128]{1,0:T(8,128)(2,1)S(1)}, u32[]{:S(2)}, u32[]{:S(2)}) collective-permute-start(bf16[432,128]{1,0:T(8,128)(2,1)S(1)} %fusion.15), channel_id=1, source_target_pairs={{0,16},{4,20},{8,24},{12,28},{16,0},{20,4},{24,8},{28,12},{1,17},{... | collective-permute-start | bytes 331784 | tf_op jit(solution)/shard_map/ppermute | solution.py:586
  148.8 8.1 %collective-permute-start.23 = (bf16[2,464,128]{2,1,0:T(8,128)(2,1)S(1)}, bf16[2,464,128]{2,1,0:T(8,128)(2,1)S(1)}, u32[]{:S(2)}, u32[]{:S(2)}) collective-permute-start(bf16[2,464,128]{2,1,0:T(8,128)(2,1)S(1)} %pad_maximum_fusion.7), channel_id=1, source_target_pairs={{0,8},{4,12},{8,0},{12,4},{16,24},{20,28},{24,16},{28,20},{1,9},{5... | collective-permute-start | bytes 712712 | tf_op jit(solution)/shard_map/ppermute | solution.py:586
  153.4 6.6 %collective-permute-start.33 = (bf16[432,128]{1,0:T(8,128)(2,1)S(1)}, bf16[432,128]{1,0:T(8,128)(2,1)S(1)}, u32[]{:S(2)}, u32[]{:S(2)}) collective-permute-start(bf16[432,128]{1,0:T(8,128)(2,1)S(1)} %fusion.9), channel_id=1, source_target_pairs={{0,16},{4,20},{8,24},{12,28},{16,0},{20,4},{24,8},{28,12},{1,17},{... | collective-permute-start | bytes 331784 | tf_op jit(solution)/shard_map/ppermute | solution.py:586
  156.9 7.2 %collective-permute-start.24 = (bf16[464,128]{1,0:T(8,128)(2,1)S(1)}, bf16[464,128]{1,0:T(8,128)(2,1)S(1)}, u32[]{:S(2)}, u32[]{:S(2)}) collective-permute-start(bf16[464,128]{1,0:T(8,128)(2,1)S(1)} %fusion.11), channel_id=1, source_target_pairs={{0,16},{4,20},{8,24},{12,28},{16,0},{20,4},{24,8},{28,12},{1,17},{... | collective-permute-start | bytes 356360 | tf_op jit(solution)/shard_map/ppermute | solution.py:586
  160.0 6.1 %collective-permute-start.34 = (bf16[2,432,128]{2,1,0:T(8,128)(2,1)S(1)}, bf16[2,432,128]{2,1,0:T(8,128)(2,1)S(1)}, u32[]{:S(2)}, u32[]{:S(2)}) collective-permute-start(bf16[2,432,128]{2,1,0:T(8,128)(2,1)S(1)} %pad_maximum_fusion.10), channel_id=1, source_target_pairs={{0,8},{4,12},{8,0},{12,4},{16,24},{20,28},{24,16},{28,20},{1,9},{5... | collective-permute-start | bytes 663560 | tf_op jit(solution)/shard_map/ppermute | solution.py:586
  166.1 9.9 %collective-permute-start.35 = (bf16[4,432,128]{2,1,0:T(8,128)(2,1)S(1)}, bf16[4,432,128]{2,1,0:T(8,128)(2,1)S(1)}, u32[]{:S(2)}, u32[]{:S(2)}) collective-permute-start(bf16[4,432,128]{2,1,0:T(8,128)(2,1)S(1)} %pad_maximum_fusion.5.refs_0_), channel_id=1, source_target_pairs={{0,4},{4,0},{8,12},{12,8},{16,20},{20,16},{24,28},{28,24},{1,5},{5... | collective-permute-start | bytes 1327112 | tf_op jit(solution)/shard_map/ppermute | solution.py:586
  168.2 7.7 %collective-permute-start.28 = (bf16[464,128]{1,0:T(8,128)(2,1)S(1)}, bf16[464,128]{1,0:T(8,128)(2,1)S(1)}, u32[]{:S(2)}, u32[]{:S(2)}) collective-permute-start(bf16[464,128]{1,0:T(8,128)(2,1)S(1)} %fusion.8), channel_id=1, source_target_pairs={{0,16},{4,20},{8,24},{12,28},{16,0},{20,4},{24,8},{28,12},{1,17},{... | collective-permute-start | bytes 356360 | tf_op jit(solution)/shard_map/ppermute | solution.py:586
  172.4 11.4 %collective-permute-start.26 = (bf16[2,256,384]{2,1,0:T(8,128)(2,1)S(1)}, bf16[2,256,384]{2,1,0:T(8,128)(2,1)S(1)}, u32[]{:S(2)}, u32[]{:S(2)}) collective-permute-start(bf16[2,256,384]{2,1,0:T(8,128)(2,1)S(1)} %pad_maximum_fusion.6), channel_id=1, source_target_pairs={{0,8},{4,12},{8,0},{12,4},{16,24},{20,28},{24,16},{28,20},{1,9},{5... | collective-permute-start | bytes 1179656 | tf_op jit(solution)/shard_map/ppermute | solution.py:586
  176.0 10.4 %collective-permute-start.29 = (bf16[2,464,128]{2,1,0:T(8,128)(2,1)S(1)}, bf16[2,464,128]{2,1,0:T(8,128)(2,1)S(1)}, u32[]{:S(2)}, u32[]{:S(2)}) collective-permute-start(bf16[2,464,128]{2,1,0:T(8,128)(2,1)S(1)} %pad_maximum_fusion.8), channel_id=1, source_target_pairs={{0,8},{4,12},{8,0},{12,4},{16,24},{20,28},{24,16},{28,20},{1,9},{5... | collective-permute-start | bytes 712712 | tf_op jit(solution)/shard_map/ppermute | solution.py:586
  183.9 8.8 %copy-start.3 = (bf16[1,256,576]{1,2,0:T(8,128)(2,1)S(1)}, bf16[1,256,576]{1,2,0:T(8,128)(2,1)}, u32[]{:S(2)}) copy-start(bf16[1,256,576]{1,2,0:T(8,128)(2,1)} %param.11) | copy-start | bytes 884740
  183.9 8.8 %copy-start.8 = (f32[256,576]{1,0:T(8,128)S(1)}, f32[256,576]{1,0:T(8,128)}, u32[]{:S(2)}) copy-start(f32[256,576]{1,0:T(8,128)} %get-tuple-element.117.middle_grad) | copy-start | bytes 1769476
  183.9 8.6 %collective-permute-start.27 = (bf16[256,384]{1,0:T(8,128)(2,1)S(1)}, bf16[256,384]{1,0:T(8,128)(2,1)S(1)}, u32[]{:S(2)}, u32[]{:S(2)}) collective-permute-start(bf16[256,384]{1,0:T(8,128)(2,1)S(1)} %fusion.10), channel_id=1, source_target_pairs={{0,16},{4,20},{8,24},{12,28},{16,0},{20,4},{24,8},{28,12},{1,17},{... | collective-permute-start | bytes 589832 | tf_op jit(solution)/shard_map/ppermute | solution.py:586
  186.5 8.7 %collective-permute-start.30 = (bf16[4,464,128]{2,1,0:T(8,128)(2,1)S(1)}, bf16[4,464,128]{2,1,0:T(8,128)(2,1)S(1)}, u32[]{:S(2)}, u32[]{:S(2)}) collective-permute-start(bf16[4,464,128]{2,1,0:T(8,128)(2,1)S(1)} %pad_maximum_fusion.4.refs_0_), channel_id=1, source_target_pairs={{0,4},{4,0},{8,12},{12,8},{16,20},{20,16},{24,28},{28,24},{1,5},{5... | collective-permute-start | bytes 1425416 | tf_op jit(solution)/shard_map/ppermute | solution.py:586
  (6 other events, 7.4 us)

commit v2 on v1

--- a/solution.py
+++ b/solution.py
@@ -18,7 +18,7 @@
 THETA = 100000.0
 NEGATIVE = -1e30
 LANES = 128
-FF_STEP = 256
+FF_STEP = 768
 MIB = 1024 * 1024
 
 BF16 = jnp.bfloat16
@@ -153,6 +153,16 @@
     query_out[...] = (rotated(linear, *tables, 1.0) * (1.0 / math.sqrt(HD))).astype(BF16)
 
 
+def project_kernel(index, kv_weight, gains, cosine, sine, *refs, places):
+    pieces, (normed_out, kv_out) = refs[: len(places)], refs[len(places) :]
+    for slot, (place, piece) in enumerate(zip(places, pieces)):
+        owner = owner_of(place, index[0])
+        tables = [table_at(table, owner, normed_out.shape[1]) for table in (cosine, sine)]
+        normed_out[slot], kv_out[slot] = projected(
+            piece[...].T, gains[0:1, :], kv_weight[...], *tables
+        )
+
+
 def fill_masks(masks):
     shape = masks.shape[1:]
     key_pos = lax.broadcasted_iota(jnp.int32, shape, 0)
@@ -169,8 +179,11 @@
 
 
 def forward_kernel(
-    index, queries, early_normed, early_kv, kv_weight, gains, cosine, sine, *refs, places, late_places
+    index, queries, early_normed, early_kv, kv_weight, gains, cosine, sine, *refs,
+    places, more_places, late_places,
 ):
+    if more_places:
+        more, refs = refs[:2], refs[2:]
     late, rest = refs[: len(late_places)], refs[len(late_places) :]
     attended, lse_out, kv_all, *rest = rest
     q_scr, acc_scr, max_scr, sum_scr, masks = rest[-5:]
@@ -182,15 +195,18 @@
         for slot, piece in enumerate(late):
             raw_scr[slot] = piece[...]
 
-        def copy(slot, carry):
-            owner = owner_of(one_of(places, slot), here)
-
-            @pl.when((owner >= 0) & (owner <= here))
-            def _():
-                normed_all[block_at(owner, rows), :] = early_normed[slot]
-                kv_all[block_at(owner, rows), :] = early_kv[slot]
-
-            return carry
+        def copies(places, normed, kv):
+            def copy(slot, carry):
+                owner = owner_of(one_of(places, slot), here)
+
+                @pl.when((owner >= 0) & (owner <= here))
+                def _():
+                    normed_all[block_at(owner, rows), :] = normed[slot]
+                    kv_all[block_at(owner, rows), :] = kv[slot]
+
+                return carry
+
+            lax.fori_loop(0, len(places), copy, 0)
 
         def project(slot, carry):
             owner = owner_of(one_of(late_places, slot), here)
@@ -209,7 +225,8 @@
 
             return carry
 
-        lax.fori_loop(0, len(places), copy, 0)
+        copies(places, early_normed, early_kv)
+        copies(more_places, *more)
         lax.fori_loop(0, len(late_places), project, 0)
     else:
         kv_all[...] = early_kv[...]
@@ -275,13 +292,14 @@
     wi0, wi1, wi2, wi3, wd0, wd1, wd2, wd3,
     layer_out, middle_grad_out, attended_grad_out, gain_grad,
     in_mine, in_along, in_send, mine, along, send,
-    in_weight, down_weight, result_scr, back_scr, tile_scr, down_scr,
+    in_weight, down_weight, result_scr, back_scr, tile_scr, down_scr, in_flat, flat,
+    count,
 ):
     me = index[1]
     assembled(in_weight, (wi0, wi1, wi2, wi3), me)
     assembled(down_weight, (wd0, wd1, wd2, wd3), me)
-    in_outs = (in_mine, in_send.at[0], in_along, in_send.at[1])
-    outs = (mine, send.at[0], along, send.at[1])
+    in_outs = [in_flat.at[relative] for relative in range(in_flat.shape[0])]
+    outs = [flat.at[relative] for relative in range(flat.shape[0])]
     gain = gains[1:2, :]
     ff = down_weight.shape[0]
     out_weight = in_weight.at[:, 2 * ff :]
@@ -359,6 +377,20 @@
     base += wide // LANES * in_rows
     for out in outs:
         out[base:, :] = jnp.zeros((out.shape[0] - base, LANES), BF16)
+    for parts, to in (
+        (in_outs, (in_mine, in_send.at[0], in_along, in_send.at[1])),
+        (outs, (mine, send.at[0], along, send.at[1])),
+    ):
+        for part, out in zip(parts, to):
+            in_slots(index[0], part, out, count)
+
+
+def in_slots(here, flat, out, count):
+    rows = flat.shape[0] // count
+    for apart in range(count):
+        slot = (apart & 1) * (count // 2) + apart // 2
+        start = pl.multiple_of((here ^ apart) * rows, 16)
+        out[slot * rows : (slot + 1) * rows, :] = flat[pl.ds(start, rows), :]
 
 
 def put_small(outs, me, tile_scr, query_grad, kv_grad, query_weight, kv_weight, gains, ffn_gain_grad):
@@ -511,11 +543,6 @@
         (send if apart & 1 else keep)[apart // 2] = total.astype(BF16)
 
 
-def spread_both_kernel(index, mine, along, got, keep_mine, keep_along, send, count):
-    spread_kernel(index, mine, got.at[0], keep_mine, send.at[0], count=count)
-    spread_kernel(index, along, got.at[1], keep_along, send.at[1], count=count)
-
-
 def flattened(index, pieces, parts):
     here = index[0]
     if len(pieces) == 1:
@@ -661,18 +688,6 @@
     )
 
 
-def spread_both(index, mine, along, got):
-    count = lax.axis_size("ctx")
-    shape = shaped((count // 2, mine.shape[0] // count, LANES), BF16)
-    return call(
-        functools.partial(spread_both_kernel, count=count),
-        (shape, shape, shaped((2,) + shape.shape, BF16)),
-        (index, mine, along, got),
-        micros=3,
-        smem=1,
-    )
-
-
 def padded_rows(rows, count):
     return -(-rows // (16 * count)) * 16 * count
 
@@ -735,7 +750,8 @@
         tables = (cosine, sine)
 
     places = (0, 1, 4) if by_hops else (0,)
-    late_places = (2, 5, 3, 6, 7) if by_hops else ()
+    more_places = (2, 5) if by_hops else ()
+    late_places = (3, 6, 7) if by_hops else ()
     early = (tokens, mate, behind_two) if by_hops else (tokens,)
     early_normed, early_kv, queries, full_query, full_kv, gains = call(
         functools.partial(early_kernel, places=places, slice_rows=slice_rows),
@@ -758,13 +774,18 @@
     )
     if by_hops:
         behind_three, queries = lax.optimization_barrier((behind_three, queries))
-        late = (
-            behind_one,
-            swap(behind_two, "ctx", 0),
-            swap(behind_one, "ctx", 0),
-            behind_three,
-            swap(behind_three, "ctx", 0),
-        )
+        more = call(
+            functools.partial(project_kernel, places=more_places),
+            (
+                shaped((len(more_places), rows, width), BF16),
+                shaped((len(more_places), rows, 2 * KVW), BF16),
+            ),
+            (index, full_kv, gains, *tables, behind_one, swap(behind_two, "ctx", 0)),
+            micros=3,
+            smem=1,
+            vmem=60,
+        )
+        late = (swap(behind_one, "ctx", 0), behind_three, swap(behind_three, "ctx", 0))
         normed_shape = (shaped((ctx_count * rows, width), BF16),)
         raw_scr = (pltpu.VMEM((len(late_places), width, rows), BF16),)
     else:
@@ -775,6 +796,7 @@
         early_kv = jnp.concatenate(
             [turned_heads(linear[:, :KVW], *full_tables), linear[:, KVW:]], -1
         ).astype(BF16)
+        more = ()
         late = ()
         normed_shape = ()
         raw_scr = ()
@@ -786,14 +808,16 @@
     down_core = swap(down_weight, "ws", 0)
 
     attended, lse, kv_all, *normed_out = call(
-        functools.partial(forward_kernel, places=places, late_places=late_places),
+        functools.partial(
+            forward_kernel, places=places, more_places=more_places, late_places=late_places
+        ),
         (
             shaped((rows, width), F32),
             shaped((8, GROUPS * rows), F32),
             shaped((ctx_count * rows, 2 * KVW), BF16),
             *normed_shape,
         ),
-        (index, queries, early_normed, early_kv, full_kv, gains, *tables, *late),
+        (index, queries, early_normed, early_kv, full_kv, gains, *tables, *more, *late),
         scratch=(
             *raw_scr,
             pltpu.VMEM((KV, GROUPS * rows, HD), BF16),
@@ -825,7 +849,7 @@
         )
 
     layer_out, middle_grad, attended_grad, ffn_gain_grad, *tiles = call(
-        ffn_kernel,
+        functools.partial(ffn_kernel, count=ctx_count if by_hops else 1),
         (
             shaped((width, rows), BF16),
             shaped((rows, width), F32),
@@ -842,6 +866,8 @@
             pltpu.VMEM((rows, width), F32),
             pltpu.VMEM((width, 2 * ff), BF16),
             pltpu.VMEM((ff, wide), BF16),
+            pltpu.VMEM((owners, first_count, LANES), BF16),
+            pltpu.VMEM((owners, second_count, LANES), BF16),
         ),
         micros=14,
         smem=1,
@@ -853,7 +879,15 @@
     in_got = swap(in_send, "ws", 0)
     in_crossing = added(in_along, in_got[1])
     if by_hops:
-        keep_mine, keep_along, to_mate = spread_both(index, mine, along, got)
+        half = second_count // 2
+
+        def halves(value):
+            return value[:half].reshape(ctx_count // 2, second_rows, LANES), value[half:]
+
+        keep_mine, mine_to_mate = halves(added(mine, got[0]))
+        keep_along, along_to_mate = halves(added(along, got[1]))
+        to_mate = jnp.stack([mine_to_mate, along_to_mate])
+        to_mate = to_mate.reshape(2, ctx_count // 2, second_rows, LANES)
     else:
         to_mate = added(along, got[1])
     attended_grad, in_crossing, to_mate = lax.optimization_barrier(
@@ -911,7 +945,10 @@
     small_got = swap(small_send, "ws", 0)
 
     if by_hops:
-        in_keep, in_to_mate = spread(index, (in_mine, in_got[0], in_crossed))
+        in_keep, in_to_mate = (
+            added(in_mine[at], in_got[0, at], in_crossed[at]).reshape(-1, first_rows, LANES)
+            for at in (slice(first_count // 2), slice(first_count // 2, None))
+        )
         in_from_mate = swap(in_to_mate, "ctx", 0)
         more_rows = keep_along.shape[0] * second_rows
         crossing = jnp.concatenate(

time: 198 us -> 191 us (0.965)
  waiting for transfers between devices: 87.1 us -> 82.2 us
  local copies, waits for them, and re-layouts: 6.42 us -> 3.29 us
  other arithmetic: 11.6 us -> 13.8 us
    ppermute x33, waiting for transfers between devices: 86.5 us -> 81.7 us  [swap(): return lax.ppermute(value, axis, [(i, i ^ 1 << bit) for i in range(count)])]
    unnamed x71 -> x65, local copies, waits for them, and re-layouts: 5.25 us -> 2.07 us
    ppermute x33, starting transfers between devices: 36.5 us -> 33.9 us  [swap(): return lax.ppermute(value, axis, [(i, i ^ 1 << bit) for i in range(count)])]
    convert_element_type x13 -> x15, other arithmetic: 1.12 us -> 3.28 us  [added(): return total.astype(values[0].dtype)]
    pallas_call x10 -> x9, Pallas kernels: 44 us -> 43.9 us  [call(): pl.pallas_call(kernel, out_shape=outs, in_specs=[SMEM_SPEC] * smem + [VME...]
  transfers between devices with their start and end apart: 36 -> 36, of which waited for: 23 -> 24; matrix products, arithmetic and copies ran while one was open for 6% -> 7% of each run, Pallas kernels for 13% -> 14%
where the time goes in v2:
time: 191 us
  waiting for transfers between devices  82.2 us (43%)
  starting transfers between devices  46.2 us (24%)
  Pallas kernels  43.9 us (23%)
  other arithmetic  13.8 us (7%)
  local copies, waits for them, and re-layouts  3.29 us (2%)
    ppermute x33, waiting for transfers between devices, swap(): return lax.ppermute(value, axis, [(i, i ^ 1 << bit) for i in range(count)])  81.7 us
    pallas_call x9, Pallas kernels, call(): pl.pallas_call(kernel, out_shape=outs, in_specs=[SMEM_SPEC] * smem + [VME...  43.9 us
    ppermute x33, starting transfers between devices, swap(): return lax.ppermute(value, axis, [(i, i ^ 1 << bit) for i in range(count)])  33.9 us
    ppermute x2, starting transfers between devices, shifted(): return lax.ppermute(value, 'ctx', [(i, j % count) for i, j in pairs])  10.9 us
    neg x2, other arithmetic, wide_tables(): -sine  4.26 us
  transfers between devices with their start and end apart: 36, of which 24 were waited for; matrix products, arithmetic and copies ran while one was open for 7% of the time, Pallas kernels for 14%

profile of v2, /device:TPU:0, one launch (start us, length us, event | category | flops | bytes accessed | tf_op | source)
XLA Modules:
  0.0 190.7 jit_solution(13485488014802232500)
XLA Ops:
  0.6 6.7 %collective-permute-start = (bf16[576,256]{1,0:T(8,128)(2,1)}, bf16[576,256]{1,0:T(8,128)(2,1)}, u32[]{:S(2)}, u32[]{:S(2)}) collective-permute-start(bf16[576,256]{1,0:T(8,128)(2,1)} %bitcast.107), channel_id=1, source_target_pairs={{0,16},{4,20},{8,24},{12,28},{1,17},{5,21},{9,25},{13,29},{2,18},{... | collective-permute-start | bytes 884744 | tf_op jit(solution)/shard_map/ppermute | solution.py:632
  7.3 0.7 pad_maximum_fusion.15
  8.2 1.1 fusion.13
  9.3 1.6 collective-permute-start.2
  10.8 3.7 %fusion.12 = (f32[2048,32]{1,0:T(8,128)S(1)}, f32[2048,32]{1,0:T(8,128)S(1)}, f32[2048,32]{1,0:T(8,128)S(1)}) fusion(f32[32]{0:T(128)S(1)} %multiply_exponential_fusion, f32[2048]{0:T(1024)S(1)} %iota_convert_fusion), kind=kLoop, calls=%fused_computation.51 | loop fusion | flops 131072 | bytes 794752 | tf_op jit(solution)/shard_map/neg | solution.py:738
  14.6 3.0 %pad_maximum_fusion = (f32[2048,128]{1,0:T(8,128)}, f32[2048,128]{1,0:T(8,128)}) fusion(f32[2048,32]{1,0:T(8,128)S(1)} %get-tuple-element.159, f32[2048,32]{1,0:T(8,128)S(1)} %get-tuple-element.158, f32[2048,32]{1,0:T(8,128)S(1)} %get-tuple-element.157), kind=kLoop, calls=%fused_computation.8 | loop fusion | flops 1572864 | bytes 2883584 | tf_op jit(solution)/shard_map/concatenate | solution.py:738
  17.6 1.5 collective-permute-start.4
  19.1 4.2 %collective-permute-start.5 = (bf16[576,256]{1,0:T(8,128)(2,1)S(1)}, bf16[576,256]{1,0:T(8,128)(2,1)}, u32[]{:S(2)}, u32[]{:S(2)}) collective-permute-start(bf16[576,256]{1,0:T(8,128)(2,1)S(1)} %bitcast.111), channel_id=1, source_target_pairs={{0,8},{4,12},{8,16},{12,20},{16,24},{20,28},{1,9},{5,13},{9,17},{1... | collective-permute-start | bytes 884744 | tf_op jit(solution)/shard_map/ppermute | solution.py:632
  23.7 0.7 copy-done.26
  24.4 0.6 collective-permute-start.9
  25.0 0.6 pad_add_fusion.index
  25.6 0.5 collective-permute-start.6
  26.1 1.4 collective-permute-start.1
  27.5 0.5 collective-permute-done.5.refs_0_
  28.0 1.0 collective-permute-start.7
  29.1 6.3 %shard_map.194 = (bf16[3,256,576]{2,1,0:T(8,128)(2,1)}, bf16[3,256,384]{2,1,0:T(8,128)(2,1)}, bf16[256,576]{1,0:T(8,128)(2,1)}, bf16[576,576]{1,0:T(8,128)(2,1)}...) custom-call(s32[2]{0:T(128)} %pad_add_fusion.index, bf16[2,160,960]{2,1,0:T(8,128)(2,1)} %copy-done.20, ...), custom_call_target="tpu_custom_call" | custom-call | flops 6000000000 | tf_op jit(solution)/shard_map/pallas_call | solution.py:38
  35.3 1.1 collective-permute-start.8
  36.7 1.1 collective-permute-start.10
  37.8 3.7 %shard_map.195 = (bf16[2,256,576]{2,1,0:T(8,128)(2,1)}, bf16[2,256,384]{2,1,0:T(8,128)(2,1)}) custom-call(s32[2]{0:T(128)} %pad_add_fusion.index, bf16[576,384]{1,0:T(8,128)(2,1)} %get-tuple-element.83.kv_weight, f32[8,576]{1,0:T(8,128)} %get-tuple-element.84.gains, f32[2048,128]{1,0:T(8,128)} %get-tuple-element.76.cosine, ...), custom_call_target="tpu_custom_call" | custom-call | flops 3000000000 | tf_op jit(solution)/shard_map/pallas_call | solution.py:38
  41.4 0.7 collective-permute-done.7.refs_2_
  42.2 8.8 %collective-permute-done.9.wi2 = bf16[144,3648]{1,0:T(8,128)(2,1)S(1)} collective-permute-done((bf16[144,3648]{1,0:T(8,128)(2,1)S(1)}, bf16[144,3648]{1,0:T(8,128)(2,1)S(1)}, u32[]{:S(2)}, u32[]{:S(2)}) %collective-permute-start.9) | collective-permute-done | bytes 1050656 | tf_op jit(solution)/shard_map/ppermute | solution.py:613
  51.7 7.5 %shard_map.196 = (f32[256,576]{1,0:T(8,128)}, f32[8,768]{1,0:T(8,128)}, bf16[2048,384]{1,0:T(8,128)(2,1)}, bf16[2048,576]{1,0:T(8,128)(2,1)}) custom-call(s32[2]{0:T(128)} %pad_add_fusion.index, bf16[256,576]{1,0:T(8,128)(2,1)} %get-tuple-element.80.queries, bf16[3,256,576]{2,1,0:T(8,128)(2,1)} %get-tuple-element.81.early_normed, ...), custom_call_target="tpu_custom_call" | custom-call | flops 20000000000 | tf_op jit(solution)/shard_map/pallas_call | solution.py:38
  59.2 1.3 collective-permute-done.10.wd2
  60.8 0.6 collective-permute-start.13
  61.3 1.4 collective-permute-done.14.wd3
  63.1 0.8 copy-done.29
  63.8 14.4 %shard_map.197 = (bf16[576,256]{1,0:T(8,128)(2,1)}, f32[256,576]{1,0:T(8,128)}, bf16[256,576]{1,0:T(8,128)(2,1)}, f32[8,576]{1,0:T(8,128)}, bf16[3456,128]{1,0:T...) custom-call(s32[2]{0:T(128)} %pad_add_fusion.index, ...), custom_call_target="tpu_custom_call" | custom-call | flops 14000000000 | tf_op jit(solution)/shard_map/pallas_call | solution.py:38
  78.8 2.7 %collective-permute-done.16 = bf16[2,2560,128]{2,1,0:T(8,128)(2,1)S(1)} collective-permute-done((bf16[2,2560,128]{2,1,0:T(8,128)(2,1)}, bf16[2,2560,128]{2,1,0:T(8,128)(2,1)S(1)}, u32[]{:S(2)}, u32[]{:S(2)}) %collective-permute-start.16) | collective-permute-done | bytes 1310752 | tf_op jit(solution)/shard_map/ppermute | solution.py:613
  81.5 1.8 fusion.2
  83.5 0.5 collective-permute-done.15
  84.4 0.6 collective-permute-start.17
  85.0 1.1 collective-permute-start.18
  86.1 5.9 %shard_map.198 = (bf16[8,256,384]{2,1,0:T(8,128)(2,1)S(1)}, f32[256,576]{1,0:T(8,128)S(1)}, bf16[1152,128]{1,0:T(8,128)(2,1)S(1)}, bf16[1152,128]{1,0:T(8,128)(2,1)S(1)}, bf16[2,1152,128]{2,1,0:T(8,128)(2,1)S(1)}) custom-call(s32[2]{0:T(128)S(1)} %copy-done.4, bf16[256,576]{1,0:T(8,128)(2,1)S(1)} %copy-done.8, bf16[2048,384]{1,0:T(8,128)(2,1)S(1)} %copy-done.10, ...), custom_call_target="tpu_custom_call" | custom-call | flops 23000000512 | tf_op jit(solution)/shard_map/pallas_call | solution.py:38
  92.0 9.5 %collective-permute-done.18 = bf16[2,4,320,128]{3,2,1,0:T(8,128)(2,1)S(1)} collective-permute-done((bf16[2,4,320,128]{3,2,1,0:T(8,128)(2,1)S(1)}, bf16[2,4,320,128]{3,2,1,0:T(8,128)(2,1)S(1)}, u32[]{:S(2)}, u32[]{:S(2)}) %collective-permute-start.18) | collective-permute-done | bytes 655392 | tf_op jit(solution)/shard_map/ppermute | solution.py:613
  101.5 4.7 %collective-permute-done.17 = bf16[3456,128]{1,0:T(8,128)(2,1)S(1)} collective-permute-done((bf16[3456,128]{1,0:T(8,128)(2,1)S(1)}, bf16[3456,128]{1,0:T(8,128)(2,1)S(1)}, u32[]{:S(2)}, u32[]{:S(2)}) %collective-permute-start.17) | collective-permute-done | bytes 884768 | tf_op jit(solution)/shard_map/ppermute | solution.py:613
  106.1 0.5 fusion.25
  106.8 1.3 collective-permute-done.20
  108.3 0.6 collective-permute-start.21
  109.2 1.1 collective-permute-start.19
  110.5 10.7 %collective-permute-done.19 = bf16[4,432,128]{2,1,0:T(8,128)(2,1)S(1)} collective-permute-done((bf16[4,432,128]{2,1,0:T(8,128)(2,1)S(1)}, bf16[4,432,128]{2,1,0:T(8,128)(2,1)S(1)}, u32[]{:S(2)}, u32[]{:S(2)}) %collective-permute-start.19) | collective-permute-done | bytes 442400 | tf_op jit(solution)/shard_map/ppermute | solution.py:613
  121.2 3.2 %collective-permute-done.21 = bf16[2432,128]{1,0:T(8,128)(2,1)S(1)} collective-permute-done((bf16[2432,128]{1,0:T(8,128)(2,1)S(1)}, bf16[2432,128]{1,0:T(8,128)(2,1)S(1)}, u32[]{:S(2)}, u32[]{:S(2)}) %collective-permute-start.21) | collective-permute-done | bytes 622624 | tf_op jit(solution)/shard_map/ppermute | solution.py:613
  124.6 2.3 %collective-permute-start.31 = (bf16[2,432,128]{2,1,0:T(8,128)(2,1)S(1)}, bf16[2,432,128]{2,1,0:T(8,128)(2,1)S(1)}, u32[]{:S(2)}, u32[]{:S(2)}) collective-permute-start(bf16[2,432,128]{2,1,0:T(8,128)(2,1)S(1)} %pad_maximum_fusion.10), channel_id=1, source_target_pairs={{0,8},{4,12},{8,0},{12,4},{16,24},{20,28},{24,16},{28,20},{1,9},{5... | collective-permute-start | bytes 663560 | tf_op jit(solution)/shard_map/ppermute | solution.py:613
  126.9 0.7 shard_map.199
  127.5 2.3 %collective-permute-start.22 = (bf16[4,144,128]{2,1,0:T(8,128)(2,1)S(1)}, bf16[4,144,128]{2,1,0:T(8,128)(2,1)S(1)}, u32[]{:S(2)}, u32[]{:S(2)}) collective-permute-start(bf16[4,144,128]{2,1,0:T(8,128)(2,1)S(1)} %get-tuple-element.128), channel_id=1, source_target_pairs={{0,4},{4,0},{8,12},{12,8},{16,20},{20,16},{24,28},{28,24},{1,5},{5... | collective-permute-start | bytes 442376 | tf_op jit(solution)/shard_map/ppermute | solution.py:613
  130.1 4.6 %collective-permute-done.22 = bf16[4,144,128]{2,1,0:T(8,128)(2,1)S(1)} collective-permute-done((bf16[4,144,128]{2,1,0:T(8,128)(2,1)S(1)}, bf16[4,144,128]{2,1,0:T(8,128)(2,1)S(1)}, u32[]{:S(2)}, u32[]{:S(2)}) %collective-permute-start.22) | collective-permute-done | bytes 147488 | tf_op jit(solution)/shard_map/ppermute | solution.py:613
  134.7 6.9 %collective-permute-start.32 = (bf16[432,128]{1,0:T(8,128)(2,1)S(1)}, bf16[432,128]{1,0:T(8,128)(2,1)S(1)}, u32[]{:S(2)}, u32[]{:S(2)}) collective-permute-start(bf16[432,128]{1,0:T(8,128)(2,1)S(1)} %fusion.15), channel_id=1, source_target_pairs={{0,16},{4,20},{8,24},{12,28},{16,0},{20,4},{24,8},{28,12},{1,17},{... | collective-permute-start | bytes 331784 | tf_op jit(solution)/shard_map/ppermute | solution.py:613
  141.7 4.0 %collective-permute-done.32 = bf16[432,128]{1,0:T(8,128)(2,1)S(1)} collective-permute-done((bf16[432,128]{1,0:T(8,128)(2,1)S(1)}, bf16[432,128]{1,0:T(8,128)(2,1)S(1)}, u32[]{:S(2)}, u32[]{:S(2)}) %collective-permute-start.32) | collective-permute-done | bytes 110624 | tf_op jit(solution)/shard_map/ppermute | solution.py:613
  145.8 2.4 %collective-permute-start.33 = (bf16[432,128]{1,0:T(8,128)(2,1)S(1)}, bf16[432,128]{1,0:T(8,128)(2,1)S(1)}, u32[]{:S(2)}, u32[]{:S(2)}) collective-permute-start(bf16[432,128]{1,0:T(8,128)(2,1)S(1)} %fusion.17), channel_id=1, source_target_pairs={{0,16},{4,20},{8,24},{12,28},{16,0},{20,4},{24,8},{28,12},{1,17},{... | collective-permute-start | bytes 331784 | tf_op jit(solution)/shard_map/ppermute | solution.py:613
  148.2 1.4 collective-permute-done.23
  150.0 3.0 %collective-permute-done.33 = bf16[432,128]{1,0:T(8,128)(2,1)S(1)} collective-permute-done((bf16[432,128]{1,0:T(8,128)(2,1)S(1)}, bf16[432,128]{1,0:T(8,128)(2,1)S(1)}, u32[]{:S(2)}, u32[]{:S(2)}) %collective-permute-start.33) | collective-permute-done | bytes 110624 | tf_op jit(solution)/shard_map/ppermute | solution.py:613
  153.1 2.4 %collective-permute-done.24 = bf16[464,128]{1,0:T(8,128)(2,1)S(1)} collective-permute-done((bf16[464,128]{1,0:T(8,128)(2,1)S(1)}, bf16[464,128]{1,0:T(8,128)(2,1)S(1)}, u32[]{:S(2)}, u32[]{:S(2)}) %collective-permute-start.24) | collective-permute-done | bytes 118816 | tf_op jit(solution)/shard_map/ppermute | solution.py:613
  155.6 3.4 %collective-permute-done.34 = bf16[2,432,128]{2,1,0:T(8,128)(2,1)S(1)} collective-permute-done((bf16[2,432,128]{2,1,0:T(8,128)(2,1)S(1)}, bf16[2,432,128]{2,1,0:T(8,128)(2,1)S(1)}, u32[]{:S(2)}, u32[]{:S(2)}) %collective-permute-start.34) | collective-permute-done | bytes 221216 | tf_op jit(solution)/shard_map/ppermute | solution.py:613
  159.1 2.0 %collective-permute-start.35 = (bf16[4,432,128]{2,1,0:T(8,128)(2,1)S(1)}, bf16[4,432,128]{2,1,0:T(8,128)(2,1)S(1)}, u32[]{:S(2)}, u32[]{:S(2)}) collective-permute-start(bf16[4,432,128]{2,1,0:T(8,128)(2,1)S(1)} %pad_maximum_fusion.6.refs_0_), channel_id=1, source_target_pairs={{0,4},{4,0},{8,12},{12,8},{16,20},{20,16},{24,28},{28,24},{1,5},{5... | collective-permute-start | bytes 1327112 | tf_op jit(solution)/shard_map/ppermute | solution.py:613
  161.1 4.0 %collective-permute-start.28 = (bf16[464,128]{1,0:T(8,128)(2,1)S(1)}, bf16[464,128]{1,0:T(8,128)(2,1)S(1)}, u32[]{:S(2)}, u32[]{:S(2)}) collective-permute-start(bf16[464,128]{1,0:T(8,128)(2,1)S(1)} %fusion.14), channel_id=1, source_target_pairs={{0,16},{4,20},{8,24},{12,28},{16,0},{20,4},{24,8},{28,12},{1,17},{... | collective-permute-start | bytes 356360 | tf_op jit(solution)/shard_map/ppermute | solution.py:613
  165.3 3.5 %collective-permute-done.28 = bf16[464,128]{1,0:T(8,128)(2,1)S(1)} collective-permute-done((bf16[464,128]{1,0:T(8,128)(2,1)S(1)}, bf16[464,128]{1,0:T(8,128)(2,1)S(1)}, u32[]{:S(2)}, u32[]{:S(2)}) %collective-permute-start.28) | collective-permute-done | bytes 118816 | tf_op jit(solution)/shard_map/ppermute | solution.py:613
  168.9 1.9 shard_map.202
  170.8 5.8 %collective-permute-done.26 = bf16[2,256,384]{2,1,0:T(8,128)(2,1)S(1)} collective-permute-done((bf16[2,256,384]{2,1,0:T(8,128)(2,1)S(1)}, bf16[2,256,384]{2,1,0:T(8,128)(2,1)S(1)}, u32[]{:S(2)}, u32[]{:S(2)}) %collective-permute-start.26) | collective-permute-done | bytes 393248 | tf_op jit(solution)/shard_map/ppermute | solution.py:613
  176.8 0.7 collective-permute-start.27
  177.5 1.7 collective-permute-done.29
  179.7 5.7 %collective-permute-done.27 = bf16[256,384]{1,0:T(8,128)(2,1)S(1)} collective-permute-done((bf16[256,384]{1,0:T(8,128)(2,1)S(1)}, bf16[256,384]{1,0:T(8,128)(2,1)S(1)}, u32[]{:S(2)}, u32[]{:S(2)}) %collective-permute-start.27) | collective-permute-done | bytes 196640 | tf_op jit(solution)/shard_map/ppermute | solution.py:613
  185.5 1.4 shard_map.200
  186.9 1.1 collective-permute-done.30.refs_1_
  188.0 2.1 %shard_map.201 = (f32[576,384]{1,0:T(8,128)}, f32[144,576]{1,0:T(8,128)}, f32[144,576]{1,0:T(8,128)}, f32[144,192]{1,0:T(8,128)}, f32[144,192]{1,0:T(8,128)}, /*index=5*/f32[8,144]{1,0:T(8,128)S(1)}) custom-call(s32[2]{0:T(128)S(1)} %copy-done.4, bf16[4,464,128]{2,1,0:T(8,128)(2,1)S(1)} %pad_maximum_fusion.5.refs_0_, ...), custom_call_target="tpu_custom_call" | custom-call | flops 3000000000 | tf_op jit(solution)/shard_map/pallas_call | solution.py:38
  190.1 0.6 fusion.29
  (131 shorter events, 6.0 us)
Async XLA Ops:
  0.6 25.0 %collective-permute-start = (bf16[576,256]{1,0:T(8,128)(2,1)}, bf16[576,256]{1,0:T(8,128)(2,1)}, u32[]{:S(2)}, u32[]{:S(2)}) collective-permute-start(bf16[576,256]{1,0:T(8,128)(2,1)} %bitcast.107), channel_id=1, source_target_pairs={{0,16},{4,20},{8,24},{12,28},{1,17},{5,21},{9,25},{13,29},{2,18},{... | collective-permute-start | bytes 884744 | tf_op jit(solution)/shard_map/ppermute | solution.py:632
  9.3 14.2 %collective-permute-start.2 = (bf16[160,960]{1,0:T(8,128)(2,1)S(1)}, bf16[160,960]{1,0:T(8,128)(2,1)S(1)}, u32[]{:S(2)}, u32[]{:S(2)}) collective-permute-start(bf16[160,960]{1,0:T(8,128)(2,1)S(1)} %fusion.13), channel_id=1, source_target_pairs={{0,2},{1,3},{2,0},{3,1},{4,6},{5,7},{6,4},{7,5},{8,10},{9,11},{10,... | collective-permute-start | bytes 921608 | tf_op jit(solution)/shard_map/ppermute | solution.py:613
  14.6 3.0 %copy-start.2 = (bf16[1,256,576]{1,2,0:T(8,128)(2,1)S(1)}, bf16[1,256,576]{1,2,0:T(8,128)(2,1)}, u32[]{:S(2)}) copy-start(bf16[1,256,576]{1,2,0:T(8,128)(2,1)} %param.11) | copy-start | bytes 884740
  14.6 8.8 %copy-start.19 = (bf16[144,576]{1,0:T(8,128)(2,1)S(1)}, bf16[144,576]{1,0:T(8,128)(2,1)}, u32[]{:S(2)}) copy-start(bf16[144,576]{1,0:T(8,128)(2,1)} %param.13) | copy-start | bytes 497668
  14.6 8.8 %copy-start.24 = (bf16[144,192]{1,0:T(8,128)(2,1)S(1)}, bf16[144,192]{1,0:T(8,128)(2,1)}, u32[]{:S(2)}) copy-start(bf16[144,192]{1,0:T(8,128)(2,1)} %param.15) | copy-start | bytes 165892
  14.6 8.7 %copy-start.25 = (bf16[144,192]{1,0:T(8,128)(2,1)S(1)}, bf16[144,192]{1,0:T(8,128)(2,1)}, u32[]{:S(2)}) copy-start(bf16[144,192]{1,0:T(8,128)(2,1)} %param.14) | copy-start | bytes 165892
  17.6 6.0 %copy-start.22 = (bf16[144,1536]{1,0:T(8,128)(2,1)S(1)}, bf16[144,1536]{1,0:T(8,128)(2,1)}, u32[]{:S(2)}) copy-start(bf16[144,1536]{1,0:T(8,128)(2,1)} %param.18) | copy-start | bytes 1327108
  17.6 6.1 %copy-start.23 = (bf16[144,1536]{1,0:T(8,128)(2,1)S(1)}, bf16[144,1536]{1,0:T(8,128)(2,1)}, u32[]{:S(2)}) copy-start(bf16[144,1536]{1,0:T(8,128)(2,1)} %param.19) | copy-start | bytes 1327108
  17.6 8.5 %collective-permute-start.4 = (bf16[576,256]{1,0:T(8,128)(2,1)S(1)}, bf16[576,256]{1,0:T(8,128)(2,1)}, u32[]{:S(2)}, u32[]{:S(2)}) collective-permute-start(bf16[576,256]{1,0:T(8,128)(2,1)S(1)} %bitcast.110), channel_id=1, source_target_pairs={{0,4},{4,0},{8,12},{12,8},{16,20},{20,16},{24,28},{28,24},{1,5},{5... | collective-permute-start | bytes 884744 | tf_op jit(solution)/shard_map/ppermute | solution.py:613
  19.1 8.9 %collective-permute-start.5 = (bf16[576,256]{1,0:T(8,128)(2,1)S(1)}, bf16[576,256]{1,0:T(8,128)(2,1)}, u32[]{:S(2)}, u32[]{:S(2)}) collective-permute-start(bf16[576,256]{1,0:T(8,128)(2,1)S(1)} %bitcast.111), channel_id=1, source_target_pairs={{0,8},{4,12},{8,16},{12,20},{16,24},{20,28},{1,9},{5,13},{9,17},{1... | collective-permute-start | bytes 884744 | tf_op jit(solution)/shard_map/ppermute | solution.py:632
  23.5 5.5 %copy-start.20 = (bf16[2,160,960]{2,1,0:T(8,128)(2,1)}, bf16[2,160,960]{2,1,0:T(8,128)(2,1)S(1)}, u32[]{:S(2)}) copy-start(bf16[2,160,960]{2,1,0:T(8,128)(2,1)S(1)} %pad_maximum_fusion.2.here_pair) | copy-start | bytes 1843204
  23.6 5.5 %collective-permute-start.3 = (bf16[2,160,960]{2,1,0:T(8,128)(2,1)S(1)}, bf16[2,160,960]{2,1,0:T(8,128)(2,1)}, u32[]{:S(2)}, u32[]{:S(2)}) collective-permute-start(bf16[2,160,960]{2,1,0:T(8,128)(2,1)S(1)} %pad_maximum_fusion.2.here_pair), channel_id=1, source_target_pairs={{0,1},{1,0},{2,3},{3,2},{4,5},{5,4},{6,7},{7,6},{8,9},{9,8},{10,11... | collective-permute-start | bytes 1843208 | tf_op jit(solution)/shard_map/ppermute | solution.py:613
  24.4 26.6 %copy-start.27 = (bf16[144,3648]{1,0:T(8,128)(2,1)}, bf16[144,3648]{1,0:T(8,128)(2,1)S(1)}, u32[]{:S(2)}) copy-start(bf16[144,3648]{1,0:T(8,128)(2,1)S(1)} %constant_dynamic-update-slice_fusion.wi0) | copy-start | bytes 3151876
  24.4 26.6 %collective-permute-start.9 = (bf16[144,3648]{1,0:T(8,128)(2,1)S(1)}, bf16[144,3648]{1,0:T(8,128)(2,1)S(1)}, u32[]{:S(2)}, u32[]{:S(2)}) collective-permute-start(bf16[144,3648]{1,0:T(8,128)(2,1)S(1)} %constant_dynamic-update-slice_fusion.wi0), channel_id=1, source_target_pairs={{0,2},{1,3},{2,0},{3,1},{4,6},{5,7},{6,4},{7,5},{8,10},{9,11},{10,... | collective-permute-start | bytes 3151880 | tf_op jit(solution)/shard_map/ppermute | solution.py:613
  25.6 10.8 %copy-start.16 = (bf16[384,576]{0,1:T(8,128)(2,1)S(1)}, bf16[384,576]{0,1:T(8,128)(2,1)}, u32[]{:S(2)}) copy-start(bf16[384,576]{0,1:T(8,128)(2,1)} %param.20) | copy-start | bytes 1327108
  25.6 12.1 %collective-permute-start.6 = (bf16[576,256]{1,0:T(8,128)(2,1)}, bf16[576,256]{1,0:T(8,128)(2,1)}, u32[]{:S(2)}, u32[]{:S(2)}) collective-permute-start(bf16[576,256]{1,0:T(8,128)(2,1)} %collective-permute-done.refs_2_), channel_id=1, source_target_pairs={{0,4},{4,0},{8,12},{12,8},{16,20},{20,16},{24,28},{28,24},{1,5},{5... | collective-permute-start | bytes 884744 | tf_op jit(solution)/shard_map/ppermute | solution.py:613
  26.1 9.2 %collective-permute-start.1 = (bf16[576,256]{1,0:T(8,128)(2,1)}, bf16[576,256]{1,0:T(8,128)(2,1)}, u32[]{:S(2)}, u32[]{:S(2)}) collective-permute-start(bf16[576,256]{1,0:T(8,128)(2,1)} %collective-permute-done.refs_2_), channel_id=1, source_target_pairs={{16,24},{20,28},{17,25},{21,29},{18,26},{22,30},{19,27},{23,31}} | collective-permute-start | bytes 884744 | tf_op jit(solution)/shard_map/ppermute | solution.py:748
  28.0 14.2 %collective-permute-start.7 = (bf16[576,256]{1,0:T(8,128)(2,1)}, bf16[576,256]{1,0:T(8,128)(2,1)}, u32[]{:S(2)}, u32[]{:S(2)}) collective-permute-start(bf16[576,256]{1,0:T(8,128)(2,1)} %collective-permute-done.5.refs_0_), channel_id=1, source_target_pairs={{0,4},{4,0},{8,12},{12,8},{16,20},{20,16},{24,28},{28,24},{1,5},{5... | collective-permute-start | bytes 884744 | tf_op jit(solution)/shard_map/ppermute | solution.py:613
  35.3 15.6 %collective-permute-start.8 = (bf16[576,256]{1,0:T(8,128)(2,1)}, bf16[576,256]{1,0:T(8,128)(2,1)S(1)}, u32[]{:S(2)}, u32[]{:S(2)}) collective-permute-start(bf16[576,256]{1,0:T(8,128)(2,1)} %collective-permute-done.1.refs_3_), channel_id=1, source_target_pairs={{0,4},{4,0},{8,12},{12,8},{16,20},{20,16},{24,28},{28,24},{1,5},{5... | collective-permute-start | bytes 884744 | tf_op jit(solution)/shard_map/ppermute | solution.py:613
  36.7 23.8 %collective-permute-start.10 = (bf16[384,576]{1,0:T(8,128)(2,1)S(1)}, bf16[384,576]{1,0:T(8,128)(2,1)}, u32[]{:S(2)}, u32[]{:S(2)}) collective-permute-start(bf16[384,576]{1,0:T(8,128)(2,1)S(1)} %copy.26), channel_id=1, source_target_pairs={{0,2},{1,3},{2,0},{3,1},{4,6},{5,7},{6,4},{7,5},{8,10},{9,11},{10,... | collective-permute-start | bytes 1327112 | tf_op jit(solution)/shard_map/ppermute | solution.py:613
  51.0 8.2 %copy-start.28 = (bf16[144,3648]{1,0:T(8,128)(2,1)}, bf16[144,3648]{1,0:T(8,128)(2,1)S(1)}, u32[]{:S(2)}) copy-start(bf16[144,3648]{1,0:T(8,128)(2,1)S(1)} %collective-permute-done.9.wi2) | copy-start | bytes 3151876
  51.0 12.1 %collective-permute-start.11 = (bf16[144,3648]{1,0:T(8,128)(2,1)S(1)}, bf16[144,3648]{1,0:T(8,128)(2,1)}, u32[]{:S(2)}, u32[]{:S(2)}) collective-permute-start(bf16[144,3648]{1,0:T(8,128)(2,1)S(1)} %constant_dynamic-update-slice_fusion.wi0), channel_id=1, source_target_pairs={{0,1},{1,0},{2,3},{3,2},{4,5},{5,4},{6,7},{7,6},{8,9},{9,8},{10,11... | collective-permute-start | bytes 3151880 | tf_op jit(solution)/shard_map/ppermute | solution.py:613
  51.1 12.0 %collective-permute-start.12 = (bf16[144,3648]{1,0:T(8,128)(2,1)S(1)}, bf16[144,3648]{1,0:T(8,128)(2,1)}, u32[]{:S(2)}, u32[]{:S(2)}) collective-permute-start(bf16[144,3648]{1,0:T(8,128)(2,1)S(1)} %collective-permute-done.9.wi2), channel_id=1, source_target_pairs={{0,1},{1,0},{2,3},{3,2},{4,5},{5,4},{6,7},{7,6},{8,9},{9,8},{10,11... | collective-permute-start | bytes 3151880 | tf_op jit(solution)/shard_map/ppermute | solution.py:613
  60.5 2.2 %collective-permute-start.14 = (bf16[384,576]{1,0:T(8,128)(2,1)}, bf16[384,576]{1,0:T(8,128)(2,1)}, u32[]{:S(2)}, u32[]{:S(2)}) collective-permute-start(bf16[384,576]{1,0:T(8,128)(2,1)} %collective-permute-done.10.wd2), channel_id=1, source_target_pairs={{0,1},{1,0},{2,3},{3,2},{4,5},{5,4},{6,7},{7,6},{8,9},{9,8},{10,11... | collective-permute-start | bytes 1327112 | tf_op jit(solution)/shard_map/ppermute | solution.py:613
  60.8 2.3 %copy-start.21 = (bf16[384,576]{1,0:T(8,128)(2,1)}, bf16[384,576]{1,0:T(8,128)(2,1)S(1)}, u32[]{:S(2)}) copy-start(bf16[384,576]{1,0:T(8,128)(2,1)S(1)} %copy.28.wd0) | copy-start | bytes 1327108
  60.8 2.3 %collective-permute-start.13 = (bf16[384,576]{1,0:T(8,128)(2,1)S(1)}, bf16[384,576]{1,0:T(8,128)(2,1)S(1)}, u32[]{:S(2)}, u32[]{:S(2)}) collective-permute-start(bf16[384,576]{1,0:T(8,128)(2,1)S(1)} %copy.28.wd0), channel_id=1, source_target_pairs={{0,1},{1,0},{2,3},{3,2},{4,5},{5,4},{6,7},{7,6},{8,9},{9,8},{10,11... | collective-permute-start | bytes 1327112 | tf_op jit(solution)/shard_map/ppermute | solution.py:613
  78.3 3.2 %collective-permute-start.16 = (bf16[2,2560,128]{2,1,0:T(8,128)(2,1)}, bf16[2,2560,128]{2,1,0:T(8,128)(2,1)S(1)}, u32[]{:S(2)}, u32[]{:S(2)}) collective-permute-start(bf16[2,2560,128]{2,1,0:T(8,128)(2,1)} %get-tuple-element.103), channel_id=1, source_target_pairs={{0,1},{1,0},{2,3},{3,2},{4,5},{5,4},{6,7},{7,6},{8,9},{9,8},{10,11... | collective-permute-start | bytes 3932168 | tf_op jit(solution)/shard_map/ppermute | solution.py:613
  78.4 5.6 %collective-permute-start.15 = (bf16[2,3456,128]{2,1,0:T(8,128)(2,1)}, bf16[2,3456,128]{2,1,0:T(8,128)(2,1)S(1)}, u32[]{:S(2)}, u32[]{:S(2)}) collective-permute-start(bf16[2,3456,128]{2,1,0:T(8,128)(2,1)} %get-tuple-element.101), channel_id=1, source_target_pairs={{0,1},{1,0},{2,3},{3,2},{4,5},{5,4},{6,7},{7,6},{8,9},{9,8},{10,11... | collective-permute-start | bytes 5308424 | tf_op jit(solution)/shard_map/ppermute | solution.py:613
  81.5 2.5 %copy-start.18 = (bf16[3456,128]{1,0:T(8,128)(2,1)S(1)}, bf16[3456,128]{1,0:T(8,128)(2,1)}, u32[]{:S(2)}) copy-start(bf16[3456,128]{1,0:T(8,128)(2,1)} %get-tuple-element.100) | copy-start | bytes 2654212
  81.5 4.5 %copy-start.9 = (bf16[2048,576]{1,0:T(8,128)(2,1)S(1)}, bf16[2048,576]{1,0:T(8,128)(2,1)}, u32[]{:S(2)}) copy-start(bf16[2048,576]{1,0:T(8,128)(2,1)} %get-tuple-element.107.normed) | copy-start | bytes 7077892
  81.5 4.5 %copy-start.13 = (bf16[256,576]{1,0:T(8,128)(2,1)S(1)}, bf16[256,576]{1,0:T(8,128)(2,1)}, u32[]{:S(2)}) copy-start(bf16[256,576]{1,0:T(8,128)(2,1)} %get-tuple-element.105.attended_grad) | copy-start | bytes 884740
  83.3 2.7 %copy-start.11 = (f32[256,576]{1,0:T(8,128)S(1)}, f32[256,576]{1,0:T(8,128)}, u32[]{:S(2)}) copy-start(f32[256,576]{1,0:T(8,128)} %get-tuple-element.92.attended) | copy-start | bytes 1769476
  83.4 2.7 %copy-start.7 = (bf16[576,576]{1,0:T(8,128)(2,1)S(1)}, bf16[576,576]{1,0:T(8,128)(2,1)}, u32[]{:S(2)}) copy-start(bf16[576,576]{1,0:T(8,128)(2,1)} %get-tuple-element.108.query_weight) | copy-start | bytes 1990660
  83.4 2.7 %copy-start.8 = (bf16[256,576]{1,0:T(8,128)(2,1)S(1)}, bf16[256,576]{1,0:T(8,128)(2,1)}, u32[]{:S(2)}) copy-start(bf16[256,576]{1,0:T(8,128)(2,1)} %get-tuple-element.80.queries) | copy-start | bytes 884740
  83.4 2.7 %copy-start.10 = (bf16[2048,384]{1,0:T(8,128)(2,1)S(1)}, bf16[2048,384]{1,0:T(8,128)(2,1)}, u32[]{:S(2)}) copy-start(bf16[2048,384]{1,0:T(8,128)(2,1)} %get-tuple-element.98.kv_all) | copy-start | bytes 4718596
  84.1 2.0 %copy-start = (f32[2048,128]{1,0:T(8,128)S(1)}, f32[2048,128]{1,0:T(8,128)}, u32[]{:S(2)}) copy-start(f32[2048,128]{1,0:T(8,128)} %get-tuple-element.76.cosine) | copy-start | bytes 3145732
  84.1 2.0 %copy-start.1 = (f32[2048,128]{1,0:T(8,128)S(1)}, f32[2048,128]{1,0:T(8,128)}, u32[]{:S(2)}) copy-start(f32[2048,128]{1,0:T(8,128)} %get-tuple-element.77.sine) | copy-start | bytes 3145732
  84.1 2.0 %copy-start.4 = (s32[2]{0:T(128)S(1)}, s32[2]{0:T(128)}, u32[]{:S(2)}) copy-start(s32[2]{0:T(128)} %pad_add_fusion.index) | copy-start | bytes 28
  84.1 2.0 %copy-start.5 = (bf16[576,384]{1,0:T(8,128)(2,1)S(1)}, bf16[576,384]{1,0:T(8,128)(2,1)}, u32[]{:S(2)}) copy-start(bf16[576,384]{1,0:T(8,128)(2,1)} %get-tuple-element.83.kv_weight) | copy-start | bytes 1327108
  84.1 2.0 %copy-start.12 = (f32[8,576]{1,0:T(8,128)S(1)}, f32[8,576]{1,0:T(8,128)}, u32[]{:S(2)}) copy-start(f32[8,576]{1,0:T(8,128)} %get-tuple-element.84.gains) | copy-start | bytes 55300
  84.1 2.0 %copy-start.14 = (f32[8,576]{1,0:T(8,128)S(1)}, f32[8,576]{1,0:T(8,128)}, u32[]{:S(2)}) copy-start(f32[8,576]{1,0:T(8,128)} %get-tuple-element.109.ffn_gain_grad) | copy-start | bytes 55300
  84.1 2.0 %copy-start.15 = (f32[8,768]{1,0:T(8,128)S(1)}, f32[8,768]{1,0:T(8,128)}, u32[]{:S(2)}) copy-start(f32[8,768]{1,0:T(8,128)} %get-tuple-element.106.lse) | copy-start | bytes 73732
  84.4 21.8 %collective-permute-start.17 = (bf16[3456,128]{1,0:T(8,128)(2,1)S(1)}, bf16[3456,128]{1,0:T(8,128)(2,1)S(1)}, u32[]{:S(2)}, u32[]{:S(2)}) collective-permute-start(bf16[3456,128]{1,0:T(8,128)(2,1)S(1)} %fusion), channel_id=1, source_target_pairs={{0,2},{1,3},{2,0},{3,1},{4,6},{5,7},{6,4},{7,5},{8,10},{9,11},{10,... | collective-permute-start | bytes 2654216 | tf_op jit(solution)/shard_map/ppermute | solution.py:613
  85.0 16.5 %collective-permute-start.18 = (bf16[2,4,320,128]{3,2,1,0:T(8,128)(2,1)S(1)}, bf16[2,4,320,128]{3,2,1,0:T(8,128)(2,1)S(1)}, u32[]{:S(2)}, u32[]{:S(2)}) collective-permute-start(bf16[2,4,320,128]{3,2,1,0:T(8,128)(2,1)S(1)} %pad_maximum_fusion.3), channel_id=1, source_target_pairs={{0,4},{4,0},{8,12},{12,8},{16,20},{20,16},{24,28},{28,24},{1,5},{5... | collective-permute-start | bytes 1966088 | tf_op jit(solution)/shard_map/ppermute | solution.py:613
  106.1 2.0 %collective-permute-start.20 = (bf16[2,1152,128]{2,1,0:T(8,128)(2,1)S(1)}, bf16[2,1152,128]{2,1,0:T(8,128)(2,1)S(1)}, u32[]{:S(2)}, u32[]{:S(2)}) collective-permute-start(bf16[2,1152,128]{2,1,0:T(8,128)(2,1)S(1)} %get-tuple-element.123), channel_id=1, source_target_pairs={{0,1},{1,0},{2,3},{3,2},{4,5},{5,4},{6,7},{7,6},{8,9},{9,8},{10,11... | collective-permute-start | bytes 1769480 | tf_op jit(solution)/shard_map/ppermute | solution.py:613
  106.8 2.1 %copy-start.17 = (bf16[3456,128]{1,0:T(8,128)(2,1)S(1)}, bf16[3456,128]{1,0:T(8,128)(2,1)}, u32[]{:S(2)}) copy-start(bf16[3456,128]{1,0:T(8,128)(2,1)} %get-tuple-element.120) | copy-start | bytes 2654212
  108.3 16.1 %collective-permute-start.21 = (bf16[2432,128]{1,0:T(8,128)(2,1)S(1)}, bf16[2432,128]{1,0:T(8,128)(2,1)S(1)}, u32[]{:S(2)}, u32[]{:S(2)}) collective-permute-start(bf16[2432,128]{1,0:T(8,128)(2,1)S(1)} %pad_maximum_fusion.4), channel_id=1, source_target_pairs={{0,2},{1,3},{2,0},{3,1},{4,6},{5,7},{6,4},{7,5},{8,10},{9,11},{10,... | collective-permute-start | bytes 1867784 | tf_op jit(solution)/shard_map/ppermute | solution.py:613
  109.2 12.0 %collective-permute-start.19 = (bf16[4,432,128]{2,1,0:T(8,128)(2,1)S(1)}, bf16[4,432,128]{2,1,0:T(8,128)(2,1)S(1)}, u32[]{:S(2)}, u32[]{:S(2)}) collective-permute-start(bf16[4,432,128]{2,1,0:T(8,128)(2,1)S(1)} %bitcast.125), channel_id=1, source_target_pairs={{0,4},{4,0},{8,12},{12,8},{16,20},{20,16},{24,28},{28,24},{1,5},{5... | collective-permute-start | bytes 1327112 | tf_op jit(solution)/shard_map/ppermute | solution.py:613
  124.6 10.1 %collective-permute-start.31 = (bf16[2,432,128]{2,1,0:T(8,128)(2,1)S(1)}, bf16[2,432,128]{2,1,0:T(8,128)(2,1)S(1)}, u32[]{:S(2)}, u32[]{:S(2)}) collective-permute-start(bf16[2,432,128]{2,1,0:T(8,128)(2,1)S(1)} %pad_maximum_fusion.10), channel_id=1, source_target_pairs={{0,8},{4,12},{8,0},{12,4},{16,24},{20,28},{24,16},{28,20},{1,9},{5... | collective-permute-start | bytes 663560 | tf_op jit(solution)/shard_map/ppermute | solution.py:613
  127.5 7.1 %collective-permute-start.22 = (bf16[4,144,128]{2,1,0:T(8,128)(2,1)S(1)}, bf16[4,144,128]{2,1,0:T(8,128)(2,1)S(1)}, u32[]{:S(2)}, u32[]{:S(2)}) collective-permute-start(bf16[4,144,128]{2,1,0:T(8,128)(2,1)S(1)} %get-tuple-element.128), channel_id=1, source_target_pairs={{0,4},{4,0},{8,12},{12,8},{16,20},{20,16},{24,28},{28,24},{1,5},{5... | collective-permute-start | bytes 442376 | tf_op jit(solution)/shard_map/ppermute | solution.py:613
  129.9 31.2 %collective-permute-start.25 = (bf16[4,256,384]{2,1,0:T(8,128)(2,1)S(1)}, bf16[4,256,384]{2,1,0:T(8,128)(2,1)S(1)}, u32[]{:S(2)}, u32[]{:S(2)}) collective-permute-start(bf16[4,256,384]{2,1,0:T(8,128)(2,1)S(1)} %slice.195), channel_id=1, source_target_pairs={{0,4},{4,0},{8,12},{12,8},{16,20},{20,16},{24,28},{28,24},{1,5},{5... | collective-permute-start | bytes 2359304 | tf_op jit(solution)/shard_map/ppermute | solution.py:613
  134.7 11.0 %collective-permute-start.32 = (bf16[432,128]{1,0:T(8,128)(2,1)S(1)}, bf16[432,128]{1,0:T(8,128)(2,1)S(1)}, u32[]{:S(2)}, u32[]{:S(2)}) collective-permute-start(bf16[432,128]{1,0:T(8,128)(2,1)S(1)} %fusion.15), channel_id=1, source_target_pairs={{0,16},{4,20},{8,24},{12,28},{16,0},{20,4},{24,8},{28,12},{1,17},{... | collective-permute-start | bytes 331784 | tf_op jit(solution)/shard_map/ppermute | solution.py:613
  141.6 8.0 %collective-permute-start.23 = (bf16[2,464,128]{2,1,0:T(8,128)(2,1)S(1)}, bf16[2,464,128]{2,1,0:T(8,128)(2,1)S(1)}, u32[]{:S(2)}, u32[]{:S(2)}) collective-permute-start(bf16[2,464,128]{2,1,0:T(8,128)(2,1)S(1)} %pad_maximum_fusion.8), channel_id=1, source_target_pairs={{0,8},{4,12},{8,0},{12,4},{16,24},{20,28},{24,16},{28,20},{1,9},{5... | collective-permute-start | bytes 712712 | tf_op jit(solution)/shard_map/ppermute | solution.py:613
  145.8 7.2 %collective-permute-start.33 = (bf16[432,128]{1,0:T(8,128)(2,1)S(1)}, bf16[432,128]{1,0:T(8,128)(2,1)S(1)}, u32[]{:S(2)}, u32[]{:S(2)}) collective-permute-start(bf16[432,128]{1,0:T(8,128)(2,1)S(1)} %fusion.17), channel_id=1, source_target_pairs={{0,16},{4,20},{8,24},{12,28},{16,0},{20,4},{24,8},{28,12},{1,17},{... | collective-permute-start | bytes 331784 | tf_op jit(solution)/shard_map/ppermute | solution.py:613
  149.6 5.9 %collective-permute-start.24 = (bf16[464,128]{1,0:T(8,128)(2,1)S(1)}, bf16[464,128]{1,0:T(8,128)(2,1)S(1)}, u32[]{:S(2)}, u32[]{:S(2)}) collective-permute-start(bf16[464,128]{1,0:T(8,128)(2,1)S(1)} %fusion.21), channel_id=1, source_target_pairs={{0,16},{4,20},{8,24},{12,28},{16,0},{20,4},{24,8},{28,12},{1,17},{... | collective-permute-start | bytes 356360 | tf_op jit(solution)/shard_map/ppermute | solution.py:613
  153.0 6.0 %collective-permute-start.34 = (bf16[2,432,128]{2,1,0:T(8,128)(2,1)S(1)}, bf16[2,432,128]{2,1,0:T(8,128)(2,1)S(1)}, u32[]{:S(2)}, u32[]{:S(2)}) collective-permute-start(bf16[2,432,128]{2,1,0:T(8,128)(2,1)S(1)} %pad_maximum_fusion.11), channel_id=1, source_target_pairs={{0,8},{4,12},{8,0},{12,4},{16,24},{20,28},{24,16},{28,20},{1,9},{5... | collective-permute-start | bytes 663560 | tf_op jit(solution)/shard_map/ppermute | solution.py:613
  159.1 9.8 %collective-permute-start.35 = (bf16[4,432,128]{2,1,0:T(8,128)(2,1)S(1)}, bf16[4,432,128]{2,1,0:T(8,128)(2,1)S(1)}, u32[]{:S(2)}, u32[]{:S(2)}) collective-permute-start(bf16[4,432,128]{2,1,0:T(8,128)(2,1)S(1)} %pad_maximum_fusion.6.refs_0_), channel_id=1, source_target_pairs={{0,4},{4,0},{8,12},{12,8},{16,20},{20,16},{24,28},{28,24},{1,5},{5... | collective-permute-start | bytes 1327112 | tf_op jit(solution)/shard_map/ppermute | solution.py:613
  161.1 7.7 %collective-permute-start.28 = (bf16[464,128]{1,0:T(8,128)(2,1)S(1)}, bf16[464,128]{1,0:T(8,128)(2,1)S(1)}, u32[]{:S(2)}, u32[]{:S(2)}) collective-permute-start(bf16[464,128]{1,0:T(8,128)(2,1)S(1)} %fusion.14), channel_id=1, source_target_pairs={{0,16},{4,20},{8,24},{12,28},{16,0},{20,4},{24,8},{28,12},{1,17},{... | collective-permute-start | bytes 356360 | tf_op jit(solution)/shard_map/ppermute | solution.py:613
  165.3 11.4 %collective-permute-start.26 = (bf16[2,256,384]{2,1,0:T(8,128)(2,1)S(1)}, bf16[2,256,384]{2,1,0:T(8,128)(2,1)S(1)}, u32[]{:S(2)}, u32[]{:S(2)}) collective-permute-start(bf16[2,256,384]{2,1,0:T(8,128)(2,1)S(1)} %pad_maximum_fusion.7), channel_id=1, source_target_pairs={{0,8},{4,12},{8,0},{12,4},{16,24},{20,28},{24,16},{28,20},{1,9},{5... | collective-permute-start | bytes 1179656 | tf_op jit(solution)/shard_map/ppermute | solution.py:613
  168.8 10.4 %collective-permute-start.29 = (bf16[2,464,128]{2,1,0:T(8,128)(2,1)S(1)}, bf16[2,464,128]{2,1,0:T(8,128)(2,1)S(1)}, u32[]{:S(2)}, u32[]{:S(2)}) collective-permute-start(bf16[2,464,128]{2,1,0:T(8,128)(2,1)S(1)} %pad_maximum_fusion.9), channel_id=1, source_target_pairs={{0,8},{4,12},{8,0},{12,4},{16,24},{20,28},{24,16},{28,20},{1,9},{5... | collective-permute-start | bytes 712712 | tf_op jit(solution)/shard_map/ppermute | solution.py:613
  176.7 8.8 %copy-start.3 = (bf16[1,256,576]{1,2,0:T(8,128)(2,1)S(1)}, bf16[1,256,576]{1,2,0:T(8,128)(2,1)}, u32[]{:S(2)}) copy-start(bf16[1,256,576]{1,2,0:T(8,128)(2,1)} %param.11) | copy-start | bytes 884740
  176.7 8.8 %copy-start.6 = (f32[256,576]{1,0:T(8,128)S(1)}, f32[256,576]{1,0:T(8,128)}, u32[]{:S(2)}) copy-start(f32[256,576]{1,0:T(8,128)} %get-tuple-element.111.middle_grad) | copy-start | bytes 1769476
  176.8 8.6 %collective-permute-start.27 = (bf16[256,384]{1,0:T(8,128)(2,1)S(1)}, bf16[256,384]{1,0:T(8,128)(2,1)S(1)}, u32[]{:S(2)}, u32[]{:S(2)}) collective-permute-start(bf16[256,384]{1,0:T(8,128)(2,1)S(1)} %fusion.20), channel_id=1, source_target_pairs={{0,16},{4,20},{8,24},{12,28},{16,0},{20,4},{24,8},{28,12},{1,17},{... | collective-permute-start | bytes 589832 | tf_op jit(solution)/shard_map/ppermute | solution.py:613
  179.3 8.7 %collective-permute-start.30 = (bf16[4,464,128]{2,1,0:T(8,128)(2,1)S(1)}, bf16[4,464,128]{2,1,0:T(8,128)(2,1)S(1)}, u32[]{:S(2)}, u32[]{:S(2)}) collective-permute-start(bf16[4,464,128]{2,1,0:T(8,128)(2,1)S(1)} %pad_maximum_fusion.5.refs_0_), channel_id=1, source_target_pairs={{0,4},{4,0},{8,12},{12,8},{16,20},{20,16},{24,28},{28,24},{1,5},{5... | collective-permute-start | bytes 1425416 | tf_op jit(solution)/shard_map/ppermute | solution.py:613
  (3 other events, 2.5 us)

commit v3 on v2

--- a/solution.py
+++ b/solution.py
@@ -882,12 +882,13 @@
         half = second_count // 2
 
         def halves(value):
-            return value[:half].reshape(ctx_count // 2, second_rows, LANES), value[half:]
-
-        keep_mine, mine_to_mate = halves(added(mine, got[0]))
-        keep_along, along_to_mate = halves(added(along, got[1]))
-        to_mate = jnp.stack([mine_to_mate, along_to_mate])
-        to_mate = to_mate.reshape(2, ctx_count // 2, second_rows, LANES)
+            shape = (ctx_count // 2, second_rows, LANES)
+            return value[:half].reshape(shape), value[half:].reshape(shape)
+
+        keep, to_mate = (
+            jnp.concatenate(both, 1)
+            for both in zip(halves(added(mine, got[0])), halves(added(along, got[1])))
+        )
     else:
         to_mate = added(along, got[1])
     attended_grad, in_crossing, to_mate = lax.optimization_barrier(
@@ -949,33 +950,23 @@
             added(in_mine[at], in_got[0, at], in_crossed[at]).reshape(-1, first_rows, LANES)
             for at in (slice(first_count // 2), slice(first_count // 2, None))
         )
+        small_crossing = added(small_along, small_got[1])
+        in_to_mate, small_crossing, from_mate = lax.optimization_barrier(
+            (in_to_mate, small_crossing, from_mate)
+        )
         in_from_mate = swap(in_to_mate, "ctx", 0)
-        more_rows = keep_along.shape[0] * second_rows
-        crossing = jnp.concatenate(
-            [
-                added(keep_along, from_mate[1]).reshape(more_rows, LANES),
-                added(small_along, small_got[1]),
-            ],
-            0,
-        )
-        crossed = swap(crossing, "ws", 1)
-        in_from_mate, crossed = lax.optimization_barrier((in_from_mate, crossed))
-        small_keep, small_to_mate = spread(
-            index, (small_mine, small_got[0], crossed[more_rows:])
-        )
-        crossed = crossed[:more_rows].reshape(keep_mine.shape)
-        small_to_mate, kv_to_mate = lax.optimization_barrier(
-            (small_to_mate, kv_grads[ctx_count // 2 :])
+        small_crossed = swap(small_crossing, "ws", 1)
+        share = summed_column((keep, from_mate))
+        in_from_mate, small_crossed = lax.optimization_barrier((in_from_mate, small_crossed))
+        small_keep, small_to_mate = spread(index, (small_mine, small_got[0], small_crossed))
+        small_to_mate, kv_to_mate, share = lax.optimization_barrier(
+            (small_to_mate, kv_grads[ctx_count // 2 :], share)
         )
         small_from_mate = swap(small_to_mate, "ctx", 0)
         kv_from_mate = swap(kv_to_mate, "ctx", 0)
         in_share = summed_column((in_keep, in_from_mate))
-        share = summed_column(
-            (
-                jnp.concatenate([added(keep_mine, from_mate[0], crossed), small_keep], 1),
-                jnp.concatenate([jnp.zeros_like(keep_mine), small_from_mate], 1),
-            )
-        )
+        share = added(share[:second_rows], swap(share[second_rows:], "ws", 1))
+        share = jnp.concatenate([share, summed_column((small_keep, small_from_mate))], 0)
         share, kv_from_mate = lax.optimization_barrier((share, kv_from_mate))
         in_column = column_of(in_share)
         in_pieces = (in_column, swap(in_column, "ctx", 0))

time: 191 us -> 194 us (1.016)
  starting transfers between devices: 46.2 us -> 60.1 us
  waiting for transfers between devices: 82.2 us -> 71.4 us
    ppermute x33 -> x36, starting transfers between devices: 33.9 us -> 47.9 us  [swap(): return lax.ppermute(value, axis, [(i, i ^ 1 << bit) for i in range(count)])]
    ppermute x33 -> x36, waiting for transfers between devices: 81.7 us -> 71 us  [swap(): return lax.ppermute(value, axis, [(i, i ^ 1 << bit) for i in range(count)])]
  transfers between devices with their start and end apart: 36 -> 39, of which waited for: 24 -> 24; matrix products, arithmetic and copies ran while one was open for 7% -> 7% of each run, Pallas kernels for 14% -> 14%
where the time goes in v3:
time: 194 us
  waiting for transfers between devices  71.4 us (37%)
  starting transfers between devices  60.1 us (31%)
  Pallas kernels  43.8 us (23%)
  other arithmetic  13.8 us (7%)
  local copies, waits for them, and re-layouts  3.44 us (2%)
    ppermute x36, waiting for transfers between devices, swap(): return lax.ppermute(value, axis, [(i, i ^ 1 << bit) for i in range(count)])  71 us
    ppermute x36, starting transfers between devices, swap(): return lax.ppermute(value, axis, [(i, i ^ 1 << bit) for i in range(count)])  47.9 us
    pallas_call x9, Pallas kernels, call(): pl.pallas_call(kernel, out_shape=outs, in_specs=[SMEM_SPEC] * smem + [VME...  43.8 us
    ppermute x2, starting transfers between devices, shifted(): return lax.ppermute(value, 'ctx', [(i, j % count) for i, j in pairs])  10.9 us
    neg x2, other arithmetic, wide_tables(): -sine  4.26 us
  transfers between devices with their start and end apart: 39, of which 24 were waited for; matrix products, arithmetic and copies ran while one was open for 7% of the time, Pallas kernels for 14%

profile of v3, /device:TPU:0, one launch (start us, length us, event | category | flops | bytes accessed | tf_op | source)
XLA Modules:
  0.0 193.9 jit_solution(6438570758898312470)
XLA Ops:
  0.6 6.7 %collective-permute-start = (bf16[576,256]{1,0:T(8,128)(2,1)}, bf16[576,256]{1,0:T(8,128)(2,1)}, u32[]{:S(2)}, u32[]{:S(2)}) collective-permute-start(bf16[576,256]{1,0:T(8,128)(2,1)} %bitcast.105), channel_id=1, source_target_pairs={{0,16},{4,20},{8,24},{12,28},{1,17},{5,21},{9,25},{13,29},{2,18},{... | collective-permute-start | bytes 884744 | tf_op jit(solution)/shard_map/ppermute | solution.py:632
  7.3 0.7 pad_maximum_fusion.16
  8.1 1.1 fusion.11
  9.3 1.6 collective-permute-start.2
  10.8 3.7 %fusion.10 = (f32[2048,32]{1,0:T(8,128)S(1)}, f32[2048,32]{1,0:T(8,128)S(1)}, f32[2048,32]{1,0:T(8,128)S(1)}) fusion(f32[32]{0:T(128)S(1)} %multiply_exponential_fusion, f32[2048]{0:T(1024)S(1)} %iota_convert_fusion), kind=kLoop, calls=%fused_computation.41 | loop fusion | flops 131072 | bytes 794752 | tf_op jit(solution)/shard_map/neg | solution.py:738
  14.6 3.0 %pad_maximum_fusion = (f32[2048,128]{1,0:T(8,128)}, f32[2048,128]{1,0:T(8,128)}) fusion(f32[2048,32]{1,0:T(8,128)S(1)} %get-tuple-element.171, f32[2048,32]{1,0:T(8,128)S(1)} %get-tuple-element.170, f32[2048,32]{1,0:T(8,128)S(1)} %get-tuple-element.169), kind=kLoop, calls=%fused_computation.8 | loop fusion | flops 1572864 | bytes 2883584 | tf_op jit(solution)/shard_map/concatenate | solution.py:738
  17.6 1.5 collective-permute-start.4
  19.1 4.2 %collective-permute-start.5 = (bf16[576,256]{1,0:T(8,128)(2,1)S(1)}, bf16[576,256]{1,0:T(8,128)(2,1)}, u32[]{:S(2)}, u32[]{:S(2)}) collective-permute-start(bf16[576,256]{1,0:T(8,128)(2,1)S(1)} %bitcast.109), channel_id=1, source_target_pairs={{0,8},{4,12},{8,16},{12,20},{16,24},{20,28},{1,9},{5,13},{9,17},{1... | collective-permute-start | bytes 884744 | tf_op jit(solution)/shard_map/ppermute | solution.py:632
  23.7 0.7 copy-done.26
  24.4 0.6 collective-permute-start.9
  25.0 0.7 pad_add_fusion.index
  26.2 1.4 collective-permute-start.1
  28.0 1.1 collective-permute-start.7
  29.1 6.3 %shard_map.194 = (bf16[3,256,576]{2,1,0:T(8,128)(2,1)}, bf16[3,256,384]{2,1,0:T(8,128)(2,1)}, bf16[256,576]{1,0:T(8,128)(2,1)}, bf16[576,576]{1,0:T(8,128)(2,1)}...) custom-call(s32[2]{0:T(128)} %pad_add_fusion.index, bf16[2,160,960]{2,1,0:T(8,128)(2,1)} %copy-done.20, ...), custom_call_target="tpu_custom_call" | custom-call | flops 6000000000 | tf_op jit(solution)/shard_map/pallas_call | solution.py:38
  35.4 1.0 collective-permute-start.8
  36.7 1.1 collective-permute-start.10
  37.8 3.7 %shard_map.195 = (bf16[2,256,576]{2,1,0:T(8,128)(2,1)}, bf16[2,256,384]{2,1,0:T(8,128)(2,1)}) custom-call(s32[2]{0:T(128)} %pad_add_fusion.index, bf16[576,384]{1,0:T(8,128)(2,1)} %get-tuple-element.87.kv_weight, f32[8,576]{1,0:T(8,128)} %get-tuple-element.88.gains, f32[2048,128]{1,0:T(8,128)} %get-tuple-element.80.cosine, ...), custom_call_target="tpu_custom_call" | custom-call | flops 3000000000 | tf_op jit(solution)/shard_map/pallas_call | solution.py:38
  41.5 0.8 collective-permute-done.7.refs_2_
  42.3 8.7 %collective-permute-done.9.wi2 = bf16[144,3648]{1,0:T(8,128)(2,1)S(1)} collective-permute-done((bf16[144,3648]{1,0:T(8,128)(2,1)S(1)}, bf16[144,3648]{1,0:T(8,128)(2,1)S(1)}, u32[]{:S(2)}, u32[]{:S(2)}) %collective-permute-start.9) | collective-permute-done | bytes 1050656 | tf_op jit(solution)/shard_map/ppermute | solution.py:613
  51.7 7.5 %shard_map.196 = (f32[256,576]{1,0:T(8,128)}, f32[8,768]{1,0:T(8,128)}, bf16[2048,384]{1,0:T(8,128)(2,1)}, bf16[2048,576]{1,0:T(8,128)(2,1)}) custom-call(s32[2]{0:T(128)} %pad_add_fusion.index, bf16[256,576]{1,0:T(8,128)(2,1)} %get-tuple-element.84.queries, bf16[3,256,576]{2,1,0:T(8,128)(2,1)} %get-tuple-element.85.early_normed, ...), custom_call_target="tpu_custom_call" | custom-call | flops 20000000000 | tf_op jit(solution)/shard_map/pallas_call | solution.py:38
  59.2 1.3 collective-permute-done.10.wd2
  60.8 0.6 collective-permute-start.13
  61.3 1.4 collective-permute-done.14.wd3
  63.1 0.8 copy-done.29
  63.8 14.5 %shard_map.197 = (bf16[576,256]{1,0:T(8,128)(2,1)}, f32[256,576]{1,0:T(8,128)}, bf16[256,576]{1,0:T(8,128)(2,1)}, f32[8,576]{1,0:T(8,128)}, bf16[3456,128]{1,0:T...) custom-call(s32[2]{0:T(128)} %pad_add_fusion.index, ...), custom_call_target="tpu_custom_call" | custom-call | flops 14000000000 | tf_op jit(solution)/shard_map/pallas_call | solution.py:38
  79.4 2.1 %collective-permute-done.16 = bf16[2,2560,128]{2,1,0:T(8,128)(2,1)S(1)} collective-permute-done((bf16[2,2560,128]{2,1,0:T(8,128)(2,1)}, bf16[2,2560,128]{2,1,0:T(8,128)(2,1)S(1)}, u32[]{:S(2)}, u32[]{:S(2)}) %collective-permute-start.16) | collective-permute-done | bytes 1310752 | tf_op jit(solution)/shard_map/ppermute | solution.py:613
  81.5 1.8 fusion.2
  84.3 0.6 collective-permute-start.17
  84.9 1.1 collective-permute-start.18
  86.3 5.8 %shard_map.198 = (bf16[8,256,384]{2,1,0:T(8,128)(2,1)S(1)}, f32[256,576]{1,0:T(8,128)S(1)}, bf16[1152,128]{1,0:T(8,128)(2,1)S(1)}, bf16[1152,128]{1,0:T(8,128)(2,1)S(1)}, bf16[2,1152,128]{2,1,0:T(8,128)(2,1)S(1)}) custom-call(s32[2]{0:T(128)S(1)} %copy-done.4, bf16[256,576]{1,0:T(8,128)(2,1)S(1)} %copy-done.8, bf16[2048,384]{1,0:T(8,128)(2,1)S(1)} %copy-done.10, ...), custom_call_target="tpu_custom_call" | custom-call | flops 23000000512 | tf_op jit(solution)/shard_map/pallas_call | solution.py:38
  92.1 9.4 %collective-permute-done.18 = bf16[4,640,128]{2,1,0:T(8,128)(2,1)S(1)} collective-permute-done((bf16[4,640,128]{2,1,0:T(8,128)(2,1)S(1)}, bf16[4,640,128]{2,1,0:T(8,128)(2,1)S(1)}, u32[]{:S(2)}, u32[]{:S(2)}) %collective-permute-start.18) | collective-permute-done | bytes 655392 | tf_op jit(solution)/shard_map/ppermute | solution.py:613
  101.5 4.7 %collective-permute-done.17 = bf16[3456,128]{1,0:T(8,128)(2,1)S(1)} collective-permute-done((bf16[3456,128]{1,0:T(8,128)(2,1)S(1)}, bf16[3456,128]{1,0:T(8,128)(2,1)S(1)}, u32[]{:S(2)}, u32[]{:S(2)}) %collective-permute-start.17) | collective-permute-done | bytes 884768 | tf_op jit(solution)/shard_map/ppermute | solution.py:613
  106.8 1.3 collective-permute-done.19
  108.2 1.1 collective-permute-start.20
  110.0 3.5 %collective-permute-start.22 = (bf16[2,640,128]{2,1,0:T(8,128)(2,1)S(1)}, bf16[2,640,128]{2,1,0:T(8,128)(2,1)S(1)}, u32[]{:S(2)}, u32[]{:S(2)}) collective-permute-start(bf16[2,640,128]{2,1,0:T(8,128)(2,1)S(1)} %pad_maximum_fusion.7), channel_id=1, source_target_pairs={{0,8},{4,12},{8,0},{12,4},{16,24},{20,28},{24,16},{28,20},{1,9},{5... | collective-permute-start | bytes 983048 | tf_op jit(solution)/shard_map/ppermute | solution.py:613
  113.5 7.4 %collective-permute-done.22 = bf16[2,640,128]{2,1,0:T(8,128)(2,1)S(1)} collective-permute-done((bf16[2,640,128]{2,1,0:T(8,128)(2,1)S(1)}, bf16[2,640,128]{2,1,0:T(8,128)(2,1)S(1)}, u32[]{:S(2)}, u32[]{:S(2)}) %collective-permute-start.22) | collective-permute-done | bytes 327712 | tf_op jit(solution)/shard_map/ppermute | solution.py:613
  121.0 7.0 %collective-permute-start.23 = (bf16[640,128]{1,0:T(8,128)(2,1)S(1)}, bf16[640,128]{1,0:T(8,128)(2,1)S(1)}, u32[]{:S(2)}, u32[]{:S(2)}) collective-permute-start(bf16[640,128]{1,0:T(8,128)(2,1)S(1)} %fusion.19), channel_id=1, source_target_pairs={{0,16},{4,20},{8,24},{12,28},{16,0},{20,4},{24,8},{28,12},{1,17},{... | collective-permute-start | bytes 491528 | tf_op jit(solution)/shard_map/ppermute | solution.py:613
  128.1 0.7 shard_map.199
  128.8 6.1 %collective-permute-done.23 = bf16[640,128]{1,0:T(8,128)(2,1)S(1)} collective-permute-done((bf16[640,128]{1,0:T(8,128)(2,1)S(1)}, bf16[640,128]{1,0:T(8,128)(2,1)S(1)}, u32[]{:S(2)}, u32[]{:S(2)}) %collective-permute-start.23) | collective-permute-done | bytes 163872 | tf_op jit(solution)/shard_map/ppermute | solution.py:613
  135.0 1.4 collective-permute-start.24
  136.4 0.7 collective-permute-start.34
  137.2 0.7 collective-permute-start.25
  137.9 1.3 collective-permute-start.28
  139.6 4.4 %collective-permute-done.25 = bf16[4,144,128]{2,1,0:T(8,128)(2,1)S(1)} collective-permute-done((bf16[4,144,128]{2,1,0:T(8,128)(2,1)S(1)}, bf16[4,144,128]{2,1,0:T(8,128)(2,1)S(1)}, u32[]{:S(2)}, u32[]{:S(2)}) %collective-permute-start.25) | collective-permute-done | bytes 147488 | tf_op jit(solution)/shard_map/ppermute | solution.py:613
  144.1 3.4 %collective-permute-start.35 = (bf16[432,128]{1,0:T(8,128)(2,1)S(1)}, bf16[432,128]{1,0:T(8,128)(2,1)S(1)}, u32[]{:S(2)}, u32[]{:S(2)}) collective-permute-start(bf16[432,128]{1,0:T(8,128)(2,1)S(1)} %fusion.13), channel_id=1, source_target_pairs={{0,16},{4,20},{8,24},{12,28},{16,0},{20,4},{24,8},{28,12},{1,17},{... | collective-permute-start | bytes 331784 | tf_op jit(solution)/shard_map/ppermute | solution.py:613
  147.7 3.8 %collective-permute-done.35 = bf16[432,128]{1,0:T(8,128)(2,1)S(1)} collective-permute-done((bf16[432,128]{1,0:T(8,128)(2,1)S(1)}, bf16[432,128]{1,0:T(8,128)(2,1)S(1)}, u32[]{:S(2)}, u32[]{:S(2)}) %collective-permute-start.35) | collective-permute-done | bytes 110624 | tf_op jit(solution)/shard_map/ppermute | solution.py:613
  151.5 1.8 collective-permute-start.36
  153.4 1.2 collective-permute-start.27
  154.6 3.4 %collective-permute-done.36 = bf16[432,128]{1,0:T(8,128)(2,1)S(1)} collective-permute-done((bf16[432,128]{1,0:T(8,128)(2,1)S(1)}, bf16[432,128]{1,0:T(8,128)(2,1)S(1)}, u32[]{:S(2)}, u32[]{:S(2)}) %collective-permute-start.36) | collective-permute-done | bytes 110624 | tf_op jit(solution)/shard_map/ppermute | solution.py:613
  158.1 0.7 collective-permute-done.27
  158.8 5.2 %collective-permute-done.37 = bf16[2,432,128]{2,1,0:T(8,128)(2,1)S(1)} collective-permute-done((bf16[2,432,128]{2,1,0:T(8,128)(2,1)S(1)}, bf16[2,432,128]{2,1,0:T(8,128)(2,1)S(1)}, u32[]{:S(2)}, u32[]{:S(2)}) %collective-permute-start.37) | collective-permute-done | bytes 221216 | tf_op jit(solution)/shard_map/ppermute | solution.py:613
  164.1 1.1 collective-permute-start.38
  165.2 2.5 %collective-permute-start.31 = (bf16[464,128]{1,0:T(8,128)(2,1)S(1)}, bf16[464,128]{1,0:T(8,128)(2,1)S(1)}, u32[]{:S(2)}, u32[]{:S(2)}) collective-permute-start(bf16[464,128]{1,0:T(8,128)(2,1)S(1)} %pad_maximum_fusion.14), channel_id=1, source_target_pairs={{0,16},{4,20},{8,24},{12,28},{16,0},{20,4},{24,8},{28,12},{1,17},{... | collective-permute-start | bytes 356360 | tf_op jit(solution)/shard_map/ppermute | solution.py:613
  167.9 3.4 %collective-permute-start.29 = (bf16[2,256,384]{2,1,0:T(8,128)(2,1)S(1)}, bf16[2,256,384]{2,1,0:T(8,128)(2,1)S(1)}, u32[]{:S(2)}, u32[]{:S(2)}) collective-permute-start(bf16[2,256,384]{2,1,0:T(8,128)(2,1)S(1)} %pad_maximum_fusion.6), channel_id=1, source_target_pairs={{0,8},{4,12},{8,0},{12,4},{16,24},{20,28},{24,16},{28,20},{1,9},{5... | collective-permute-start | bytes 1179656 | tf_op jit(solution)/shard_map/ppermute | solution.py:613
  171.5 3.8 %collective-permute-start.32 = (bf16[2,464,128]{2,1,0:T(8,128)(2,1)S(1)}, bf16[2,464,128]{2,1,0:T(8,128)(2,1)S(1)}, u32[]{:S(2)}, u32[]{:S(2)}) collective-permute-start(bf16[2,464,128]{2,1,0:T(8,128)(2,1)S(1)} %pad_maximum_fusion.8), channel_id=1, source_target_pairs={{0,8},{4,12},{8,0},{12,4},{16,24},{20,28},{24,16},{28,20},{1,9},{5... | collective-permute-start | bytes 712712 | tf_op jit(solution)/shard_map/ppermute | solution.py:613
  175.3 1.9 shard_map.202
  177.2 2.6 %collective-permute-done.29 = bf16[2,256,384]{2,1,0:T(8,128)(2,1)S(1)} collective-permute-done((bf16[2,256,384]{2,1,0:T(8,128)(2,1)S(1)}, bf16[2,256,384]{2,1,0:T(8,128)(2,1)S(1)}, u32[]{:S(2)}, u32[]{:S(2)}) %collective-permute-start.29) | collective-permute-done | bytes 393248 | tf_op jit(solution)/shard_map/ppermute | solution.py:613
  179.9 1.6 collective-permute-start.30
  181.6 0.8 collective-permute-done.32
  182.5 1.6 collective-permute-start.33
  184.1 4.6 %collective-permute-done.30 = bf16[256,384]{1,0:T(8,128)(2,1)S(1)} collective-permute-done((bf16[256,384]{1,0:T(8,128)(2,1)S(1)}, bf16[256,384]{1,0:T(8,128)(2,1)S(1)}, u32[]{:S(2)}, u32[]{:S(2)}) %collective-permute-start.30) | collective-permute-done | bytes 196640 | tf_op jit(solution)/shard_map/ppermute | solution.py:613
  188.8 1.4 shard_map.200
  190.2 1.0 collective-permute-done.33.refs_1_
  191.2 2.1 %shard_map.201 = (f32[576,384]{1,0:T(8,128)}, f32[144,576]{1,0:T(8,128)}, f32[144,576]{1,0:T(8,128)}, f32[144,192]{1,0:T(8,128)}, f32[144,192]{1,0:T(8,128)}, /*index=5*/f32[8,144]{1,0:T(8,128)S(1)}) custom-call(s32[2]{0:T(128)S(1)} %copy-done.4, bf16[4,464,128]{2,1,0:T(8,128)(2,1)S(1)} %pad_maximum_fusion.4.refs_0_, ...), custom_call_target="tpu_custom_call" | custom-call | flops 3000000000 | tf_op jit(solution)/shard_map/pallas_call | solution.py:38
  (138 shorter events, 9.2 us)
Async XLA Ops:
  0.6 25.0 %collective-permute-start = (bf16[576,256]{1,0:T(8,128)(2,1)}, bf16[576,256]{1,0:T(8,128)(2,1)}, u32[]{:S(2)}, u32[]{:S(2)}) collective-permute-start(bf16[576,256]{1,0:T(8,128)(2,1)} %bitcast.105), channel_id=1, source_target_pairs={{0,16},{4,20},{8,24},{12,28},{1,17},{5,21},{9,25},{13,29},{2,18},{... | collective-permute-start | bytes 884744 | tf_op jit(solution)/shard_map/ppermute | solution.py:632
  9.3 14.2 %collective-permute-start.2 = (bf16[160,960]{1,0:T(8,128)(2,1)S(1)}, bf16[160,960]{1,0:T(8,128)(2,1)S(1)}, u32[]{:S(2)}, u32[]{:S(2)}) collective-permute-start(bf16[160,960]{1,0:T(8,128)(2,1)S(1)} %fusion.11), channel_id=1, source_target_pairs={{0,2},{1,3},{2,0},{3,1},{4,6},{5,7},{6,4},{7,5},{8,10},{9,11},{10,... | collective-permute-start | bytes 921608 | tf_op jit(solution)/shard_map/ppermute | solution.py:613
  14.6 3.0 %copy-start.2 = (bf16[1,256,576]{1,2,0:T(8,128)(2,1)S(1)}, bf16[1,256,576]{1,2,0:T(8,128)(2,1)}, u32[]{:S(2)}) copy-start(bf16[1,256,576]{1,2,0:T(8,128)(2,1)} %param.11) | copy-start | bytes 884740
  14.6 8.8 %copy-start.19 = (bf16[144,576]{1,0:T(8,128)(2,1)S(1)}, bf16[144,576]{1,0:T(8,128)(2,1)}, u32[]{:S(2)}) copy-start(bf16[144,576]{1,0:T(8,128)(2,1)} %param.13) | copy-start | bytes 497668
  14.6 8.7 %copy-start.24 = (bf16[144,192]{1,0:T(8,128)(2,1)S(1)}, bf16[144,192]{1,0:T(8,128)(2,1)}, u32[]{:S(2)}) copy-start(bf16[144,192]{1,0:T(8,128)(2,1)} %param.15) | copy-start | bytes 165892
  14.6 8.7 %copy-start.25 = (bf16[144,192]{1,0:T(8,128)(2,1)S(1)}, bf16[144,192]{1,0:T(8,128)(2,1)}, u32[]{:S(2)}) copy-start(bf16[144,192]{1,0:T(8,128)(2,1)} %param.14) | copy-start | bytes 165892
  17.6 6.0 %copy-start.22 = (bf16[144,1536]{1,0:T(8,128)(2,1)S(1)}, bf16[144,1536]{1,0:T(8,128)(2,1)}, u32[]{:S(2)}) copy-start(bf16[144,1536]{1,0:T(8,128)(2,1)} %param.18) | copy-start | bytes 1327108
  17.6 6.1 %copy-start.23 = (bf16[144,1536]{1,0:T(8,128)(2,1)S(1)}, bf16[144,1536]{1,0:T(8,128)(2,1)}, u32[]{:S(2)}) copy-start(bf16[144,1536]{1,0:T(8,128)(2,1)} %param.19) | copy-start | bytes 1327108
  17.6 8.6 %collective-permute-start.4 = (bf16[576,256]{1,0:T(8,128)(2,1)S(1)}, bf16[576,256]{1,0:T(8,128)(2,1)}, u32[]{:S(2)}, u32[]{:S(2)}) collective-permute-start(bf16[576,256]{1,0:T(8,128)(2,1)S(1)} %bitcast.108), channel_id=1, source_target_pairs={{0,4},{4,0},{8,12},{12,8},{16,20},{20,16},{24,28},{28,24},{1,5},{5... | collective-permute-start | bytes 884744 | tf_op jit(solution)/shard_map/ppermute | solution.py:613
  19.1 8.9 %collective-permute-start.5 = (bf16[576,256]{1,0:T(8,128)(2,1)S(1)}, bf16[576,256]{1,0:T(8,128)(2,1)}, u32[]{:S(2)}, u32[]{:S(2)}) collective-permute-start(bf16[576,256]{1,0:T(8,128)(2,1)S(1)} %bitcast.109), channel_id=1, source_target_pairs={{0,8},{4,12},{8,16},{12,20},{16,24},{20,28},{1,9},{5,13},{9,17},{1... | collective-permute-start | bytes 884744 | tf_op jit(solution)/shard_map/ppermute | solution.py:632
  23.5 5.6 %copy-start.20 = (bf16[2,160,960]{2,1,0:T(8,128)(2,1)}, bf16[2,160,960]{2,1,0:T(8,128)(2,1)S(1)}, u32[]{:S(2)}) copy-start(bf16[2,160,960]{2,1,0:T(8,128)(2,1)S(1)} %pad_maximum_fusion.2.here_pair) | copy-start | bytes 1843204
  23.6 5.5 %collective-permute-start.3 = (bf16[2,160,960]{2,1,0:T(8,128)(2,1)S(1)}, bf16[2,160,960]{2,1,0:T(8,128)(2,1)}, u32[]{:S(2)}, u32[]{:S(2)}) collective-permute-start(bf16[2,160,960]{2,1,0:T(8,128)(2,1)S(1)} %pad_maximum_fusion.2.here_pair), channel_id=1, source_target_pairs={{0,1},{1,0},{2,3},{3,2},{4,5},{5,4},{6,7},{7,6},{8,9},{9,8},{10,11... | collective-permute-start | bytes 1843208 | tf_op jit(solution)/shard_map/ppermute | solution.py:613
  24.4 26.6 %copy-start.27 = (bf16[144,3648]{1,0:T(8,128)(2,1)}, bf16[144,3648]{1,0:T(8,128)(2,1)S(1)}, u32[]{:S(2)}) copy-start(bf16[144,3648]{1,0:T(8,128)(2,1)S(1)} %constant_dynamic-update-slice_fusion.wi0) | copy-start | bytes 3151876
  24.4 26.6 %collective-permute-start.9 = (bf16[144,3648]{1,0:T(8,128)(2,1)S(1)}, bf16[144,3648]{1,0:T(8,128)(2,1)S(1)}, u32[]{:S(2)}, u32[]{:S(2)}) collective-permute-start(bf16[144,3648]{1,0:T(8,128)(2,1)S(1)} %constant_dynamic-update-slice_fusion.wi0), channel_id=1, source_target_pairs={{0,2},{1,3},{2,0},{3,1},{4,6},{5,7},{6,4},{7,5},{8,10},{9,11},{10,... | collective-permute-start | bytes 3151880 | tf_op jit(solution)/shard_map/ppermute | solution.py:613
  25.7 10.8 %copy-start.16 = (bf16[384,576]{0,1:T(8,128)(2,1)S(1)}, bf16[384,576]{0,1:T(8,128)(2,1)}, u32[]{:S(2)}) copy-start(bf16[384,576]{0,1:T(8,128)(2,1)} %param.20) | copy-start | bytes 1327108
  25.7 12.1 %collective-permute-start.6 = (bf16[576,256]{1,0:T(8,128)(2,1)}, bf16[576,256]{1,0:T(8,128)(2,1)}, u32[]{:S(2)}, u32[]{:S(2)}) collective-permute-start(bf16[576,256]{1,0:T(8,128)(2,1)} %collective-permute-done.refs_2_), channel_id=1, source_target_pairs={{0,4},{4,0},{8,12},{12,8},{16,20},{20,16},{24,28},{28,24},{1,5},{5... | collective-permute-start | bytes 884744 | tf_op jit(solution)/shard_map/ppermute | solution.py:613
  26.2 9.2 %collective-permute-start.1 = (bf16[576,256]{1,0:T(8,128)(2,1)}, bf16[576,256]{1,0:T(8,128)(2,1)}, u32[]{:S(2)}, u32[]{:S(2)}) collective-permute-start(bf16[576,256]{1,0:T(8,128)(2,1)} %collective-permute-done.refs_2_), channel_id=1, source_target_pairs={{16,24},{20,28},{17,25},{21,29},{18,26},{22,30},{19,27},{23,31}} | collective-permute-start | bytes 884744 | tf_op jit(solution)/shard_map/ppermute | solution.py:748
  28.0 14.2 %collective-permute-start.7 = (bf16[576,256]{1,0:T(8,128)(2,1)}, bf16[576,256]{1,0:T(8,128)(2,1)}, u32[]{:S(2)}, u32[]{:S(2)}) collective-permute-start(bf16[576,256]{1,0:T(8,128)(2,1)} %collective-permute-done.5.refs_0_), channel_id=1, source_target_pairs={{0,4},{4,0},{8,12},{12,8},{16,20},{20,16},{24,28},{28,24},{1,5},{5... | collective-permute-start | bytes 884744 | tf_op jit(solution)/shard_map/ppermute | solution.py:613
  35.4 15.6 %collective-permute-start.8 = (bf16[576,256]{1,0:T(8,128)(2,1)}, bf16[576,256]{1,0:T(8,128)(2,1)S(1)}, u32[]{:S(2)}, u32[]{:S(2)}) collective-permute-start(bf16[576,256]{1,0:T(8,128)(2,1)} %collective-permute-done.1.refs_3_), channel_id=1, source_target_pairs={{0,4},{4,0},{8,12},{12,8},{16,20},{20,16},{24,28},{28,24},{1,5},{5... | collective-permute-start | bytes 884744 | tf_op jit(solution)/shard_map/ppermute | solution.py:613
  36.7 23.8 %collective-permute-start.10 = (bf16[384,576]{1,0:T(8,128)(2,1)S(1)}, bf16[384,576]{1,0:T(8,128)(2,1)}, u32[]{:S(2)}, u32[]{:S(2)}) collective-permute-start(bf16[384,576]{1,0:T(8,128)(2,1)S(1)} %copy.26), channel_id=1, source_target_pairs={{0,2},{1,3},{2,0},{3,1},{4,6},{5,7},{6,4},{7,5},{8,10},{9,11},{10,... | collective-permute-start | bytes 1327112 | tf_op jit(solution)/shard_map/ppermute | solution.py:613
  51.0 8.2 %copy-start.28 = (bf16[144,3648]{1,0:T(8,128)(2,1)}, bf16[144,3648]{1,0:T(8,128)(2,1)S(1)}, u32[]{:S(2)}) copy-start(bf16[144,3648]{1,0:T(8,128)(2,1)S(1)} %collective-permute-done.9.wi2) | copy-start | bytes 3151876
  51.0 12.1 %collective-permute-start.11 = (bf16[144,3648]{1,0:T(8,128)(2,1)S(1)}, bf16[144,3648]{1,0:T(8,128)(2,1)}, u32[]{:S(2)}, u32[]{:S(2)}) collective-permute-start(bf16[144,3648]{1,0:T(8,128)(2,1)S(1)} %constant_dynamic-update-slice_fusion.wi0), channel_id=1, source_target_pairs={{0,1},{1,0},{2,3},{3,2},{4,5},{5,4},{6,7},{7,6},{8,9},{9,8},{10,11... | collective-permute-start | bytes 3151880 | tf_op jit(solution)/shard_map/ppermute | solution.py:613
  51.1 12.0 %collective-permute-start.12 = (bf16[144,3648]{1,0:T(8,128)(2,1)S(1)}, bf16[144,3648]{1,0:T(8,128)(2,1)}, u32[]{:S(2)}, u32[]{:S(2)}) collective-permute-start(bf16[144,3648]{1,0:T(8,128)(2,1)S(1)} %collective-permute-done.9.wi2), channel_id=1, source_target_pairs={{0,1},{1,0},{2,3},{3,2},{4,5},{5,4},{6,7},{7,6},{8,9},{9,8},{10,11... | collective-permute-start | bytes 3151880 | tf_op jit(solution)/shard_map/ppermute | solution.py:613
  60.5 2.2 %collective-permute-start.14 = (bf16[384,576]{1,0:T(8,128)(2,1)}, bf16[384,576]{1,0:T(8,128)(2,1)}, u32[]{:S(2)}, u32[]{:S(2)}) collective-permute-start(bf16[384,576]{1,0:T(8,128)(2,1)} %collective-permute-done.10.wd2), channel_id=1, source_target_pairs={{0,1},{1,0},{2,3},{3,2},{4,5},{5,4},{6,7},{7,6},{8,9},{9,8},{10,11... | collective-permute-start | bytes 1327112 | tf_op jit(solution)/shard_map/ppermute | solution.py:613
  60.7 2.3 %copy-start.21 = (bf16[384,576]{1,0:T(8,128)(2,1)}, bf16[384,576]{1,0:T(8,128)(2,1)S(1)}, u32[]{:S(2)}) copy-start(bf16[384,576]{1,0:T(8,128)(2,1)S(1)} %copy.28.wd0) | copy-start | bytes 1327108
  60.8 2.3 %collective-permute-start.13 = (bf16[384,576]{1,0:T(8,128)(2,1)S(1)}, bf16[384,576]{1,0:T(8,128)(2,1)S(1)}, u32[]{:S(2)}, u32[]{:S(2)}) collective-permute-start(bf16[384,576]{1,0:T(8,128)(2,1)S(1)} %copy.28.wd0), channel_id=1, source_target_pairs={{0,1},{1,0},{2,3},{3,2},{4,5},{5,4},{6,7},{7,6},{8,9},{9,8},{10,11... | collective-permute-start | bytes 1327112 | tf_op jit(solution)/shard_map/ppermute | solution.py:613
  78.3 3.2 %collective-permute-start.16 = (bf16[2,2560,128]{2,1,0:T(8,128)(2,1)}, bf16[2,2560,128]{2,1,0:T(8,128)(2,1)S(1)}, u32[]{:S(2)}, u32[]{:S(2)}) collective-permute-start(bf16[2,2560,128]{2,1,0:T(8,128)(2,1)} %get-tuple-element.107), channel_id=1, source_target_pairs={{0,1},{1,0},{2,3},{3,2},{4,5},{5,4},{6,7},{7,6},{8,9},{9,8},{10,11... | collective-permute-start | bytes 3932168 | tf_op jit(solution)/shard_map/ppermute | solution.py:613
  79.0 5.1 %collective-permute-start.15 = (bf16[2,3456,128]{2,1,0:T(8,128)(2,1)}, bf16[2,3456,128]{2,1,0:T(8,128)(2,1)S(1)}, u32[]{:S(2)}, u32[]{:S(2)}) collective-permute-start(bf16[2,3456,128]{2,1,0:T(8,128)(2,1)} %get-tuple-element.105), channel_id=1, source_target_pairs={{0,1},{1,0},{2,3},{3,2},{4,5},{5,4},{6,7},{7,6},{8,9},{9,8},{10,11... | collective-permute-start | bytes 5308424 | tf_op jit(solution)/shard_map/ppermute | solution.py:613
  81.5 2.5 %copy-start.18 = (bf16[3456,128]{1,0:T(8,128)(2,1)S(1)}, bf16[3456,128]{1,0:T(8,128)(2,1)}, u32[]{:S(2)}) copy-start(bf16[3456,128]{1,0:T(8,128)(2,1)} %get-tuple-element.104) | copy-start | bytes 2654212
  81.5 4.5 %copy-start.10 = (bf16[2048,384]{1,0:T(8,128)(2,1)S(1)}, bf16[2048,384]{1,0:T(8,128)(2,1)}, u32[]{:S(2)}) copy-start(bf16[2048,384]{1,0:T(8,128)(2,1)} %get-tuple-element.102.kv_all) | copy-start | bytes 4718596
  81.5 4.5 %copy-start.11 = (f32[256,576]{1,0:T(8,128)S(1)}, f32[256,576]{1,0:T(8,128)}, u32[]{:S(2)}) copy-start(f32[256,576]{1,0:T(8,128)} %get-tuple-element.96.attended) | copy-start | bytes 1769476
  81.5 4.5 %copy-start.15 = (f32[8,768]{1,0:T(8,128)S(1)}, f32[8,768]{1,0:T(8,128)}, u32[]{:S(2)}) copy-start(f32[8,768]{1,0:T(8,128)} %get-tuple-element.110.lse) | copy-start | bytes 73732
  83.3 2.7 %copy-start.9 = (bf16[2048,576]{1,0:T(8,128)(2,1)S(1)}, bf16[2048,576]{1,0:T(8,128)(2,1)}, u32[]{:S(2)}) copy-start(bf16[2048,576]{1,0:T(8,128)(2,1)} %get-tuple-element.111.normed) | copy-start | bytes 7077892
  83.4 2.6 %copy-start.7 = (bf16[576,576]{1,0:T(8,128)(2,1)S(1)}, bf16[576,576]{1,0:T(8,128)(2,1)}, u32[]{:S(2)}) copy-start(bf16[576,576]{1,0:T(8,128)(2,1)} %get-tuple-element.112.query_weight) | copy-start | bytes 1990660
  83.4 2.6 %copy-start.8 = (bf16[256,576]{1,0:T(8,128)(2,1)S(1)}, bf16[256,576]{1,0:T(8,128)(2,1)}, u32[]{:S(2)}) copy-start(bf16[256,576]{1,0:T(8,128)(2,1)} %get-tuple-element.84.queries) | copy-start | bytes 884740
  83.5 2.6 %copy-start.13 = (bf16[256,576]{1,0:T(8,128)(2,1)S(1)}, bf16[256,576]{1,0:T(8,128)(2,1)}, u32[]{:S(2)}) copy-start(bf16[256,576]{1,0:T(8,128)(2,1)} %get-tuple-element.109.attended_grad) | copy-start | bytes 884740
  84.1 2.2 %copy-start.5 = (bf16[576,384]{1,0:T(8,128)(2,1)S(1)}, bf16[576,384]{1,0:T(8,128)(2,1)}, u32[]{:S(2)}) copy-start(bf16[576,384]{1,0:T(8,128)(2,1)} %get-tuple-element.87.kv_weight) | copy-start | bytes 1327108
  84.1 2.2 %copy-start.12 = (f32[8,576]{1,0:T(8,128)S(1)}, f32[8,576]{1,0:T(8,128)}, u32[]{:S(2)}) copy-start(f32[8,576]{1,0:T(8,128)} %get-tuple-element.88.gains) | copy-start | bytes 55300
  84.1 2.2 %copy-start.14 = (f32[8,576]{1,0:T(8,128)S(1)}, f32[8,576]{1,0:T(8,128)}, u32[]{:S(2)}) copy-start(f32[8,576]{1,0:T(8,128)} %get-tuple-element.113.ffn_gain_grad) | copy-start | bytes 55300
  84.3 21.8 %collective-permute-start.17 = (bf16[3456,128]{1,0:T(8,128)(2,1)S(1)}, bf16[3456,128]{1,0:T(8,128)(2,1)S(1)}, u32[]{:S(2)}, u32[]{:S(2)}) collective-permute-start(bf16[3456,128]{1,0:T(8,128)(2,1)S(1)} %fusion), channel_id=1, source_target_pairs={{0,2},{1,3},{2,0},{3,1},{4,6},{5,7},{6,4},{7,5},{8,10},{9,11},{10,... | collective-permute-start | bytes 2654216 | tf_op jit(solution)/shard_map/ppermute | solution.py:613
  84.9 16.5 %collective-permute-start.18 = (bf16[4,640,128]{2,1,0:T(8,128)(2,1)S(1)}, bf16[4,640,128]{2,1,0:T(8,128)(2,1)S(1)}, u32[]{:S(2)}, u32[]{:S(2)}) collective-permute-start(bf16[4,640,128]{2,1,0:T(8,128)(2,1)S(1)} %pad_maximum_fusion.3), channel_id=1, source_target_pairs={{0,4},{4,0},{8,12},{12,8},{16,20},{20,16},{24,28},{28,24},{1,5},{5... | collective-permute-start | bytes 1966088 | tf_op jit(solution)/shard_map/ppermute | solution.py:613
  92.1 14.4 %copy-start.17 = (bf16[3456,128]{1,0:T(8,128)(2,1)S(1)}, bf16[3456,128]{1,0:T(8,128)(2,1)}, u32[]{:S(2)}) copy-start(bf16[3456,128]{1,0:T(8,128)(2,1)} %get-tuple-element.125) | copy-start | bytes 2654212
  106.1 2.0 %collective-permute-start.19 = (bf16[2,1152,128]{2,1,0:T(8,128)(2,1)S(1)}, bf16[2,1152,128]{2,1,0:T(8,128)(2,1)S(1)}, u32[]{:S(2)}, u32[]{:S(2)}) collective-permute-start(bf16[2,1152,128]{2,1,0:T(8,128)(2,1)S(1)} %get-tuple-element.124), channel_id=1, source_target_pairs={{0,1},{1,0},{2,3},{3,2},{4,5},{5,4},{6,7},{7,6},{8,9},{9,8},{10,11... | collective-permute-start | bytes 1769480 | tf_op jit(solution)/shard_map/ppermute | solution.py:613
  108.2 19.8 %collective-permute-start.20 = (bf16[4,432,128]{2,1,0:T(8,128)(2,1)S(1)}, bf16[4,432,128]{2,1,0:T(8,128)(2,1)S(1)}, u32[]{:S(2)}, u32[]{:S(2)}) collective-permute-start(bf16[4,432,128]{2,1,0:T(8,128)(2,1)S(1)} %bitcast.127), channel_id=1, source_target_pairs={{0,4},{4,0},{8,12},{12,8},{16,20},{20,16},{24,28},{28,24},{1,5},{5... | collective-permute-start | bytes 1327112 | tf_op jit(solution)/shard_map/ppermute | solution.py:613
  109.3 18.7 %collective-permute-start.21 = (bf16[1152,128]{1,0:T(8,128)(2,1)S(1)}, bf16[1152,128]{1,0:T(8,128)(2,1)S(1)}, u32[]{:S(2)}, u32[]{:S(2)}) collective-permute-start(bf16[1152,128]{1,0:T(8,128)(2,1)S(1)} %fusion.8), channel_id=1, source_target_pairs={{0,2},{1,3},{2,0},{3,1},{4,6},{5,7},{6,4},{7,5},{8,10},{9,11},{10,... | collective-permute-start | bytes 884744 | tf_op jit(solution)/shard_map/ppermute | solution.py:613
  110.0 10.9 %collective-permute-start.22 = (bf16[2,640,128]{2,1,0:T(8,128)(2,1)S(1)}, bf16[2,640,128]{2,1,0:T(8,128)(2,1)S(1)}, u32[]{:S(2)}, u32[]{:S(2)}) collective-permute-start(bf16[2,640,128]{2,1,0:T(8,128)(2,1)S(1)} %pad_maximum_fusion.7), channel_id=1, source_target_pairs={{0,8},{4,12},{8,0},{12,4},{16,24},{20,28},{24,16},{28,20},{1,9},{5... | collective-permute-start | bytes 983048 | tf_op jit(solution)/shard_map/ppermute | solution.py:613
  121.0 13.9 %collective-permute-start.23 = (bf16[640,128]{1,0:T(8,128)(2,1)S(1)}, bf16[640,128]{1,0:T(8,128)(2,1)S(1)}, u32[]{:S(2)}, u32[]{:S(2)}) collective-permute-start(bf16[640,128]{1,0:T(8,128)(2,1)S(1)} %fusion.19), channel_id=1, source_target_pairs={{0,16},{4,20},{8,24},{12,28},{16,0},{20,4},{24,8},{28,12},{1,17},{... | collective-permute-start | bytes 491528 | tf_op jit(solution)/shard_map/ppermute | solution.py:613
  135.0 4.5 %collective-permute-start.24 = (bf16[320,128]{1,0:T(8,128)(2,1)S(1)}, bf16[320,128]{1,0:T(8,128)(2,1)S(1)}, u32[]{:S(2)}, u32[]{:S(2)}) collective-permute-start(bf16[320,128]{1,0:T(8,128)(2,1)S(1)} %slice.226), channel_id=1, source_target_pairs={{0,2},{1,3},{2,0},{3,1},{4,6},{5,7},{6,4},{7,5},{8,10},{9,11},{10,... | collective-permute-start | bytes 245768 | tf_op jit(solution)/shard_map/ppermute | solution.py:613
  136.4 7.6 %collective-permute-start.34 = (bf16[2,432,128]{2,1,0:T(8,128)(2,1)S(1)}, bf16[2,432,128]{2,1,0:T(8,128)(2,1)S(1)}, u32[]{:S(2)}, u32[]{:S(2)}) collective-permute-start(bf16[2,432,128]{2,1,0:T(8,128)(2,1)S(1)} %pad_maximum_fusion.9), channel_id=1, source_target_pairs={{0,8},{4,12},{8,0},{12,4},{16,24},{20,28},{24,16},{28,20},{1,9},{5... | collective-permute-start | bytes 663560 | tf_op jit(solution)/shard_map/ppermute | solution.py:613
  137.2 6.8 %collective-permute-start.25 = (bf16[4,144,128]{2,1,0:T(8,128)(2,1)S(1)}, bf16[4,144,128]{2,1,0:T(8,128)(2,1)S(1)}, u32[]{:S(2)}, u32[]{:S(2)}) collective-permute-start(bf16[4,144,128]{2,1,0:T(8,128)(2,1)S(1)} %get-tuple-element.136), channel_id=1, source_target_pairs={{0,4},{4,0},{8,12},{12,8},{16,20},{20,16},{24,28},{28,24},{1,5},{5... | collective-permute-start | bytes 442376 | tf_op jit(solution)/shard_map/ppermute | solution.py:613
  137.9 27.4 %collective-permute-start.28 = (bf16[4,256,384]{2,1,0:T(8,128)(2,1)S(1)}, bf16[4,256,384]{2,1,0:T(8,128)(2,1)S(1)}, u32[]{:S(2)}, u32[]{:S(2)}) collective-permute-start(bf16[4,256,384]{2,1,0:T(8,128)(2,1)S(1)} %slice.212), channel_id=1, source_target_pairs={{0,4},{4,0},{8,12},{12,8},{16,20},{20,16},{24,28},{28,24},{1,5},{5... | collective-permute-start | bytes 2359304 | tf_op jit(solution)/shard_map/ppermute | solution.py:613
  144.1 7.4 %collective-permute-start.35 = (bf16[432,128]{1,0:T(8,128)(2,1)S(1)}, bf16[432,128]{1,0:T(8,128)(2,1)S(1)}, u32[]{:S(2)}, u32[]{:S(2)}) collective-permute-start(bf16[432,128]{1,0:T(8,128)(2,1)S(1)} %fusion.13), channel_id=1, source_target_pairs={{0,16},{4,20},{8,24},{12,28},{16,0},{20,4},{24,8},{28,12},{1,17},{... | collective-permute-start | bytes 331784 | tf_op jit(solution)/shard_map/ppermute | solution.py:613
  147.5 5.8 %collective-permute-start.26 = (bf16[2,144,128]{2,1,0:T(8,128)(2,1)S(1)}, bf16[2,144,128]{2,1,0:T(8,128)(2,1)S(1)}, u32[]{:S(2)}, u32[]{:S(2)}) collective-permute-start(bf16[2,144,128]{2,1,0:T(8,128)(2,1)S(1)} %pad_maximum_fusion.15), channel_id=1, source_target_pairs={{0,8},{4,12},{8,0},{12,4},{16,24},{20,28},{24,16},{28,20},{1,9},{5... | collective-permute-start | bytes 221192 | tf_op jit(solution)/shard_map/ppermute | solution.py:613
  151.5 6.5 %collective-permute-start.36 = (bf16[432,128]{1,0:T(8,128)(2,1)S(1)}, bf16[432,128]{1,0:T(8,128)(2,1)S(1)}, u32[]{:S(2)}, u32[]{:S(2)}) collective-permute-start(bf16[432,128]{1,0:T(8,128)(2,1)S(1)} %fusion.15), channel_id=1, source_target_pairs={{0,16},{4,20},{8,24},{12,28},{16,0},{20,4},{24,8},{28,12},{1,17},{... | collective-permute-start | bytes 331784 | tf_op jit(solution)/shard_map/ppermute | solution.py:613
  153.4 5.4 %collective-permute-start.27 = (bf16[144,128]{1,0:T(8,128)(2,1)S(1)}, bf16[144,128]{1,0:T(8,128)(2,1)S(1)}, u32[]{:S(2)}, u32[]{:S(2)}) collective-permute-start(bf16[144,128]{1,0:T(8,128)(2,1)S(1)} %fusion.25), channel_id=1, source_target_pairs={{0,16},{4,20},{8,24},{12,28},{16,0},{20,4},{24,8},{28,12},{1,17},{... | collective-permute-start | bytes 110600 | tf_op jit(solution)/shard_map/ppermute | solution.py:613
  158.0 6.0 %collective-permute-start.37 = (bf16[2,432,128]{2,1,0:T(8,128)(2,1)S(1)}, bf16[2,432,128]{2,1,0:T(8,128)(2,1)S(1)}, u32[]{:S(2)}, u32[]{:S(2)}) collective-permute-start(bf16[2,432,128]{2,1,0:T(8,128)(2,1)S(1)} %pad_maximum_fusion.10), channel_id=1, source_target_pairs={{0,8},{4,12},{8,0},{12,4},{16,24},{20,28},{24,16},{28,20},{1,9},{5... | collective-permute-start | bytes 663560 | tf_op jit(solution)/shard_map/ppermute | solution.py:613
  164.1 11.1 %collective-permute-start.38 = (bf16[4,432,128]{2,1,0:T(8,128)(2,1)S(1)}, bf16[4,432,128]{2,1,0:T(8,128)(2,1)S(1)}, u32[]{:S(2)}, u32[]{:S(2)}) collective-permute-start(bf16[4,432,128]{2,1,0:T(8,128)(2,1)S(1)} %pad_maximum_fusion.5.refs_0_), channel_id=1, source_target_pairs={{0,4},{4,0},{8,12},{12,8},{16,20},{20,16},{24,28},{28,24},{1,5},{5... | collective-permute-start | bytes 1327112 | tf_op jit(solution)/shard_map/ppermute | solution.py:613
  165.2 6.2 %collective-permute-start.31 = (bf16[464,128]{1,0:T(8,128)(2,1)S(1)}, bf16[464,128]{1,0:T(8,128)(2,1)S(1)}, u32[]{:S(2)}, u32[]{:S(2)}) collective-permute-start(bf16[464,128]{1,0:T(8,128)(2,1)S(1)} %pad_maximum_fusion.14), channel_id=1, source_target_pairs={{0,16},{4,20},{8,24},{12,28},{16,0},{20,4},{24,8},{28,12},{1,17},{... | collective-permute-start | bytes 356360 | tf_op jit(solution)/shard_map/ppermute | solution.py:613
  167.9 11.9 %collective-permute-start.29 = (bf16[2,256,384]{2,1,0:T(8,128)(2,1)S(1)}, bf16[2,256,384]{2,1,0:T(8,128)(2,1)S(1)}, u32[]{:S(2)}, u32[]{:S(2)}) collective-permute-start(bf16[2,256,384]{2,1,0:T(8,128)(2,1)S(1)} %pad_maximum_fusion.6), channel_id=1, source_target_pairs={{0,8},{4,12},{8,0},{12,4},{16,24},{20,28},{24,16},{28,20},{1,9},{5... | collective-permute-start | bytes 1179656 | tf_op jit(solution)/shard_map/ppermute | solution.py:613
  171.5 10.9 %collective-permute-start.32 = (bf16[2,464,128]{2,1,0:T(8,128)(2,1)S(1)}, bf16[2,464,128]{2,1,0:T(8,128)(2,1)S(1)}, u32[]{:S(2)}, u32[]{:S(2)}) collective-permute-start(bf16[2,464,128]{2,1,0:T(8,128)(2,1)S(1)} %pad_maximum_fusion.8), channel_id=1, source_target_pairs={{0,8},{4,12},{8,0},{12,4},{16,24},{20,28},{24,16},{28,20},{1,9},{5... | collective-permute-start | bytes 712712 | tf_op jit(solution)/shard_map/ppermute | solution.py:613
  179.9 8.9 %copy-start.3 = (bf16[1,256,576]{1,2,0:T(8,128)(2,1)S(1)}, bf16[1,256,576]{1,2,0:T(8,128)(2,1)}, u32[]{:S(2)}) copy-start(bf16[1,256,576]{1,2,0:T(8,128)(2,1)} %param.11) | copy-start | bytes 884740
  179.9 8.9 %copy-start.6 = (f32[256,576]{1,0:T(8,128)S(1)}, f32[256,576]{1,0:T(8,128)}, u32[]{:S(2)}) copy-start(f32[256,576]{1,0:T(8,128)} %get-tuple-element.115.middle_grad) | copy-start | bytes 1769476
  179.9 8.7 %collective-permute-start.30 = (bf16[256,384]{1,0:T(8,128)(2,1)S(1)}, bf16[256,384]{1,0:T(8,128)(2,1)S(1)}, u32[]{:S(2)}, u32[]{:S(2)}) collective-permute-start(bf16[256,384]{1,0:T(8,128)(2,1)S(1)} %fusion.18), channel_id=1, source_target_pairs={{0,16},{4,20},{8,24},{12,28},{16,0},{20,4},{24,8},{28,12},{1,17},{... | collective-permute-start | bytes 589832 | tf_op jit(solution)/shard_map/ppermute | solution.py:613
  182.5 8.7 %collective-permute-start.33 = (bf16[4,464,128]{2,1,0:T(8,128)(2,1)S(1)}, bf16[4,464,128]{2,1,0:T(8,128)(2,1)S(1)}, u32[]{:S(2)}, u32[]{:S(2)}) collective-permute-start(bf16[4,464,128]{2,1,0:T(8,128)(2,1)S(1)} %pad_maximum_fusion.4.refs_0_), channel_id=1, source_target_pairs={{0,4},{4,0},{8,12},{12,8},{16,20},{20,16},{24,28},{28,24},{1,5},{5... | collective-permute-start | bytes 1425416 | tf_op jit(solution)/shard_map/ppermute | solution.py:613
  (6 other events, 8.7 us)
